TPU v7x, 512 devices: a whole 4x8x8 slice. The times are simulated.
512 devices in a mesh: dp: 32 (over y, x), seq: 16 (over z, core).
Axes of the slice: x: 4, y: 8, z: 8, core: 2. Of those that a mesh axis runs over, the one named last changes fastest.
Arguments:
- queries: bfloat16 [65536, 6144], P(('dp', 'seq')), may hold values from -5 to 5
- keys: bfloat16 [65536, 512], P(('dp', 'seq')), may hold values from -5 to 5
- values: bfloat16 [65536, 512], P(('dp', 'seq')), may hold values from -5 to 5
- grad_out: bfloat16 [65536, 6144], P(('dp', 'seq')), may hold values from -5 to 5
- prefix_keys: bfloat16 [384, 512], P('seq'), may hold values from -5 to 5
- prefix_values: bfloat16 [384, 512], P('seq'), may hold values from -5 to 5
- doc_lengths: int32 [32, 8], P('dp'), may hold values from 1 to 512, 2048 in all within a row
- doc_tenants: int32 [32, 8], P('dp'), may hold values from 0 to 5
- tenant_slots: int32 [6], replicated, may hold values from 0 to 5, each once
Outputs:
- grad_keys: bfloat16 [65536, 512], P(('dp', 'seq'))
- grad_values: bfloat16 [65536, 512], P(('dp', 'seq'))
- prefix_key_grads: float32 [384, 512], P('seq')
- prefix_value_grads: float32 [384, 512], P('seq')
Inputs may be any that keep to these rules, and one draw needn't show every extreme that they name: `doc_lengths`: each row sums to 2048; its largest entry is exactly 512. `tenant_slots`: each slot once.
All inputs are finite; a program needn't handle non-finite values.
Results may differ from a plain program's by a relative error of at most 0.0058.
Values may be sent and summed in bfloat16 or wider, within the bound.
No kernel may reach another device: no remote copies, remote signals or barrier semaphores. Data moves between devices by JAX's collectives and lax.ppermute only.
A program may use at most 64 MiB of HBM per device.

v0:
```python
import math

import jax
import jax.numpy as jnp
from jax import lax
from jax.sharding import PartitionSpec as P

HQ = 48
KVH = 4
HD = 128
PLEN = 64
QBLK = 256


def token_layout(lengths, tenants, slots, seq_len):
    doc_ends = jnp.cumsum(lengths)
    positions = jnp.arange(seq_len, dtype=jnp.int32)
    doc_of = jnp.sum((positions[:, None] >= doc_ends[None, :]).astype(jnp.int32), axis=1)
    tenant_range = jnp.arange(slots.shape[0], dtype=jnp.int32)
    doc_slot = jnp.sum(
        jnp.where(tenants[:, None] == tenant_range[None, :], slots[None, :], 0), axis=1
    )
    doc_range = jnp.arange(lengths.shape[0], dtype=jnp.int32)
    token_slot = jnp.sum(
        jnp.where(doc_of[:, None] == doc_range[None, :], doc_slot[None, :], 0), axis=1
    )
    return (doc_of, token_slot)


def block_grads(query_blk, grad_blk, keys_all, values_all, allowed, inv_root):
    scores = (
        jnp.einsum("qhd,kd->hqk", query_blk, keys_all, preferred_element_type=jnp.float32)
        * inv_root
    )
    scores = jnp.where(allowed[None], scores, jnp.float32(-1e30))
    row_max = jnp.max(scores, axis=-1, keepdims=True)
    probs = jnp.exp(scores - row_max)
    probs = probs / jnp.sum(probs, axis=-1, keepdims=True)
    probs_b = probs.astype(jnp.bfloat16)
    grad_probs = jnp.einsum("qhd,kd->hqk", grad_blk, values_all, preferred_element_type=jnp.float32)
    row_delta = jnp.sum(probs * grad_probs, axis=-1, keepdims=True)
    grad_scores = (probs * (grad_probs - row_delta)).astype(jnp.bfloat16)
    key_grad = (
        jnp.einsum("hqk,qhd->kd", grad_scores, query_blk, preferred_element_type=jnp.float32)
        * inv_root
    )
    value_grad = jnp.einsum("hqk,qhd->kd", probs_b, grad_blk, preferred_element_type=jnp.float32)
    return (key_grad, value_grad)


def per_device(
    queries,
    keys,
    values,
    grad_out,
    prefix_keys,
    prefix_values,
    doc_lengths,
    doc_tenants,
    tenant_slots,
):
    seq_count = lax.axis_size("seq")
    tok_count = queries.shape[0]
    seq_len = tok_count * seq_count
    repeat_count = seq_count // KVH
    pref_rows = prefix_keys.shape[0] * seq_count
    doc_most = min(512, seq_len // 2)
    window = doc_most + QBLK
    inv_root = 1.0 / math.sqrt(HD)
    query_heads = queries.reshape(tok_count, HQ, HD)
    grad_heads = grad_out.reshape(tok_count, HQ, HD)
    query_seq, grad_seq = (
        lax.all_to_all(query_heads, "seq", split_axis=1, concat_axis=0, tiled=True),
        lax.all_to_all(grad_heads, "seq", split_axis=1, concat_axis=0, tiled=True),
    )
    kv_index = lax.axis_index("seq") // repeat_count
    key_rows, value_rows, pkey_rows, pvalue_rows = (
        lax.all_gather(keys, "seq", axis=0, tiled=True),
        lax.all_gather(values, "seq", axis=0, tiled=True),
        lax.all_gather(prefix_keys, "seq", axis=0, tiled=True),
        lax.all_gather(prefix_values, "seq", axis=0, tiled=True),
    )
    own_keys = lax.dynamic_slice_in_dim(key_rows, kv_index * HD, HD, 1)
    own_values = lax.dynamic_slice_in_dim(value_rows, kv_index * HD, HD, 1)
    own_pkeys = lax.dynamic_slice_in_dim(pkey_rows, kv_index * HD, HD, 1)
    own_pvalues = lax.dynamic_slice_in_dim(pvalue_rows, kv_index * HD, HD, 1)
    doc_of, token_slot = token_layout(doc_lengths[0], doc_tenants[0], tenant_slots, seq_len)
    doc_pad = jnp.concatenate([jnp.full((doc_most,), -1, jnp.int32), doc_of])
    zero_rows = jnp.zeros((doc_most, HD), jnp.bfloat16)
    key_pad = jnp.concatenate([zero_rows, own_keys], axis=0)
    value_pad = jnp.concatenate([zero_rows, own_values], axis=0)
    pref_slot = jnp.arange(pref_rows, dtype=jnp.int32) // PLEN

    def block_step(block_index, carried):
        dkey_pad, dvalue_pad, dkey_pref, dvalue_pref = carried
        row_start = jnp.asarray(block_index * QBLK).astype(jnp.int32)
        query_blk = lax.dynamic_slice_in_dim(query_seq, row_start, QBLK, 0)
        grad_blk = lax.dynamic_slice_in_dim(grad_seq, row_start, QBLK, 0)
        key_win = lax.dynamic_slice_in_dim(key_pad, row_start, window, 0)
        value_win = lax.dynamic_slice_in_dim(value_pad, row_start, window, 0)
        doc_win = lax.dynamic_slice_in_dim(doc_pad, row_start, window, 0)
        key_pos = row_start - doc_most + jnp.arange(window, dtype=jnp.int32)
        query_doc = lax.dynamic_slice_in_dim(doc_of, row_start, QBLK, 0)
        query_slot = lax.dynamic_slice_in_dim(token_slot, row_start, QBLK, 0)
        query_pos = row_start + jnp.arange(QBLK, dtype=jnp.int32)
        token_allowed = (doc_win[None, :] == query_doc[:, None]) & (
            key_pos[None, :] <= query_pos[:, None]
        )
        prefix_allowed = pref_slot[None, :] == query_slot[:, None]
        allowed = jnp.concatenate([token_allowed, prefix_allowed], axis=1)
        keys_cat = jnp.concatenate([key_win, own_pkeys], axis=0)
        values_cat = jnp.concatenate([value_win, own_pvalues], axis=0)
        key_grad, value_grad = block_grads(
            query_blk, grad_blk, keys_cat, values_cat, allowed, inv_root
        )
        old_keys = lax.dynamic_slice_in_dim(dkey_pad, row_start, window, 0)
        old_values = lax.dynamic_slice_in_dim(dvalue_pad, row_start, window, 0)
        dkey_pad = lax.dynamic_update_slice_in_dim(
            dkey_pad, old_keys + key_grad[:window], row_start, 0
        )
        dvalue_pad = lax.dynamic_update_slice_in_dim(
            dvalue_pad, old_values + value_grad[:window], row_start, 0
        )
        return (
            dkey_pad,
            dvalue_pad,
            dkey_pref + key_grad[window:],
            dvalue_pref + value_grad[window:],
        )

    zero_pad = jnp.zeros((doc_most + seq_len, HD), jnp.float32)
    zero_pref = jnp.zeros((pref_rows, HD), jnp.float32)
    dkey_pad, dvalue_pad, dkey_pref, dvalue_pref = lax.fori_loop(
        0, seq_len // QBLK, block_step, (zero_pad, zero_pad, zero_pref, zero_pref)
    )
    dkey_own = dkey_pad[doc_most:].astype(jnp.bfloat16)
    dvalue_own = dvalue_pad[doc_most:].astype(jnp.bfloat16)
    dkey_pref, dvalue_pref = lax.psum((dkey_pref, dvalue_pref), "dp")
    back_keys, back_values = (
        lax.all_to_all(
            dkey_own.reshape(seq_len, 1, HD), "seq", split_axis=0, concat_axis=1, tiled=True
        ),
        lax.all_to_all(
            dvalue_own.reshape(seq_len, 1, HD), "seq", split_axis=0, concat_axis=1, tiled=True
        ),
    )
    back_pkeys, back_pvalues = (
        lax.all_to_all(
            dkey_pref.reshape(pref_rows, 1, HD), "seq", split_axis=0, concat_axis=1, tiled=True
        ),
        lax.all_to_all(
            dvalue_pref.reshape(pref_rows, 1, HD), "seq", split_axis=0, concat_axis=1, tiled=True
        ),
    )

    def fold_heads(received):
        row_count = received.shape[0]
        widened = received.astype(jnp.float32).reshape(row_count, KVH, repeat_count, HD)
        return jnp.sum(widened, axis=2).reshape(row_count, KVH * HD)

    grad_keys = fold_heads(back_keys).astype(jnp.bfloat16)
    grad_values = fold_heads(back_values).astype(jnp.bfloat16)
    prefix_key_grads = fold_heads(back_pkeys)
    prefix_value_grads = fold_heads(back_pvalues)
    return (grad_keys, grad_values, prefix_key_grads, prefix_value_grads)


def solution(mesh):
    placed = (
        P(("dp", "seq"), None),
        P(("dp", "seq"), None),
        P(("dp", "seq"), None),
        P(("dp", "seq"), None),
        P("seq", None),
        P("seq", None),
        P("dp", None),
        P("dp", None),
        P(),
    )
    return jax.shard_map(
        per_device,
        mesh=mesh,
        in_specs=placed,
        out_specs=(P(("dp", "seq"), None), P(("dp", "seq"), None), P("seq", None), P("seq", None)),
        check_vma=False,
    )
```

profile of v0, /device:TPU:1, one launch (start us, length us, event | category | flops | bytes accessed | tf_op | source)
XLA Modules:
  0.0 554.4 jit_solution(7314837822015914566)
XLA Ops:
  7.9 2.6 copy.42
  10.5 12.0 %all-to-all-start.1 = ((bf16[128,48,128]{0,2,1:T(8,128)(2,1)}), bf16[128,48,128]{0,2,1:T(8,128)(2,1)S(1)}, u32[]{:S(2)}, u32[]{:S(2)}) async-start(bf16[128,48,128]{0,2,1:T(8,128)(2,1)} %bitcast.8), calls=%async_computation.1 | async-start | bytes 3145728 | tf_op jit(solution)/shard_map/all_to_all | solution.py:74
  23.2 1.6 copy.39
  24.9 42.4 %all-to-all-done.1 = bf16[128,48,128]{0,2,1:T(8,128)(2,1)S(1)} async-done(((bf16[128,48,128]{0,2,1:T(8,128)(2,1)}), bf16[128,48,128]{0,2,1:T(8,128)(2,1)S(1)}, u32[]{:S(2)}, u32[]{:S(2)}) %all-to-all-start.1) | async-done | bytes 1572896 | tf_op jit(solution)/shard_map/all_to_all | solution.py:74
  67.2 6.0 %all-to-all-start = ((bf16[128,48,128]{0,2,1:T(8,128)(2,1)}), bf16[128,48,128]{0,2,1:T(8,128)(2,1)}, u32[]{:S(2)}, u32[]{:S(2)}) async-start(bf16[128,48,128]{0,2,1:T(8,128)(2,1)} %bitcast.3), calls=%async_computation | async-start | bytes 3145728 | tf_op jit(solution)/shard_map/all_to_all | solution.py:73
  73.9 54.4 %all_gather.13 = bf16[384,512]{1,0:T(8,128)(2,1)S(1)} all-gather(bf16[24,512]{1,0:T(8,128)(2,1)S(1)} %copy-done.3), channel_id=1, replica_groups=mesh['dp'=32,'seq'=16] {'seq'}, dimensions={0}, use_global_device_ids=true | all-gather | bytes 417792 | tf_op jit(solution)/shard_map/all_gather | solution.py:80
  128.4 16.5 %all_gather.15 = bf16[384,512]{1,0:T(8,128)(2,1)S(1)} all-gather(bf16[24,512]{1,0:T(8,128)(2,1)S(1)} %copy-done.4), channel_id=1, replica_groups=mesh['dp'=32,'seq'=16] {'seq'}, dimensions={0}, use_global_device_ids=true | all-gather | bytes 417792 | tf_op jit(solution)/shard_map/all_gather | solution.py:81
  145.6 1.6 copy.44
  147.1 2.6 copy.41
  149.8 1.1 constant_dynamic-slice_fusion.3
  151.7 1.1 constant_dynamic-slice_fusion.5
  153.8 1.1 broadcast_in_dim.99.clone
  154.9 162.9 %while.22 = (s32[]{:T(128)}, f32[2560,128]{1,0:T(8,128)S(1)}, f32[2560,128]{1,0:T(8,128)}, f32[384,128]{1,0:T(8,128)S(1)}, f32[384,128]{1,0:T(8,128)S(1)}, /*ind...) while((s32[]{:T(128)}, f32[2560,128]{1,0:T(8,128)S(1)}, ...), condition=%wide.region_8.9_spmd.clone, body=%wide.region_4.8_spmd.clone.sunk | while | flops 1379655808 | bytes 23836984 | solution.py:133
  156.6 4.0 fusion.66
  161.6 4.7 multiply_reduce_fusion.2
  166.3 4.1 fusion.67
  170.4 2.9 convolution_bitcast_fusion.4
  173.4 1.8 fusion.68
  177.0 4.0 fusion.66
  181.9 4.7 multiply_reduce_fusion.2
  186.6 4.1 fusion.67
  190.7 2.9 convolution_bitcast_fusion.4
  193.8 1.9 fusion.68
  197.3 4.0 fusion.66
  202.3 4.7 multiply_reduce_fusion.2
  207.0 4.1 fusion.67
  211.1 2.9 convolution_bitcast_fusion.4
  214.1 1.9 fusion.68
  217.7 4.0 fusion.66
  222.7 4.7 multiply_reduce_fusion.2
  227.3 4.1 fusion.67
  231.5 2.9 convolution_bitcast_fusion.4
  234.5 1.9 fusion.68
  238.1 4.0 fusion.66
  243.0 4.7 multiply_reduce_fusion.2
  247.7 4.1 fusion.67
  251.8 2.9 convolution_bitcast_fusion.4
  254.9 1.9 fusion.68
  258.5 4.0 fusion.66
  263.4 4.7 multiply_reduce_fusion.2
  268.1 4.1 fusion.67
  272.2 2.9 convolution_bitcast_fusion.4
  275.2 1.9 fusion.68
  278.8 4.0 fusion.66
  283.7 4.7 multiply_reduce_fusion.2
  288.4 4.1 fusion.67
  292.5 2.9 convolution_bitcast_fusion.4
  295.6 1.9 fusion.68
  299.1 4.0 fusion.66
  304.1 4.7 multiply_reduce_fusion.2
  308.8 4.1 fusion.67
  312.9 2.9 convolution_bitcast_fusion.4
  315.9 1.9 fusion.68
  318.6 150.5 %all-reduce.6.cloned.1.call-done = (f32[384,1,128]{2,1,0:T(1,128)}, f32[384,1,128]{2,1,0:T(1,128)}) async-done(((f32[384,1,128]{2,1,0:T(1,128)}, f32[384,1,128]{2,1,0:T(1,128)}), (f32[384,1,128]{2,1,0:T(1,128)}, f32[384,1,128]{2,1,0:T(1,128)})) %all-reduce.6.cloned.1.call-update) | async-done | bytes 393232 | tf_op jit(solution)/shard_map/psum | solution.py:138
  469.1 22.9 %all_to_all.84 = f32[384,1,128]{2,1,0:T(1,128)S(1)} all-to-all(f32[384,1,128]{2,1,0:T(1,128)} %get-tuple-element.446), channel_id=1, replica_groups=mesh['dp'=32,'seq'=16] {'seq'}, dimensions={0} | all-to-all | bytes 393216 | tf_op jit(solution)/shard_map/all_to_all | solution.py:148
  492.0 3.4 all-to-all-start.5
  495.4 1.4 fusion.44
  497.3 1.0 reduce.2
  499.2 6.0 %all-to-all-done.5 = f32[384,1,128]{2,1,0:T(1,128)S(1)} async-done(((f32[384,1,128]{2,1,0:T(1,128)}), f32[384,1,128]{2,1,0:T(1,128)S(1)}, u32[]{:S(2)}, u32[]{:S(2)}) %all-to-all-start.5) | async-done | bytes 196640 | tf_op jit(solution)/shard_map/all_to_all | solution.py:151
  505.3 3.5 all-to-all-start.2
  508.7 1.0 reduce.3
  510.7 15.4 %all-to-all-done.2 = bf16[16,2,8192]{2,1,0:T(2,128)(2,1)S(1)} async-done(((bf16[16,2,8192]{2,1,0:T(2,128)(2,1)}), bf16[16,2,8192]{2,1,0:T(2,128)(2,1)S(1)}, u32[]{:S(2)}, u32[]{:S(2)}) %all-to-all-start.2) | async-done | bytes 524320 | tf_op jit(solution)/shard_map/all_to_all | solution.py:140
  526.1 3.5 all-to-all-start.3
  531.9 14.4 %all-to-all-done.3 = bf16[16,2,8192]{2,1,0:T(2,128)(2,1)S(1)} async-done(((bf16[16,2,8192]{2,1,0:T(2,128)(2,1)}), bf16[16,2,8192]{2,1,0:T(2,128)(2,1)S(1)}, u32[]{:S(2)}, u32[]{:S(2)}) %all-to-all-start.3) | async-done | bytes 524320 | tf_op jit(solution)/shard_map/all_to_all | solution.py:143
  (149 shorter events, 33.4 us)
Async XLA Ops:
  7.2 142.6 %all-gather.3.cloned.1.call-start = ((), (), s32[]{:S(2)}) async-start(), calls=%async_computation.6 | async-start | bytes 2228224 | tf_op jit(solution)/shard_map/all_gather | solution.py:78
  10.5 12.7 %copy-start.2 = (bf16[128,6144]{1,0:T(8,128)(2,1)S(1)}, bf16[128,6144]{1,0:T(8,128)(2,1)}, u32[]{:S(2)}) copy-start(bf16[128,6144]{1,0:T(8,128)(2,1)} %param.11) | copy-start | bytes 4718596
  10.5 56.7 %all-to-all-start.1 = ((bf16[128,48,128]{0,2,1:T(8,128)(2,1)}), bf16[128,48,128]{0,2,1:T(8,128)(2,1)S(1)}, u32[]{:S(2)}, u32[]{:S(2)}) async-start(bf16[128,48,128]{0,2,1:T(8,128)(2,1)} %bitcast.8), calls=%async_computation.1 | async-start | bytes 3145728 | tf_op jit(solution)/shard_map/all_to_all | solution.py:74
  22.5 129.3 %all-gather.5.cloned.1.call-start = ((), (), s32[]{:S(2)}) async-start(), calls=%async_computation.7 | async-start | bytes 2228224 | tf_op jit(solution)/shard_map/all_gather | solution.py:79
  24.8 48.5 %copy-start.5 = (s32[1,8]{1,0:T(1,128)S(1)}, s32[1,8]{1,0:T(1,128)}, u32[]{:S(2)}) copy-start(s32[1,8]{1,0:T(1,128)} %param.17) | copy-start | bytes 100
  24.8 48.8 %copy-start.6 = (s32[6]{0:T(128)S(1)}, s32[6]{0:T(128)}, u32[]{:S(2)}) copy-start(s32[6]{0:T(128)} %param.19) | copy-start | bytes 76
  24.8 48.8 %copy-start.7 = (s32[1,8]{1,0:T(1,128)S(1)}, s32[1,8]{1,0:T(1,128)}, u32[]{:S(2)}) copy-start(s32[1,8]{1,0:T(1,128)} %param.18) | copy-start | bytes 100
  24.8 49.1 %copy-start.3 = (bf16[24,512]{1,0:T(8,128)(2,1)S(1)}, bf16[24,512]{1,0:T(8,128)(2,1)}, u32[]{:S(2)}) copy-start(bf16[24,512]{1,0:T(8,128)(2,1)} %param.15) | copy-start | bytes 73732
  24.8 103.5 %copy-start.4 = (bf16[24,512]{1,0:T(8,128)(2,1)S(1)}, bf16[24,512]{1,0:T(8,128)(2,1)}, u32[]{:S(2)}) copy-start(bf16[24,512]{1,0:T(8,128)(2,1)} %param.16) | copy-start | bytes 73732
  67.2 79.9 %all-to-all-start = ((bf16[128,48,128]{0,2,1:T(8,128)(2,1)}), bf16[128,48,128]{0,2,1:T(8,128)(2,1)}, u32[]{:S(2)}, u32[]{:S(2)}) async-start(bf16[128,48,128]{0,2,1:T(8,128)(2,1)} %bitcast.3), calls=%async_computation | async-start | bytes 3145728 | tf_op jit(solution)/shard_map/all_to_all | solution.py:73
  73.2 395.9 %all-reduce.6.cloned.1.call-start = ((), (), s32[]{:S(2)}) async-start(), calls=%async_computation.8 | async-start | bytes 786432 | tf_op jit(solution)/shard_map/psum | solution.py:138
  317.8 0.7 copy-start
  317.8 0.7 copy-start.1
  492.0 13.3 %all-to-all-start.5 = ((f32[384,1,128]{2,1,0:T(1,128)}), f32[384,1,128]{2,1,0:T(1,128)S(1)}, u32[]{:S(2)}, u32[]{:S(2)}) async-start(f32[384,1,128]{2,1,0:T(1,128)} %get-tuple-element.447), calls=%async_computation.5 | async-start | bytes 393216 | tf_op jit(solution)/shard_map/all_to_all | solution.py:151
  505.3 20.8 %all-to-all-start.2 = ((bf16[16,2,8192]{2,1,0:T(2,128)(2,1)}), bf16[16,2,8192]{2,1,0:T(2,128)(2,1)S(1)}, u32[]{:S(2)}, u32[]{:S(2)}) async-start(bf16[16,2,8192]{2,1,0:T(2,128)(2,1)} %reshape.116), calls=%async_computation.2 | async-start | bytes 1048576 | tf_op jit(solution)/shard_map/all_to_all | solution.py:140
  526.1 20.2 %all-to-all-start.3 = ((bf16[16,2,8192]{2,1,0:T(2,128)(2,1)}), bf16[16,2,8192]{2,1,0:T(2,128)(2,1)S(1)}, u32[]{:S(2)}, u32[]{:S(2)}) async-start(bf16[16,2,8192]{2,1,0:T(2,128)(2,1)} %reshape.118), calls=%async_computation.3 | async-start | bytes 1048576 | tf_op jit(solution)/shard_map/all_to_all | solution.py:143
Sparse Core Ops, SparseCore 0:
  10.1 64.8 all-gather.2
  77.1 53.6 all-gather.4
  318.7 150.3 all-reduce.5
where the time goes:
time: 556 us; the launch traced here: 554 us
  waiting for transfers between devices  230 us (41%)
  matrix products  126 us (23%)
  blocking collectives  93.9 us (17%)
  local copies, waits for them, and re-layouts  39.3 us (7%)
  starting transfers between devices  28.4 us (5%)
  other arithmetic  22.6 us (4%)
  between operations  14 us (3%)
    psum x1, waiting for transfers between devices, per_device(): dkey_pref, dvalue_pref = lax.psum((dkey_pref, dvalue_pref), 'dp')  151 us
    all_gather x1, blocking collectives, per_device(): lax.all_gather(prefix_keys, 'seq', axis=0, tiled=True)  54.4 us
    all_to_all x1, waiting for transfers between devices, per_device(): lax.all_to_all(grad_heads, 'seq', split_axis=1, concat_axis=0, tiled=True)  42.4 us
    dot_general x8, matrix products, block_grads(): jnp.einsum('qhd,kd->hqk', grad_blk, values_all, preferred_element_type=jn...  37.3 us
    dot_general x8, matrix products, block_grads(): jnp.einsum('hqk,qhd->kd', grad_scores, query_blk, preferred_element_type=...  33.1 us
    sub x8, matrix products, block_grads(): probs = jnp.exp(scores - row_max)  32 us
    dot_general x8, matrix products, block_grads(): jnp.einsum('hqk,qhd->kd', probs_b, grad_blk, preferred_element_type=jnp.f...  23.3 us
    all_to_all x1, blocking collectives, per_device(): lax.all_to_all(dkey_pref.reshape(pref_rows, 1, HD), 'seq', split_axis=0,...  22.9 us
  transfers between devices with their start and end apart: 8, of which 5 were waited for; matrix products, arithmetic and copies ran while one was open for 4% of the time, Pallas kernels for 0%

commit v1 on v0

v1 whole, which is shorter than its diff:
```python
import functools
import math

import jax
import jax.numpy as jnp
from jax import lax
from jax.experimental import pallas as pl
from jax.experimental.pallas import tpu as pltpu
from jax.sharding import Mesh, PartitionSpec as P

HQ = 48
KVH = 4
HD = 128
PLEN = 64
DOC_MOST = 512
SEQ = ("z", "core")
DP = ("y", "x")
NT = (((1,), (1,)), ((), ()))
NN = (((1,), (0,)), ((), ()))


def grads_kernel(per, q_ref, g_ref, *refs):
    k_refs, v_refs, (pk_ref, pv_ref, bias_ref) = refs[:5], refs[5:10], refs[10:13]
    near_k, near_v, far_k, far_v, pref_ref = refs[13:]
    heads = q_ref.shape[1] // HD
    toks = q_ref.shape[0]
    scale = 1.0 / math.sqrt(HD)
    log2e = scale * math.log2(math.e)
    keys = jnp.concatenate([r[...] for r in k_refs] + [pk_ref[...]], axis=0)
    values = jnp.concatenate([r[...] for r in v_refs] + [pv_ref[...]], axis=0)
    rows = keys.shape[0]
    bias = jnp.concatenate([bias_ref[...]] * per, axis=1)

    def step(i, sums):
        dk, dv = sums
        cols = [pl.ds(pl.multiple_of((i * per + j) * HD, HD), HD) for j in range(per)]
        q = jnp.concatenate([q_ref[:, c] for c in cols], axis=0)
        g = jnp.concatenate([g_ref[:, c] for c in cols], axis=0)
        s = lax.dot_general(keys, q, NT, preferred_element_type=jnp.float32) + bias
        dp = lax.dot_general(values, g, NT, preferred_element_type=jnp.float32)
        top = jnp.max(s, axis=0, keepdims=True) * log2e
        e = jnp.exp2(s * log2e - top)
        inv = 1.0 / jnp.sum(e, axis=0, keepdims=True)
        delta = jnp.sum(e * dp, axis=0, keepdims=True) * inv
        p = e * inv
        ds = (p * (dp - delta)).astype(jnp.bfloat16)
        dk = dk + lax.dot_general(ds, q, NN, preferred_element_type=jnp.float32)
        dv = dv + lax.dot_general(
            p.astype(jnp.bfloat16), g, NN, preferred_element_type=jnp.float32
        )
        return dk, dv

    zero = jnp.zeros((rows, HD), jnp.float32)
    dk, dv = lax.fori_loop(0, heads // per, step, (zero, zero))
    dk = dk * scale
    near = 3 * toks
    win = 5 * toks
    near_k[...] = dk[:near]
    near_v[...] = dv[:near]
    far_k[...] = dk[near:win].astype(jnp.bfloat16)
    far_v[...] = dv[near:win].astype(jnp.bfloat16)
    halves, parts, both, _ = pref_ref.shape
    each = both // 2
    for half in range(halves):
        for part in range(parts):
            at = win + (part * halves + half) * each
            pref_ref[half, part, :each, :] = dk[at : at + each]
            pref_ref[half, part, each:, :] = dv[at : at + each]


def grads(q, g, blocks, pref, bias, halves, parts, per=2):
    toks, width = q.shape
    prefs = pref.shape[0]
    both = 2 * prefs // (halves * parts)
    run = width // KVH

    def cols(rows, wide, shift=0):
        return pl.BlockSpec((rows, wide), lambda h: (0, h + shift))

    return pl.pallas_call(
        functools.partial(grads_kernel, per),
        grid=(KVH,),
        in_specs=[cols(toks, run)] * 2
        + [cols(toks, HD)] * 5
        + [cols(toks, HD, KVH)] * 5
        + [cols(prefs, HD), cols(prefs, HD, KVH)]
        + [pl.BlockSpec(bias.shape, lambda h: (0, 0))],
        out_specs=[cols(3 * toks, HD)] * 2
        + [cols(2 * toks, HD)] * 2
        + [pl.BlockSpec((halves, parts, both, HD), lambda h: (0, 0, 0, h))],
        out_shape=[jax.ShapeDtypeStruct((3 * toks, KVH * HD), jnp.float32)] * 2
        + [jax.ShapeDtypeStruct((2 * toks, KVH * HD), jnp.bfloat16)] * 2
        + [jax.ShapeDtypeStruct((halves, parts, both, KVH * HD), jnp.float32)],
        compiler_params=pltpu.CompilerParams(vmem_limit_bytes=56 << 20),
        cost_estimate=pl.CostEstimate(
            flops=8 * toks * width * bias.shape[0],
            bytes_accessed=10 << 20,
            transcendentals=toks * width // HD * bias.shape[0],
        ),
    )(q, g, *blocks, *blocks, pref, pref, bias)


def visible_bias(lengths, tenants, slots, index, shards, toks, prefs):
    ends = jnp.cumsum(lengths)
    slot_of = jnp.sum(
        jnp.where(tenants[:, None] == jnp.arange(slots.shape[0])[None, :], slots[None, :], 0), axis=1
    )
    here = index * toks + jnp.arange(toks, dtype=jnp.int32)
    doc = jnp.sum((here[None, :] >= ends[:, None]).astype(jnp.int32), axis=0)
    starts = ends - lengths
    pick = doc[None, :] == jnp.arange(lengths.shape[0])[:, None]
    first = jnp.sum(jnp.where(pick, starts[:, None], 0), axis=0)
    slot = jnp.sum(jnp.where(pick, slot_of[:, None], 0), axis=0)
    key = jnp.concatenate([s * toks + jnp.arange(toks, dtype=jnp.int32) for s in shards])
    token_ok = (key[:, None] >= first[None, :]) & (key[:, None] <= here[None, :])
    pref_ok = (jnp.arange(prefs, dtype=jnp.int32) // PLEN)[:, None] == slot[None, :]
    ok = jnp.concatenate([token_ok, pref_ok], axis=0)
    return jnp.where(ok, 0.0, -1e30).astype(jnp.float32)


def per_device(
    queries, keys, values, grad_out, prefix_keys, prefix_values, doc_lengths, doc_tenants, tenant_slots
):
    toks = queries.shape[0]
    parts, halves = lax.axis_size("z"), lax.axis_size("core")
    count = parts * halves
    copies = lax.axis_size("y") * lax.axis_size("x")
    index, core = lax.axis_index(SEQ), lax.axis_index("core")

    def shift(x, steps):
        pairs = [(i, i + 2 * steps) for i in range(count) if 0 <= i + 2 * steps < count]
        return lax.ppermute(x, SEQ, pairs)

    def swap(x):
        return lax.ppermute(x, SEQ, [(i, i ^ 1) for i in range(count)])

    own = jnp.concatenate([keys, values], axis=1)
    back1, back2 = shift(own, 1), shift(own, 2)
    pref = lax.all_gather(
        jnp.concatenate([prefix_keys, prefix_values], axis=1), SEQ, axis=0, tiled=True
    )
    cross1 = swap(back1)
    cross02 = swap(jnp.where(core == 0, own, back2))
    even = core == 0
    shards = [
        index - 4,
        index - 2,
        index,
        jnp.where(even, index - 3, index - 1),
        jnp.where(even, index - 1, index - 3),
    ]
    bias = visible_bias(
        doc_lengths[0], doc_tenants[0], tenant_slots, index, shards, toks, pref.shape[0]
    )
    near_k, near_v, far_k, far_v, dpref = grads(
        queries, grad_out, (back2, back1, own, cross02, cross1), pref, bias, halves, parts
    )

    other = swap(jnp.where(even, dpref[1], dpref[0]))
    mine = jnp.where(even, dpref[0], dpref[1]) + other
    got = lax.all_to_all(mine.astype(jnp.bfloat16), "z", split_axis=0, concat_axis=0, tiled=True)
    summed = jnp.sum(got.astype(jnp.float32), axis=0)
    pieces = summed.reshape(copies, -1, HD)
    got = lax.all_to_all(pieces, DP, split_axis=0, concat_axis=0, tiled=True)
    piece = jnp.sum(got, axis=0)
    spread = jnp.broadcast_to(piece[None], pieces.shape)
    full = lax.all_to_all(spread, DP, split_axis=0, concat_axis=0, tiled=True)
    full = full.reshape(summed.shape)
    each = prefix_keys.shape[0]

    far = swap(jnp.concatenate([far_k, far_v], axis=1)).astype(jnp.float32)
    near = jnp.concatenate([near_k, near_v], axis=1)
    zero = jnp.zeros((toks, far.shape[1]), jnp.float32)
    two = near[:toks] + jnp.where(even, zero, far[:toks])
    one = near[toks : 2 * toks] + far[toks:]
    home = near[2 * toks :] + jnp.where(even, far[:toks], zero)
    one = shift(one.astype(jnp.bfloat16), -1)
    two = shift(two.astype(jnp.bfloat16), -2)
    total = (home + one.astype(jnp.float32) + two.astype(jnp.float32)).astype(jnp.bfloat16)
    wide = KVH * HD
    return total[:, :wide], total[:, wide:], full[:each], full[each:]


def solution(mesh):
    devices = mesh.devices.reshape(8, 4, 8, 2)
    mesh = Mesh(devices, ("y", "x", "z", "core"))
    rows, dp, seq = P(("y", "x", "z", "core"), None), P(DP, None), P(SEQ, None)
    return jax.shard_map(
        per_device,
        mesh=mesh,
        in_specs=(rows, rows, rows, rows, seq, seq, dp, dp, P()),
        out_specs=(rows, rows, seq, seq),
        check_vma=False,
    )
```

time: 556 us -> 155 us (0.28)
  waiting for transfers between devices: 230 us -> 27.1 us
  matrix products: 126 us -> 0 us
  blocking collectives: 93.9 us -> 29.3 us
  Pallas kernels: 0 us -> 36.3 us
  local copies, waits for them, and re-layouts: 39.3 us -> 7.84 us
  starting transfers between devices: 28.4 us -> 42 us
  between operations: 14 us -> 0.99 us
  other arithmetic: 22.6 us -> 10.2 us
    psum x1 -> x0, waiting for transfers between devices: 151 us -> none  [per_device(): dkey_pref, dvalue_pref = lax.psum((dkey_pref, dvalue_pref), 'dp')]
    dot_general x24 -> x0, matrix products: 93.6 us -> none  [the longest x8 37.3 us: block_grads(): jnp.einsum('qhd,kd->hqk', grad_blk, values_all, preferred_element_type=jn...]
    all_to_all x5 -> x3, waiting for transfers between devices: 78.2 us -> 24.1 us  [the longest x1 10.2 us: per_device(): lax.all_to_all(mine.astype(jnp.bfloat16), 'z', split_axis=0, concat_axis=...]
    all_gather x2 -> x1, blocking collectives: 71 us -> 29.3 us  [per_device(): lax.all_gather(jnp.concatenate([prefix_keys, prefix_values], axis=1), SEQ...]
    pallas_call x0 -> x1, Pallas kernels: none -> 36.3 us  [grads(): pl.pallas_call(functools.partial(grads_kernel, per), grid=(KVH,), in_spec...]
    sub x8 -> x0, matrix products: 32 us -> none  [block_grads(): probs = jnp.exp(scores - row_max)]
    ppermute x0 -> x8, starting transfers between devices: none -> 23 us  [the longest x4 13.2 us: shift(): return lax.ppermute(x, SEQ, pairs)]
    all_to_all x1 -> x0, blocking collectives: 22.9 us -> none  [per_device(): lax.all_to_all(dkey_pref.reshape(pref_rows, 1, HD), 'seq', split_axis=0,...]
  transfers between devices with their start and end apart: 8 -> 11, of which waited for: 5 -> 4; matrix products, arithmetic and copies ran while one was open for 4% -> 7% of each run, Pallas kernels for 0% -> 0%
where the time goes in v1:
time: 155 us; the launch traced here: 154 us
  starting transfers between devices  42 us (27%)
  Pallas kernels  36.3 us (23%)
  blocking collectives  29.3 us (19%)
  waiting for transfers between devices  27.1 us (17%)
  other arithmetic  10.2 us (7%)
  local copies, waits for them, and re-layouts  7.84 us (5%)
    pallas_call x1, Pallas kernels, grads(): pl.pallas_call(functools.partial(grads_kernel, per), grid=(KVH,), in_spec...  36.3 us
    all_gather x1, blocking collectives, per_device(): lax.all_gather(jnp.concatenate([prefix_keys, prefix_values], axis=1), SEQ...  29.3 us
    ppermute x4, starting transfers between devices, shift(): return lax.ppermute(x, SEQ, pairs)  13.2 us
    all_to_all x1, waiting for transfers between devices, per_device(): lax.all_to_all(mine.astype(jnp.bfloat16), 'z', split_axis=0, concat_axis=...  10.2 us
    ppermute x4, starting transfers between devices, swap(): return lax.ppermute(x, SEQ, [(i, i ^ 1) for i in range(count)])  9.75 us
    all_to_all x1, starting transfers between devices, per_device(): got = lax.all_to_all(pieces, DP, split_axis=0, concat_axis=0, tiled=True)  9.67 us
    all_to_all x1, waiting for transfers between devices, per_device(): full = lax.all_to_all(spread, DP, split_axis=0, concat_axis=0, tiled=True)  8.63 us
    all_to_all x1, waiting for transfers between devices, per_device(): got = lax.all_to_all(pieces, DP, split_axis=0, concat_axis=0, tiled=True)  5.29 us
  transfers between devices with their start and end apart: 11, of which 4 were waited for; matrix products, arithmetic and copies ran while one was open for 7% of the time, Pallas kernels for 0%

profile of v1, /device:TPU:1, one launch (start us, length us, event | category | flops | bytes accessed | tf_op | source)
XLA Modules:
  0.0 153.7 jit_solution(11708862267483915654)
XLA Ops:
  0.6 0.9 constant_dynamic-update-slice_fusion.1
  1.5 0.9 constant_dynamic-update-slice_fusion.refs_2_.refs_7_
  2.5 0.0 copy-start.2
  2.5 6.7 %collective-permute-start = (bf16[128,1024]{1,0:T(8,128)(2,1)S(1)}, bf16[128,1024]{1,0:T(8,128)(2,1)S(1)}, u32[]{:S(2)}, u32[]{:S(2)}) collective-permute-start(bf16[128,1024]{1,0:T(8,128)(2,1)S(1)} %constant_dynamic-update-slice_fusion.refs_2_.refs_7_), channel_id=1, source_target_pairs={{0,4},{1,5},{2,6},{3,7},{4,8},{5,9},{6,10},{7,11},{8,12},{9,13},{1... | collective-permute-start | bytes 786440 | tf_op jit(solution)/shard_map/ppermute | solution.py:132
  9.1 4.0 %collective-permute-start.1 = (bf16[128,1024]{1,0:T(8,128)(2,1)S(1)}, bf16[128,1024]{1,0:T(8,128)(2,1)S(1)}, u32[]{:S(2)}, u32[]{:S(2)}) collective-permute-start(bf16[128,1024]{1,0:T(8,128)(2,1)S(1)} %constant_dynamic-update-slice_fusion.refs_2_.refs_7_), channel_id=1, source_target_pairs={{0,2},{1,3},{2,4},{3,5},{4,6},{5,7},{6,8},{7,9},{8,10},{9,11},{10,... | collective-permute-start | bytes 786440 | tf_op jit(solution)/shard_map/ppermute | solution.py:132
  13.2 0.8 reduce-window.7
  14.0 0.7 bitcast_subtract_fusion
  14.8 0.1 convert_reduce_fusion.1
  14.8 0.9 select_reduce_fusion.1
  15.7 0.1 select_reduce_fusion.2
  15.8 0.2 compare_and_fusion
  15.9 0.1 broadcast_compare_fusion
  16.1 0.8 add_select_fusion.refs_12_
  16.9 0.8 pad_maximum_fusion.1
  17.7 0.0 collective-permute-done.refs_0_.refs_5_
  17.7 0.0 copy-start.3
  17.7 3.1 %collective-permute-start.2 = (bf16[128,1024]{1,0:T(8,128)(2,1)S(1)}, bf16[128,1024]{1,0:T(8,128)(2,1)S(1)}, u32[]{:S(2)}, u32[]{:S(2)}) collective-permute-start(bf16[128,1024]{1,0:T(8,128)(2,1)S(1)} %broadcast_select_fusion), channel_id=1, source_target_pairs={{0,1},{1,0},{2,3},{3,2},{4,5},{5,4},{6,7},{7,6},{8,9},{9,8},{10,11... | collective-permute-start | bytes 786440 | tf_op jit(solution)/shard_map/ppermute | solution.py:135
  20.9 0.0 collective-permute-done.1.refs_1_.refs_6_
  20.9 0.0 copy-start.6
  20.9 2.3 %collective-permute-start.3 = (bf16[128,1024]{1,0:T(8,128)(2,1)S(1)}, bf16[128,1024]{1,0:T(8,128)(2,1)S(1)}, u32[]{:S(2)}, u32[]{:S(2)}) collective-permute-start(bf16[128,1024]{1,0:T(8,128)(2,1)S(1)} %collective-permute-done.1.refs_1_.refs_6_), channel_id=1, source_target_pairs={{0,1},{1,0},{2,3},{3,2},{4,5},{5,4},{6,7},{7,6},{8,9},{9,8},{10,11... | collective-permute-start | bytes 786440 | tf_op jit(solution)/shard_map/ppermute | solution.py:135
  23.2 29.3 %all_gather.3.refs_10_.refs_11_ = bf16[384,1024]{1,0:T(8,128)(2,1)} all-gather(bf16[24,1024]{1,0:T(8,128)(2,1)S(1)} %pad_maximum_fusion.1), channel_id=1, replica_groups=mesh['y'=8,'x'=4,'z'=8,'core'=2] {'z','core'}, dimensions={0}, use_global_device_ids=true | all-gather | bytes 835584 | tf_op jit(solution)/shard_map/all_gather | solution.py:139
  52.5 0.0 collective-permute-done.2.refs_3_.refs_8_
  52.5 0.0 collective-permute-done.3.refs_4_.refs_9_
  52.5 0.0 copy-done.2
  52.5 0.0 copy-done.3
  52.5 0.0 copy-done.6
  52.5 0.7 copy-done.7
  53.2 0.7 copy-done.8
  53.9 36.3 %shard_map.120 = (f32[384,512]{1,0:T(8,128)}, f32[384,512]{1,0:T(8,128)}, bf16[256,512]{1,0:T(8,128)(2,1)}, bf16[256,512]{1,0:T(8,128)(2,1)}, f32[2,8,48,512]{3,2,1,0:T(8,128)}) custom-call(bf16[128,6144]{1,0:T(8,128)(2,1)} %q_ref.1, bf16[128,6144]{1,0:T(8,128)(2,1)} %g_ref.1, bf16[128,1024]{1,0:T(8,128)(2,1)} %copy-done.3, bf16[128,1024]{1,0:T(8,128)(2,1)} %copy-done.6, ...), custom_call_target="tpu_custom_call" | custom-call | flops 6442450944 | bytes 10485760 | tf_op jit(solution)/shard_map/pallas_call | solution.py:80
  90.2 0.0 copy-start.4
  90.2 0.0 copy-start.5
  90.2 0.0 copy-start
  90.3 1.7 %select_bitcast_fusion = f32[8,48,512]{2,1,0:T(8,128)S(1)} fusion(f32[2,8,48,512]{3,2,1,0:T(8,128)} %get-tuple-element.13, pred[]{:T(512)S(6)} %eq.22), kind=kLoop, calls=%fused_computation.3 | loop fusion | flops 196608 | bytes 2359297 | tf_op jit(solution)/shard_map/jit(_where)/select_n | solution.py:159
  91.9 2.1 %collective-permute-start.7 = (f32[8,48,512]{2,1,0:T(8,128)S(1)}, f32[8,48,512]{2,1,0:T(8,128)S(1)}, u32[]{:S(2)}, u32[]{:S(2)}) collective-permute-start(f32[8,48,512]{2,1,0:T(8,128)S(1)} %select_bitcast_fusion), channel_id=1, source_target_pairs={{0,1},{1,0},{2,3},{3,2},{4,5},{5,4},{6,7},{7,6},{8,9},{9,8},{10,11... | collective-permute-start | bytes 2359304 | tf_op jit(solution)/shard_map/ppermute | solution.py:135
  94.0 0.0 copy-done.4
  94.0 0.0 copy-done.5
  94.0 0.9 pad_maximum_fusion
  94.9 2.2 %collective-permute-start.4 = (bf16[256,1024]{1,0:T(8,128)(2,1)}, bf16[256,1024]{1,0:T(8,128)(2,1)S(1)}, u32[]{:S(2)}, u32[]{:S(2)}) collective-permute-start(bf16[256,1024]{1,0:T(8,128)(2,1)} %pad_maximum_fusion), channel_id=1, source_target_pairs={{0,1},{1,0},{2,3},{3,2},{4,5},{5,4},{6,7},{7,6},{8,9},{9,8},{10,11... | collective-permute-start | bytes 1572872 | tf_op jit(solution)/shard_map/ppermute | solution.py:135
  97.1 0.0 collective-permute-done.7
  97.2 0.0 copy-done
  97.2 0.9 fusion
  98.1 5.0 %all-to-all-start = ((bf16[8,48,512]{2,1,0:T(8,128)(2,1)}), bf16[8,48,512]{2,1,0:T(8,128)(2,1)S(1)}, u32[]{:S(2)}, u32[]{:S(2)}) async-start(bf16[8,48,512]{2,1,0:T(8,128)(2,1)} %fusion), calls=%async_computation | async-start | bytes 786432 | tf_op jit(solution)/shard_map/all_to_all | solution.py:161
  103.1 1.2 constant_dynamic-update-slice_fusion.4
  104.3 0.0 copy-done.1
  104.3 0.1 constant_dynamic-update-slice_fusion.3
  104.4 0.0 collective-permute-done.4
  104.4 0.1 convert_element_type.28
  104.5 1.0 fusion.2
  105.5 1.3 collective-permute-start.5
  106.8 1.3 collective-permute-start.6
  108.1 10.2 %all-to-all-done = bf16[8,48,512]{2,1,0:T(8,128)(2,1)S(1)} async-done(((bf16[8,48,512]{2,1,0:T(8,128)(2,1)}), bf16[8,48,512]{2,1,0:T(8,128)(2,1)S(1)}, u32[]{:S(2)}, u32[]{:S(2)}) %all-to-all-start) | async-done | bytes 393248 | tf_op jit(solution)/shard_map/all_to_all | solution.py:161
  118.3 0.1 convert_reduce_fusion
  118.3 0.7 reshape.73
  119.0 9.7 %all-to-all-start.1 = ((f32[32,6,128]{2,1,0:T(8,128)}), f32[32,6,128]{2,1,0:T(8,128)S(1)}, u32[]{:S(2)}, u32[]{:S(2)}) async-start(f32[32,6,128]{2,1,0:T(8,128)} %reshape.73), calls=%async_computation.1 | async-start | bytes 262144 | tf_op jit(solution)/shard_map/all_to_all | solution.py:164
  128.7 0.0 collective-permute-done.5
  128.7 3.0 %collective-permute-done.6 = bf16[128,1024]{1,0:T(8,128)(2,1)} collective-permute-done((bf16[128,1024]{1,0:T(8,128)(2,1)}, bf16[128,1024]{1,0:T(8,128)(2,1)}, u32[]{:S(2)}, u32[]{:S(2)}) %collective-permute-start.6) | collective-permute-done | bytes 262176 | tf_op jit(solution)/shard_map/ppermute | solution.py:132
  131.6 1.1 fusion.5
  132.7 5.3 %all-to-all-done.1 = f32[32,6,128]{2,1,0:T(8,128)S(1)} async-done(((f32[32,6,128]{2,1,0:T(8,128)}), f32[32,6,128]{2,1,0:T(8,128)S(1)}, u32[]{:S(2)}, u32[]{:S(2)}) %all-to-all-start.1) | async-done | bytes 98336 | tf_op jit(solution)/shard_map/all_to_all | solution.py:164
  138.1 0.7 broadcast_in_dim.69
  138.7 4.4 %all-to-all-start.2 = ((f32[32,6,128]{2,1,0:T(8,128)}), f32[32,6,128]{2,1,0:T(8,128)S(1)}, u32[]{:S(2)}, u32[]{:S(2)}) async-start(f32[32,6,128]{2,1,0:T(8,128)} %broadcast_in_dim.69), calls=%async_computation.2 | async-start | bytes 262144 | tf_op jit(solution)/shard_map/all_to_all | solution.py:167
  143.1 0.7 fusion.9
  143.8 8.6 %all-to-all-done.2 = f32[32,6,128]{2,1,0:T(8,128)S(1)} async-done(((f32[32,6,128]{2,1,0:T(8,128)}), f32[32,6,128]{2,1,0:T(8,128)S(1)}, u32[]{:S(2)}, u32[]{:S(2)}) %all-to-all-start.2) | async-done | bytes 98336 | tf_op jit(solution)/shard_map/all_to_all | solution.py:167
  152.5 0.6 slice.52
  153.1 0.6 slice.54
  (13 shorter events, 0.1 us)
Async XLA Ops:
  2.5 50.0 %copy-start.2 = (bf16[128,1024]{1,0:T(8,128)(2,1)}, bf16[128,1024]{1,0:T(8,128)(2,1)S(1)}, u32[]{:S(2)}) copy-start(bf16[128,1024]{1,0:T(8,128)(2,1)S(1)} %constant_dynamic-update-slice_fusion.refs_2_.refs_7_) | copy-start | bytes 786436
  2.5 15.2 %collective-permute-start = (bf16[128,1024]{1,0:T(8,128)(2,1)S(1)}, bf16[128,1024]{1,0:T(8,128)(2,1)S(1)}, u32[]{:S(2)}, u32[]{:S(2)}) collective-permute-start(bf16[128,1024]{1,0:T(8,128)(2,1)S(1)} %constant_dynamic-update-slice_fusion.refs_2_.refs_7_), channel_id=1, source_target_pairs={{0,4},{1,5},{2,6},{3,7},{4,8},{5,9},{6,10},{7,11},{8,12},{9,13},{1... | collective-permute-start | bytes 786440 | tf_op jit(solution)/shard_map/ppermute | solution.py:132
  9.1 11.7 %collective-permute-start.1 = (bf16[128,1024]{1,0:T(8,128)(2,1)S(1)}, bf16[128,1024]{1,0:T(8,128)(2,1)S(1)}, u32[]{:S(2)}, u32[]{:S(2)}) collective-permute-start(bf16[128,1024]{1,0:T(8,128)(2,1)S(1)} %constant_dynamic-update-slice_fusion.refs_2_.refs_7_), channel_id=1, source_target_pairs={{0,2},{1,3},{2,4},{3,5},{4,6},{5,7},{6,8},{7,9},{8,10},{9,11},{10,... | collective-permute-start | bytes 786440 | tf_op jit(solution)/shard_map/ppermute | solution.py:132
  17.7 34.8 %copy-start.3 = (bf16[128,1024]{1,0:T(8,128)(2,1)}, bf16[128,1024]{1,0:T(8,128)(2,1)S(1)}, u32[]{:S(2)}) copy-start(bf16[128,1024]{1,0:T(8,128)(2,1)S(1)} %collective-permute-done.refs_0_.refs_5_) | copy-start | bytes 786436
  17.7 34.7 %collective-permute-start.2 = (bf16[128,1024]{1,0:T(8,128)(2,1)S(1)}, bf16[128,1024]{1,0:T(8,128)(2,1)S(1)}, u32[]{:S(2)}, u32[]{:S(2)}) collective-permute-start(bf16[128,1024]{1,0:T(8,128)(2,1)S(1)} %broadcast_select_fusion), channel_id=1, source_target_pairs={{0,1},{1,0},{2,3},{3,2},{4,5},{5,4},{6,7},{7,6},{8,9},{9,8},{10,11... | collective-permute-start | bytes 786440 | tf_op jit(solution)/shard_map/ppermute | solution.py:135
  20.9 31.6 %copy-start.6 = (bf16[128,1024]{1,0:T(8,128)(2,1)}, bf16[128,1024]{1,0:T(8,128)(2,1)S(1)}, u32[]{:S(2)}) copy-start(bf16[128,1024]{1,0:T(8,128)(2,1)S(1)} %collective-permute-done.1.refs_1_.refs_6_) | copy-start | bytes 786436
  20.9 31.6 %collective-permute-start.3 = (bf16[128,1024]{1,0:T(8,128)(2,1)S(1)}, bf16[128,1024]{1,0:T(8,128)(2,1)S(1)}, u32[]{:S(2)}, u32[]{:S(2)}) collective-permute-start(bf16[128,1024]{1,0:T(8,128)(2,1)S(1)} %collective-permute-done.1.refs_1_.refs_6_), channel_id=1, source_target_pairs={{0,1},{1,0},{2,3},{3,2},{4,5},{5,4},{6,7},{7,6},{8,9},{9,8},{10,11... | collective-permute-start | bytes 786440 | tf_op jit(solution)/shard_map/ppermute | solution.py:135
  52.5 0.7 copy-start.7
  53.2 0.7 copy-start.8
  90.2 3.8 %copy-start.4 = (bf16[256,512]{1,0:T(8,128)(2,1)S(1)}, bf16[256,512]{1,0:T(8,128)(2,1)}, u32[]{:S(2)}) copy-start(bf16[256,512]{1,0:T(8,128)(2,1)} %get-tuple-element.11) | copy-start | bytes 786436
  90.2 3.8 %copy-start.5 = (bf16[256,512]{1,0:T(8,128)(2,1)S(1)}, bf16[256,512]{1,0:T(8,128)(2,1)}, u32[]{:S(2)}) copy-start(bf16[256,512]{1,0:T(8,128)(2,1)} %get-tuple-element.12) | copy-start | bytes 786436
  90.2 6.9 %copy-start = (f32[2,8,48,512]{3,2,1,0:T(8,128)S(1)}, f32[2,8,48,512]{3,2,1,0:T(8,128)}, u32[]{:S(2)}) copy-start(f32[2,8,48,512]{3,2,1,0:T(8,128)} %get-tuple-element.13) | copy-start | bytes 4718596
  91.9 5.2 %collective-permute-start.7 = (f32[8,48,512]{2,1,0:T(8,128)S(1)}, f32[8,48,512]{2,1,0:T(8,128)S(1)}, u32[]{:S(2)}, u32[]{:S(2)}) collective-permute-start(f32[8,48,512]{2,1,0:T(8,128)S(1)} %select_bitcast_fusion), channel_id=1, source_target_pairs={{0,1},{1,0},{2,3},{3,2},{4,5},{5,4},{6,7},{7,6},{8,9},{9,8},{10,11... | collective-permute-start | bytes 2359304 | tf_op jit(solution)/shard_map/ppermute | solution.py:135
  94.9 9.5 %collective-permute-start.4 = (bf16[256,1024]{1,0:T(8,128)(2,1)}, bf16[256,1024]{1,0:T(8,128)(2,1)S(1)}, u32[]{:S(2)}, u32[]{:S(2)}) collective-permute-start(bf16[256,1024]{1,0:T(8,128)(2,1)} %pad_maximum_fusion), channel_id=1, source_target_pairs={{0,1},{1,0},{2,3},{3,2},{4,5},{5,4},{6,7},{7,6},{8,9},{9,8},{10,11... | collective-permute-start | bytes 1572872 | tf_op jit(solution)/shard_map/ppermute | solution.py:135
  98.1 6.2 %copy-start.1 = (f32[384,512]{1,0:T(8,128)S(1)}, f32[384,512]{1,0:T(8,128)}, u32[]{:S(2)}) copy-start(f32[384,512]{1,0:T(8,128)} %get-tuple-element.10) | copy-start | bytes 2359300
  98.1 20.2 %all-to-all-start = ((bf16[8,48,512]{2,1,0:T(8,128)(2,1)}), bf16[8,48,512]{2,1,0:T(8,128)(2,1)S(1)}, u32[]{:S(2)}, u32[]{:S(2)}) async-start(bf16[8,48,512]{2,1,0:T(8,128)(2,1)} %fusion), calls=%async_computation | async-start | bytes 786432 | tf_op jit(solution)/shard_map/all_to_all | solution.py:161
  105.5 23.2 %collective-permute-start.5 = (bf16[128,1024]{1,0:T(8,128)(2,1)}, bf16[128,1024]{1,0:T(8,128)(2,1)S(1)}, u32[]{:S(2)}, u32[]{:S(2)}) collective-permute-start(bf16[128,1024]{1,0:T(8,128)(2,1)} %get-tuple-element.16), channel_id=1, source_target_pairs={{2,0},{3,1},{4,2},{5,3},{6,4},{7,5},{8,6},{9,7},{10,8},{11,9},{12,... | collective-permute-start | bytes 786440 | tf_op jit(solution)/shard_map/ppermute | solution.py:132
  106.8 24.9 %collective-permute-start.6 = (bf16[128,1024]{1,0:T(8,128)(2,1)}, bf16[128,1024]{1,0:T(8,128)(2,1)}, u32[]{:S(2)}, u32[]{:S(2)}) collective-permute-start(bf16[128,1024]{1,0:T(8,128)(2,1)} %get-tuple-element.17), channel_id=1, source_target_pairs={{4,0},{5,1},{6,2},{7,3},{8,4},{9,5},{10,6},{11,7},{12,8},{13,9},{1... | collective-permute-start | bytes 786440 | tf_op jit(solution)/shard_map/ppermute | solution.py:132
  119.0 19.0 %all-to-all-start.1 = ((f32[32,6,128]{2,1,0:T(8,128)}), f32[32,6,128]{2,1,0:T(8,128)S(1)}, u32[]{:S(2)}, u32[]{:S(2)}) async-start(f32[32,6,128]{2,1,0:T(8,128)} %reshape.73), calls=%async_computation.1 | async-start | bytes 262144 | tf_op jit(solution)/shard_map/all_to_all | solution.py:164
  138.7 13.8 %all-to-all-start.2 = ((f32[32,6,128]{2,1,0:T(8,128)}), f32[32,6,128]{2,1,0:T(8,128)S(1)}, u32[]{:S(2)}, u32[]{:S(2)}) async-start(f32[32,6,128]{2,1,0:T(8,128)} %broadcast_in_dim.69), calls=%async_computation.2 | async-start | bytes 262144 | tf_op jit(solution)/shard_map/all_to_all | solution.py:167

commit v2 on v1

v2 whole, which is shorter than its diff:
```python
import functools
import math

import jax
import jax.numpy as jnp
from jax import lax
from jax.experimental import pallas as pl
from jax.experimental.pallas import tpu as pltpu
from jax.sharding import Mesh, PartitionSpec as P

HQ = 48
KVH = 4
HD = 128
PLEN = 64
NT = (((1,), (1,)), ((), ()))
NN = (((1,), (0,)), ((), ()))
SEQ = ("z", "core")
SCALE = 1.0 / math.sqrt(HD)
TO_LOG2 = SCALE * math.log2(math.e)
F32 = jnp.float32
BF16 = jnp.bfloat16


def stacked(ref):
    return jnp.concatenate(
        [ref[:, j * HD : (j + 1) * HD] for j in range(ref.shape[1] // HD)], axis=0
    )


def joined(ref):
    return jnp.concatenate([ref[0, j : j + 1, :] for j in range(ref.shape[1])], axis=1)


def split(ref, row):
    for j in range(ref.shape[1]):
        ref[0, j : j + 1, :] = row[:, j * HD : (j + 1) * HD]


def token_stats_kernel(q_ref, g_ref, *refs):
    kv_refs, (bias_ref, top_ref, sum_ref, dot_ref) = refs[:-4], refs[-4:]
    blocks = len(kv_refs) // 2
    keys = jnp.concatenate([r[0] for r in kv_refs[:blocks]], axis=0)
    values = jnp.concatenate([r[0] for r in kv_refs[blocks:]], axis=0)
    toks = q_ref.shape[0]
    s_all = lax.dot_general(keys, stacked(q_ref), NT, preferred_element_type=F32)
    dp_all = lax.dot_general(values, stacked(g_ref), NT, preferred_element_type=F32)
    for j in range(q_ref.shape[1] // HD):
        cols = slice(j * toks, (j + 1) * toks)
        top = total = dot = None
        for b in range(blocks):
            rows = slice(b * toks, (b + 1) * toks)
            s = (s_all[rows, cols] + bias_ref[rows, :]).reshape(toks // 8, 8, toks)
            dp = dp_all[rows, cols].reshape(toks // 8, 8, toks)
            new = jnp.max(s, axis=0)
            new = new if top is None else jnp.maximum(top, new)
            e = jnp.exp2(s * TO_LOG2 - (new * TO_LOG2)[None])
            e_sum, e_dot = jnp.sum(e, axis=0), jnp.sum(e * dp, axis=0)
            if top is not None:
                old = jnp.exp2(top * TO_LOG2 - new * TO_LOG2)
                e_sum, e_dot = old * total + e_sum, old * dot + e_dot
            top, total, dot = new, e_sum, e_dot
        most = jnp.max(top, axis=0, keepdims=True)
        weight = jnp.exp2((top - most) * TO_LOG2)
        top_ref[0, j : j + 1, :] = most * TO_LOG2
        sum_ref[0, j : j + 1, :] = jnp.sum(total * weight, axis=0, keepdims=True)
        dot_ref[0, j : j + 1, :] = jnp.sum(dot * weight, axis=0, keepdims=True)


def prefix_kernel(
    core_ref, q_ref, g_ref, own_ref, other_ref, slot_ref, top_ref, sum_ref, dot_ref,
    lse_ref, delta_ref, mine_ref, theirs_ref,
):
    even = core_ref[0] == 0
    parts, _, each, _ = own_ref.shape

    def gathered(which):
        rows = []
        for part in range(parts):
            own, other = own_ref[part, which].astype(F32), other_ref[part, which].astype(F32)
            rows += [jnp.where(even, own, other), jnp.where(even, other, own)]
        return jnp.concatenate(rows, axis=0).astype(BF16)

    heads = q_ref.shape[1] // HD
    slot = jnp.concatenate([slot_ref[...]] * heads, axis=1)
    q, g = stacked(q_ref), stacked(g_ref)
    s_all = lax.dot_general(gathered(0), q, NT, preferred_element_type=F32)
    dp_all = lax.dot_general(gathered(1), g, NT, preferred_element_type=F32)
    slots = s_all.shape[0] // PLEN
    s, dp = s_all[:PLEN], dp_all[:PLEN]
    for k in range(1, slots):
        rows = slice(k * PLEN, (k + 1) * PLEN)
        s = jnp.where(slot == k, s_all[rows], s)
        dp = jnp.where(slot == k, dp_all[rows], dp)
    top = joined(top_ref)
    new = jnp.maximum(top, jnp.max(s, axis=0, keepdims=True) * TO_LOG2)
    e = jnp.exp2(s * TO_LOG2 - new)
    old = jnp.exp2(top - new)
    total = old * joined(sum_ref) + jnp.sum(e, axis=0, keepdims=True)
    dot = old * joined(dot_ref) + jnp.sum(e * dp, axis=0, keepdims=True)
    inverse = 1.0 / total
    delta = dot * inverse
    p = e * inverse
    ds = p * (dp - delta)
    split(lse_ref, new + jnp.log2(total))
    split(delta_ref, delta)
    zero = jnp.zeros_like(p)

    def spread(x):
        return jnp.concatenate(
            [jnp.where(slot == k, x, zero).astype(BF16) for k in range(slots)], axis=0
        )

    dk = lax.dot_general(spread(ds), q, NN, preferred_element_type=F32) * SCALE
    dv = lax.dot_general(spread(p), g, NN, preferred_element_type=F32)
    for which, grad in enumerate((dk, dv)):
        for part in range(parts):
            at = 2 * part * each
            low, high = grad[at : at + each], grad[at + each : at + 2 * each]
            mine_ref[part, which] = jnp.where(even, low, high)
            theirs_ref[part, which] = jnp.where(even, high, low)


def token_grads_kernel(q_ref, g_ref, *refs):
    kv_refs, (bias_ref, lse_ref, delta_ref, near_ref, far_ref) = refs[:-5], refs[-5:]
    blocks = len(kv_refs) // 2
    keys = jnp.concatenate([r[0] for r in kv_refs[:blocks]], axis=0)
    values = jnp.concatenate([r[0] for r in kv_refs[blocks:]], axis=0)
    heads = q_ref.shape[1] // HD
    q, g = stacked(q_ref), stacked(g_ref)
    bias = jnp.concatenate([bias_ref[...]] * heads, axis=1)
    s = lax.dot_general(keys, q, NT, preferred_element_type=F32) + bias
    dp = lax.dot_general(values, g, NT, preferred_element_type=F32)
    p = jnp.exp2(s * TO_LOG2 - joined(lse_ref))
    ds = (p * (dp - joined(delta_ref))).astype(BF16)
    dk = lax.dot_general(ds, q, NN, preferred_element_type=F32) * SCALE
    dv = lax.dot_general(p.astype(BF16), g, NN, preferred_element_type=F32)
    near = near_ref.shape[1]
    for which, grad in enumerate((dk, dv)):
        near_ref[which] = grad[:near]
        far_ref[which] = grad[near:].astype(BF16)


def plane(rows, which):
    return pl.BlockSpec((1, rows, HD), lambda h: (which, 0, h))


def planes(shape):
    lead = (0,) * (len(shape) - 1)
    return pl.BlockSpec((*shape[:-1], HD), lambda h: (*lead, h))


def whole(shape):
    return pl.BlockSpec(shape, lambda h: (0,) * len(shape))


def common(q):
    toks, width = q.shape
    run = width // KVH
    rows = pl.BlockSpec((toks, run), lambda h: (0, h))
    stat = pl.BlockSpec((1, run // HD, toks), lambda h: (h, 0, 0))
    return rows, stat, jax.ShapeDtypeStruct((KVH, run // HD, toks), F32)


def params(flops, exps):
    return dict(
        grid=(KVH,),
        compiler_params=pltpu.CompilerParams(vmem_limit_bytes=56 << 20),
        cost_estimate=pl.CostEstimate(flops=flops, bytes_accessed=5 << 20, transcendentals=exps),
    )


def token_stats(q, g, blocks, bias):
    rows, stat, shape = common(q)
    toks = q.shape[0]
    work = q.size // HD * bias.shape[0]
    return pl.pallas_call(
        token_stats_kernel,
        in_specs=[rows, rows]
        + [plane(toks, 0)] * len(blocks)
        + [plane(toks, 1)] * len(blocks)
        + [whole(bias.shape)],
        out_specs=[stat] * 3,
        out_shape=[shape] * 3,
        **params(4 * HD * work, work),
    )(q, g, *blocks, *blocks, bias)


def prefix_grads(core, q, g, own, other, slot, stats):
    rows, stat, shape = common(q)
    work = q.size // HD * 2 * own.shape[0] * own.shape[2]
    half = jax.ShapeDtypeStruct(own.shape, F32)
    return pl.pallas_call(
        prefix_kernel,
        in_specs=[pl.BlockSpec(memory_space=pltpu.SMEM), rows, rows]
        + [planes(own.shape)] * 2
        + [whole(slot.shape)]
        + [stat] * 3,
        out_specs=[stat, stat, planes(own.shape), planes(own.shape)],
        out_shape=[shape, shape, half, half],
        **params(8 * HD * work, work // 4),
    )(core, q, g, own, other, slot, *stats)


def token_grads(q, g, blocks, bias, lse, delta):
    rows, stat, _ = common(q)
    toks = q.shape[0]
    work = q.size // HD * bias.shape[0]
    near, far = (2, 3 * toks, KVH * HD), (2, 2 * toks, KVH * HD)
    return pl.pallas_call(
        token_grads_kernel,
        in_specs=[rows, rows]
        + [plane(toks, 0)] * len(blocks)
        + [plane(toks, 1)] * len(blocks)
        + [whole(bias.shape), stat, stat],
        out_specs=[planes(near), planes(far)],
        out_shape=[jax.ShapeDtypeStruct(near, F32), jax.ShapeDtypeStruct(far, BF16)],
        **params(8 * HD * work, work),
    )(q, g, *blocks, *blocks, bias, lse, delta)


def layout(lengths, tenants, slots, index, shards, toks):
    ends = jnp.cumsum(lengths)
    slot_of = jnp.sum(
        jnp.where(tenants[:, None] == jnp.arange(slots.shape[0])[None, :], slots[None, :], 0), axis=1
    )
    here = index * toks + jnp.arange(toks, dtype=jnp.int32)
    doc = jnp.sum((here[None, :] >= ends[:, None]).astype(jnp.int32), axis=0)
    pick = doc[None, :] == jnp.arange(lengths.shape[0])[:, None]
    first = jnp.sum(jnp.where(pick, (ends - lengths)[:, None], 0), axis=0)
    slot = jnp.sum(jnp.where(pick, slot_of[:, None], 0), axis=0)
    key = jnp.concatenate([s * toks + jnp.arange(toks, dtype=jnp.int32) for s in shards])
    ok = (key[:, None] >= first[None, :]) & (key[:, None] <= here[None, :])
    return jnp.where(ok, 0.0, -1e30).astype(F32), slot[None, :].astype(jnp.int32)


def per_device(
    queries, keys, values, grad_out, prefix_keys, prefix_values, doc_lengths, doc_tenants, tenant_slots
):
    toks = queries.shape[0]
    parts = lax.axis_size("z")
    count = parts * lax.axis_size("core")
    index, core = lax.axis_index(SEQ), lax.axis_index("core")
    even = core == 0

    def shift(x, steps):
        pairs = [(i, i + 2 * steps) for i in range(count) if 0 <= i + 2 * steps < count]
        return lax.ppermute(x, SEQ, pairs)

    def swap(x):
        return lax.ppermute(x, SEQ, [(i, i ^ 1) for i in range(count)])

    def exchange(x, axis):
        return lax.all_to_all(x, axis, split_axis=0, concat_axis=0, tiled=True)

    def to_all(x, axis):
        return exchange(jnp.broadcast_to(x[None], (lax.axis_size(axis), *x.shape)), axis)

    own = jnp.stack([keys, values])
    back1, back2 = shift(own, 1), shift(own, 2)
    pref_own = to_all(jnp.stack([prefix_keys, prefix_values]), "z")
    cross1 = swap(back1)
    cross02 = swap(jnp.where(even, own, back2))
    shards = [
        index - 4,
        index - 2,
        index,
        jnp.where(even, index - 3, index - 1),
        jnp.where(even, index - 1, index - 3),
    ]
    blocks = (back2, back1, own, cross02, cross1)
    bias, slot = layout(doc_lengths[0], doc_tenants[0], tenant_slots, index, shards, toks)
    stats = token_stats(queries, grad_out, blocks, bias)
    pref_other = swap(pref_own)
    lse, delta, mine, theirs = prefix_grads(
        core.astype(jnp.int32)[None], queries, grad_out, pref_own, pref_other, slot, stats
    )

    mine = (mine + swap(theirs)).astype(BF16)
    rows = jnp.sum(exchange(mine, "z").astype(F32), axis=0)
    rows = jnp.sum(to_all(rows, "x"), axis=0)
    rows = jnp.sum(to_all(rows.astype(BF16), "y").astype(F32), axis=0)

    near, far = token_grads(queries, grad_out, blocks, bias, lse, delta)
    far = swap(far).astype(F32)
    zero = jnp.zeros((2, toks, far.shape[2]), F32)
    two = near[:, :toks] + jnp.where(even, zero, far[:, :toks])
    one = near[:, toks : 2 * toks] + far[:, toks:]
    home = near[:, 2 * toks :] + jnp.where(even, far[:, :toks], zero)
    one = shift(one.astype(BF16), -1)
    two = shift(two.astype(BF16), -2)
    total = (home + one.astype(F32) + two.astype(F32)).astype(BF16)
    return total[0], total[1], rows[0], rows[1]


def solution(mesh):
    mesh = Mesh(mesh.devices.reshape(8, 4, 8, 2), ("y", "x", "z", "core"))
    rows, dp, seq = P(("y", "x", "z", "core"), None), P(("y", "x"), None), P(SEQ, None)
    return jax.shard_map(
        per_device,
        mesh=mesh,
        in_specs=(rows, rows, rows, rows, seq, seq, dp, dp, P()),
        out_specs=(rows, rows, seq, seq),
        check_vma=False,
    )
```

time: 155 us -> 125 us (0.81)
  the two profiles are of different devices: /device:TPU:1 before, /device:TPU:64 now
where the time goes in v2:
time: 125 us; the launch traced here: 124 us
  starting transfers between devices  52.2 us (42%)
  waiting for transfers between devices  28.6 us (23%)
  Pallas kernels  27.6 us (22%)
  other arithmetic  7.95 us (6%)
  local copies, waits for them, and re-layouts  6.65 us (5%)
    all_to_all x4, starting transfers between devices, exchange(): return lax.all_to_all(x, axis, split_axis=0, concat_axis=0, tiled=True)  27.2 us
    all_to_all x4, waiting for transfers between devices, exchange(): return lax.all_to_all(x, axis, split_axis=0, concat_axis=0, tiled=True)  17.7 us
    ppermute x4, starting transfers between devices, shift(): return lax.ppermute(x, SEQ, pairs)  14.8 us
    pallas_call x1, Pallas kernels, token_grads(): pl.pallas_call(token_grads_kernel, in_specs=[rows, rows] + [plane(toks, 0...  11.3 us
    ppermute x5, starting transfers between devices, swap(): return lax.ppermute(x, SEQ, [(i, i ^ 1) for i in range(count)])  10.2 us
    pallas_call x1, Pallas kernels, token_stats(): pl.pallas_call(token_stats_kernel, in_specs=[rows, rows] + [plane(toks, 0...  8.48 us
    pallas_call x1, Pallas kernels, prefix_grads(): pl.pallas_call(prefix_kernel, in_specs=[pl.BlockSpec(memory_space=pltpu.S...  7.81 us
    ppermute x4, waiting for transfers between devices, shift(): return lax.ppermute(x, SEQ, pairs)  6.72 us
  transfers between devices with their start and end apart: 13, of which 7 were waited for; matrix products, arithmetic and copies ran while one was open for 6% of the time, Pallas kernels for 16%

profile of v2, /device:TPU:64, one launch (start us, length us, event | category | flops | bytes accessed | tf_op | source)
XLA Modules:
  0.0 123.8 jit_solution(13523058815330006335)
XLA Ops:
  0.6 0.0 copy-start.2
  0.6 0.0 copy-start.1
  0.7 0.0 copy-start.10
  0.7 0.0 copy-start.12
  0.7 0.0 copy-start.11
  0.7 1.1 pad_maximum_fusion.refs_2_.refs_7_
  1.8 0.0 copy-start.4
  1.8 6.1 %collective-permute-start = (bf16[2,128,512]{2,1,0:T(8,128)(2,1)S(1)}, bf16[2,128,512]{2,1,0:T(8,128)(2,1)S(1)}, u32[]{:S(2)}, u32[]{:S(2)}) collective-permute-start(bf16[2,128,512]{2,1,0:T(8,128)(2,1)S(1)} %pad_maximum_fusion.refs_2_.refs_7_), channel_id=1, source_target_pairs={{0,4},{1,5},{2,6},{3,7},{4,8},{5,9},{6,10},{7,11},{8,12},{9,13},{1... | collective-permute-start | bytes 786440 | tf_op jit(solution)/shard_map/ppermute | solution.py:247
  7.9 5.5 %collective-permute-start.1 = (bf16[2,128,512]{2,1,0:T(8,128)(2,1)S(1)}, bf16[2,128,512]{2,1,0:T(8,128)(2,1)S(1)}, u32[]{:S(2)}, u32[]{:S(2)}) collective-permute-start(bf16[2,128,512]{2,1,0:T(8,128)(2,1)S(1)} %pad_maximum_fusion.refs_2_.refs_7_), channel_id=1, source_target_pairs={{0,2},{1,3},{2,4},{3,5},{4,6},{5,7},{6,8},{7,9},{8,10},{9,11},{10,... | collective-permute-start | bytes 786440 | tf_op jit(solution)/shard_map/ppermute | solution.py:247
  13.4 0.8 pad_maximum_fusion.1
  14.2 0.8 broadcast_in_dim.82
  14.9 6.0 %all-to-all-start = ((bf16[8,2,24,512]{3,2,1,0:T(8,128)(2,1)}), bf16[8,2,24,512]{3,2,1,0:T(8,128)(2,1)S(1)}, u32[]{:S(2)}, u32[]{:S(2)}) async-start(bf16[8,2,24,512]{3,2,1,0:T(8,128)(2,1)} %broadcast_in_dim.82), calls=%async_computation | async-start | bytes 786432 | tf_op jit(solution)/shard_map/all_to_all | solution.py:253
  21.0 0.0 copy-done.10
  21.0 0.2 reduce-window.7
  21.2 0.1 convert_reduce_fusion.2
  21.3 0.0 copy-done.12
  21.3 0.0 copy-done.11
  21.3 0.2 select_reduce_fusion.1
  21.5 0.0 collective-permute-done.refs_0_.refs_5_
  21.5 0.0 copy-done.2
  21.5 0.0 copy-done.1
  21.5 0.0 copy-start.5
  21.6 1.9 %collective-permute-start.2 = (bf16[2,128,512]{2,1,0:T(8,128)(2,1)S(1)}, bf16[2,128,512]{2,1,0:T(8,128)(2,1)S(1)}, u32[]{:S(2)}, u32[]{:S(2)}) collective-permute-start(bf16[2,128,512]{2,1,0:T(8,128)(2,1)S(1)} %broadcast_select_fusion), channel_id=1, source_target_pairs={{0,1},{1,0},{2,3},{3,2},{4,5},{5,4},{6,7},{7,6},{8,9},{9,8},{10,11... | collective-permute-start | bytes 786440 | tf_op jit(solution)/shard_map/ppermute | solution.py:250
  23.5 5.1 %collective-permute-done.1.refs_1_.refs_6_ = bf16[2,128,512]{2,1,0:T(8,128)(2,1)S(1)} collective-permute-done((bf16[2,128,512]{2,1,0:T(8,128)(2,1)S(1)}, bf16[2,128,512]{2,1,0:T(8,128)(2,1)S(1)}, u32[]{:S(2)}, u32[]{:S(2)}) %collective-permute-start.1) | collective-permute-done | bytes 262176 | tf_op jit(solution)/shard_map/ppermute | solution.py:247
  28.6 1.9 %collective-permute-start.3 = (bf16[2,128,512]{2,1,0:T(8,128)(2,1)S(1)}, bf16[2,128,512]{2,1,0:T(8,128)(2,1)S(1)}, u32[]{:S(2)}, u32[]{:S(2)}) collective-permute-start(bf16[2,128,512]{2,1,0:T(8,128)(2,1)S(1)} %collective-permute-done.1.refs_1_.refs_6_), channel_id=1, source_target_pairs={{0,1},{1,0},{2,3},{3,2},{4,5},{5,4},{6,7},{7,6},{8,9},{9,8},{10,11... | collective-permute-start | bytes 786440 | tf_op jit(solution)/shard_map/ppermute | solution.py:250
  30.5 0.6 select_reduce_fusion
  31.1 2.6 %all-to-all-done.own_ref = bf16[8,2,24,512]{3,2,1,0:T(8,128)(2,1)S(1)} async-done(((bf16[8,2,24,512]{3,2,1,0:T(8,128)(2,1)}), bf16[8,2,24,512]{3,2,1,0:T(8,128)(2,1)S(1)}, u32[]{:S(2)}, u32[]{:S(2)}) %all-to-all-start) | async-done | bytes 393248 | tf_op jit(solution)/shard_map/all_to_all | solution.py:253
  33.6 1.9 %collective-permute-start.4 = (bf16[8,2,24,512]{3,2,1,0:T(8,128)(2,1)S(1)}, bf16[8,2,24,512]{3,2,1,0:T(8,128)(2,1)S(1)}, u32[]{:S(2)}, u32[]{:S(2)}) collective-permute-start(bf16[8,2,24,512]{3,2,1,0:T(8,128)(2,1)S(1)} %all-to-all-done.own_ref), channel_id=1, source_target_pairs={{0,1},{1,0},{2,3},{3,2},{4,5},{5,4},{6,7},{7,6},{8,9},{9,8},{10,11... | collective-permute-start | bytes 1179656 | tf_op jit(solution)/shard_map/ppermute | solution.py:250
  35.6 0.9 and_select_fusion.refs_10_
  36.4 0.0 collective-permute-done.2.refs_3_.refs_8_
  36.4 0.0 collective-permute-done.3.refs_4_.refs_9_
  36.5 0.7 copy-done.8
  37.2 0.7 copy-done.9
  37.8 8.5 %shard_map.120 = (f32[4,12,128]{2,1,0:T(8,128)}, f32[4,12,128]{2,1,0:T(8,128)}, f32[4,12,128]{2,1,0:T(8,128)}) custom-call(bf16[128,6144]{1,0:T(8,128)(2,1)} %q_ref.5, bf16[128,6144]{1,0:T(8,128)(2,1)} %g_ref.5, bf16[2,128,512]{2,1,0:T(8,128)(2,1)} %copy-done.5, bf16[2,128,512]{2,1,0:T(8,128)(2,1)} %copy-done.7, bf16[2,128,512]{2,1,0:T(8,128)(2,1)} %copy-done.4, ...), custom_call_target="tpu_custom_call" | custom-call | flops 2013265920 | bytes 5242880 | tf_op jit(solution)/shard_map/pallas_call | solution.py:176
  46.3 0.0 collective-permute-done.4.other_ref
  46.4 0.0 copy-start.6
  46.4 0.7 copy-done.6
  47.1 7.8 %shard_map.121 = (f32[4,12,128]{2,1,0:T(8,128)}, f32[4,12,128]{2,1,0:T(8,128)}, f32[8,2,24,512]{3,2,1,0:T(8,128)}, f32[8,2,24,512]{3,2,1,0:T(8,128)}) custom-call(s32[1]{0:T(128)} %bitcast.5.core_ref, bf16[128,6144]{1,0:T(8,128)(2,1)} %q_ref.5, bf16[128,6144]{1,0:T(8,128)(2,1)} %g_ref.5, bf16[8,2,24,512]{3,2,1,0:T(8,128)(2,1)} %copy-done.3, ...), custom_call_target="tpu_custom_call" | custom-call | flops 2415919104 | bytes 5242880 | tf_op jit(solution)/shard_map/pallas_call | solution.py:192
  54.9 2.4 %collective-permute-start.8 = (f32[8,2,24,512]{3,2,1,0:T(8,128)}, f32[8,2,24,512]{3,2,1,0:T(8,128)S(1)}, u32[]{:S(2)}, u32[]{:S(2)}) collective-permute-start(f32[8,2,24,512]{3,2,1,0:T(8,128)} %get-tuple-element.21), channel_id=1, source_target_pairs={{0,1},{1,0},{2,3},{3,2},{4,5},{5,4},{6,7},{7,6},{8,9},{9,8},{10,11... | collective-permute-start | bytes 2359304 | tf_op jit(solution)/shard_map/ppermute | solution.py:250
  57.3 2.1 %collective-permute-done.8 = f32[8,2,24,512]{3,2,1,0:T(8,128)S(1)} collective-permute-done((f32[8,2,24,512]{3,2,1,0:T(8,128)}, f32[8,2,24,512]{3,2,1,0:T(8,128)S(1)}, u32[]{:S(2)}, u32[]{:S(2)}) %collective-permute-start.8) | collective-permute-done | bytes 786464 | tf_op jit(solution)/shard_map/ppermute | solution.py:250
  59.4 2.0 %add_convert_fusion = bf16[8,2,24,512]{3,2,1,0:T(8,128)(2,1)} fusion(f32[8,2,24,512]{3,2,1,0:T(8,128)} %get-tuple-element.20, f32[8,2,24,512]{3,2,1,0:T(8,128)S(1)} %collective-permute-done.8), kind=kLoop, calls=%fused_computation.2 | loop fusion | flops 393216 | bytes 1966080 | tf_op jit(solution)/shard_map/convert_element_type | solution.py:278
  61.4 9.8 %all-to-all-start.1 = ((bf16[8,2,24,512]{3,2,1,0:T(8,128)(2,1)}), bf16[8,2,24,512]{3,2,1,0:T(8,128)(2,1)S(1)}, u32[]{:S(2)}, u32[]{:S(2)}) async-start(bf16[8,2,24,512]{3,2,1,0:T(8,128)(2,1)} %add_convert_fusion), calls=%async_computation.1 | async-start | bytes 786432 | tf_op jit(solution)/shard_map/all_to_all | solution.py:253
  71.2 11.3 %shard_map.122 = (f32[2,384,512]{2,1,0:T(8,128)}, bf16[2,256,512]{2,1,0:T(8,128)(2,1)}) custom-call(bf16[128,6144]{1,0:T(8,128)(2,1)} %q_ref.5, bf16[128,6144]{1,0:T(8,128)(2,1)} %g_ref.5, bf16[2,128,512]{2,1,0:T(8,128)(2,1)} %copy-done.5, bf16[2,128,512]{2,1,0:T(8,128)(2,1)} %copy-done.7, bf16[2,128,512]{2,1,0:T(8,128)(2,1)} %copy-done.4, ...), custom_call_target="tpu_custom_call" | custom-call | flops 4026531840 | bytes 5242880 | tf_op jit(solution)/shard_map/pallas_call | solution.py:209
  82.5 2.1 %collective-permute-start.5 = (bf16[2,256,512]{2,1,0:T(8,128)(2,1)}, bf16[2,256,512]{2,1,0:T(8,128)(2,1)S(1)}, u32[]{:S(2)}, u32[]{:S(2)}) collective-permute-start(bf16[2,256,512]{2,1,0:T(8,128)(2,1)} %get-tuple-element.19), channel_id=1, source_target_pairs={{0,1},{1,0},{2,3},{3,2},{4,5},{5,4},{6,7},{7,6},{8,9},{9,8},{10,11... | collective-permute-start | bytes 1572872 | tf_op jit(solution)/shard_map/ppermute | solution.py:250
  84.6 2.1 %collective-permute-done.5 = bf16[2,256,512]{2,1,0:T(8,128)(2,1)S(1)} collective-permute-done((bf16[2,256,512]{2,1,0:T(8,128)(2,1)}, bf16[2,256,512]{2,1,0:T(8,128)(2,1)S(1)}, u32[]{:S(2)}, u32[]{:S(2)}) %collective-permute-start.5) | collective-permute-done | bytes 524320 | tf_op jit(solution)/shard_map/ppermute | solution.py:250
  86.7 0.1 convert_element_type.38
  86.8 0.0 all-to-all-done.1
  86.8 0.1 convert_reduce_fusion.1
  86.9 0.8 broadcast_in_dim.88
  87.6 4.3 %all-to-all-start.2 = ((f32[4,2,24,512]{3,2,1,0:T(8,128)}), f32[4,2,24,512]{3,2,1,0:T(8,128)S(1)}, u32[]{:S(2)}, u32[]{:S(2)}) async-start(f32[4,2,24,512]{3,2,1,0:T(8,128)} %broadcast_in_dim.88), calls=%async_computation.2 | async-start | bytes 786432 | tf_op jit(solution)/shard_map/all_to_all | solution.py:253
  91.9 1.0 fusion
  93.0 1.9 %collective-permute-start.6 = (bf16[2,128,512]{2,1,0:T(8,128)(2,1)}, bf16[2,128,512]{2,1,0:T(8,128)(2,1)S(1)}, u32[]{:S(2)}, u32[]{:S(2)}) collective-permute-start(bf16[2,128,512]{2,1,0:T(8,128)(2,1)} %get-tuple-element.24), channel_id=1, source_target_pairs={{2,0},{3,1},{4,2},{5,3},{6,4},{7,5},{8,6},{9,7},{10,8},{11,9},{12,... | collective-permute-start | bytes 786440 | tf_op jit(solution)/shard_map/ppermute | solution.py:247
  94.9 1.3 %collective-permute-start.7 = (bf16[2,128,512]{2,1,0:T(8,128)(2,1)}, bf16[2,128,512]{2,1,0:T(8,128)(2,1)S(1)}, u32[]{:S(2)}, u32[]{:S(2)}) collective-permute-start(bf16[2,128,512]{2,1,0:T(8,128)(2,1)} %get-tuple-element.25), channel_id=1, source_target_pairs={{4,0},{5,1},{6,2},{7,3},{8,4},{9,5},{10,6},{11,7},{12,8},{13,9},{1... | collective-permute-start | bytes 786440 | tf_op jit(solution)/shard_map/ppermute | solution.py:247
  96.2 4.1 %all-to-all-done.2 = f32[4,2,24,512]{3,2,1,0:T(8,128)S(1)} async-done(((f32[4,2,24,512]{3,2,1,0:T(8,128)}), f32[4,2,24,512]{3,2,1,0:T(8,128)S(1)}, u32[]{:S(2)}, u32[]{:S(2)}) %all-to-all-start.2) | async-done | bytes 393248 | tf_op jit(solution)/shard_map/all_to_all | solution.py:253
  100.3 0.6 reduce_sum.68
  101.0 1.6 %broadcast_in_dim.89 = bf16[8,2,24,512]{3,2,1,0:T(8,128)(2,1)} broadcast(bf16[2,24,512]{2,1,0:T(8,128)(2,1)} %reduce_sum.68), dimensions={1,2,3} | broadcast | bytes 442368 | tf_op jit(solution)/shard_map/broadcast_in_dim | solution.py:256
  102.5 7.1 %all-to-all-start.3 = ((bf16[8,2,24,512]{3,2,1,0:T(8,128)(2,1)}), bf16[8,2,24,512]{3,2,1,0:T(8,128)(2,1)S(1)}, u32[]{:S(2)}, u32[]{:S(2)}) async-start(bf16[8,2,24,512]{3,2,1,0:T(8,128)(2,1)} %broadcast_in_dim.89), calls=%async_computation.3 | async-start | bytes 786432 | tf_op jit(solution)/shard_map/all_to_all | solution.py:253
  109.6 0.0 collective-permute-done.6
  109.6 1.7 %collective-permute-done.7 = bf16[2,128,512]{2,1,0:T(8,128)(2,1)S(1)} collective-permute-done((bf16[2,128,512]{2,1,0:T(8,128)(2,1)}, bf16[2,128,512]{2,1,0:T(8,128)(2,1)S(1)}, u32[]{:S(2)}, u32[]{:S(2)}) %collective-permute-start.7) | collective-permute-done | bytes 262176 | tf_op jit(solution)/shard_map/ppermute | solution.py:247
  111.3 0.2 add_convert_fusion.1
  111.4 0.7 slice_bitcast_fusion
  112.1 11.0 %all-to-all-done.3 = bf16[8,2,24,512]{3,2,1,0:T(8,128)(2,1)S(1)} async-done(((bf16[8,2,24,512]{3,2,1,0:T(8,128)(2,1)}), bf16[8,2,24,512]{3,2,1,0:T(8,128)(2,1)S(1)}, u32[]{:S(2)}, u32[]{:S(2)}) %all-to-all-start.3) | async-done | bytes 393248 | tf_op jit(solution)/shard_map/all_to_all | solution.py:253
  123.2 0.1 convert_reduce_fusion
  123.2 0.6 slice_bitcast_fusion.2
  (18 shorter events, 0.1 us)
Async XLA Ops:
  0.6 20.9 %copy-start.2 = (bf16[128,512]{1,0:T(8,128)(2,1)S(1)}, bf16[128,512]{1,0:T(8,128)(2,1)}, u32[]{:S(2)}) copy-start(bf16[128,512]{1,0:T(8,128)(2,1)} %param.10) | copy-start | bytes 393220
  0.6 20.9 %copy-start.1 = (bf16[128,512]{1,0:T(8,128)(2,1)S(1)}, bf16[128,512]{1,0:T(8,128)(2,1)}, u32[]{:S(2)}) copy-start(bf16[128,512]{1,0:T(8,128)(2,1)} %param.11) | copy-start | bytes 393220
  0.7 20.3 %copy-start.10 = (s32[1,8]{1,0:T(1,128)S(1)}, s32[1,8]{1,0:T(1,128)}, u32[]{:S(2)}) copy-start(s32[1,8]{1,0:T(1,128)} %param.15) | copy-start | bytes 100
  0.7 20.6 %copy-start.12 = (s32[1,8]{1,0:T(1,128)S(1)}, s32[1,8]{1,0:T(1,128)}, u32[]{:S(2)}) copy-start(s32[1,8]{1,0:T(1,128)} %param.16) | copy-start | bytes 100
  0.7 20.6 %copy-start.11 = (s32[6]{0:T(128)S(1)}, s32[6]{0:T(128)}, u32[]{:S(2)}) copy-start(s32[6]{0:T(128)} %param.17) | copy-start | bytes 76
  1.8 34.7 %copy-start.4 = (bf16[2,128,512]{2,1,0:T(8,128)(2,1)}, bf16[2,128,512]{2,1,0:T(8,128)(2,1)S(1)}, u32[]{:S(2)}) copy-start(bf16[2,128,512]{2,1,0:T(8,128)(2,1)S(1)} %pad_maximum_fusion.refs_2_.refs_7_) | copy-start | bytes 786436
  1.8 19.7 %collective-permute-start = (bf16[2,128,512]{2,1,0:T(8,128)(2,1)S(1)}, bf16[2,128,512]{2,1,0:T(8,128)(2,1)S(1)}, u32[]{:S(2)}, u32[]{:S(2)}) collective-permute-start(bf16[2,128,512]{2,1,0:T(8,128)(2,1)S(1)} %pad_maximum_fusion.refs_2_.refs_7_), channel_id=1, source_target_pairs={{0,4},{1,5},{2,6},{3,7},{4,8},{5,9},{6,10},{7,11},{8,12},{9,13},{1... | collective-permute-start | bytes 786440 | tf_op jit(solution)/shard_map/ppermute | solution.py:247
  7.9 20.6 %collective-permute-start.1 = (bf16[2,128,512]{2,1,0:T(8,128)(2,1)S(1)}, bf16[2,128,512]{2,1,0:T(8,128)(2,1)S(1)}, u32[]{:S(2)}, u32[]{:S(2)}) collective-permute-start(bf16[2,128,512]{2,1,0:T(8,128)(2,1)S(1)} %pad_maximum_fusion.refs_2_.refs_7_), channel_id=1, source_target_pairs={{0,2},{1,3},{2,4},{3,5},{4,6},{5,7},{6,8},{7,9},{8,10},{9,11},{10,... | collective-permute-start | bytes 786440 | tf_op jit(solution)/shard_map/ppermute | solution.py:247
  14.9 18.7 %all-to-all-start = ((bf16[8,2,24,512]{3,2,1,0:T(8,128)(2,1)}), bf16[8,2,24,512]{3,2,1,0:T(8,128)(2,1)S(1)}, u32[]{:S(2)}, u32[]{:S(2)}) async-start(bf16[8,2,24,512]{3,2,1,0:T(8,128)(2,1)} %broadcast_in_dim.82), calls=%async_computation | async-start | bytes 786432 | tf_op jit(solution)/shard_map/all_to_all | solution.py:253
  21.5 14.9 %copy-start.5 = (bf16[2,128,512]{2,1,0:T(8,128)(2,1)}, bf16[2,128,512]{2,1,0:T(8,128)(2,1)S(1)}, u32[]{:S(2)}) copy-start(bf16[2,128,512]{2,1,0:T(8,128)(2,1)S(1)} %collective-permute-done.refs_0_.refs_5_) | copy-start | bytes 786436
  21.6 14.9 %collective-permute-start.2 = (bf16[2,128,512]{2,1,0:T(8,128)(2,1)S(1)}, bf16[2,128,512]{2,1,0:T(8,128)(2,1)S(1)}, u32[]{:S(2)}, u32[]{:S(2)}) collective-permute-start(bf16[2,128,512]{2,1,0:T(8,128)(2,1)S(1)} %broadcast_select_fusion), channel_id=1, source_target_pairs={{0,1},{1,0},{2,3},{3,2},{4,5},{5,4},{6,7},{7,6},{8,9},{9,8},{10,11... | collective-permute-start | bytes 786440 | tf_op jit(solution)/shard_map/ppermute | solution.py:250
  28.6 7.9 %copy-start.7 = (bf16[2,128,512]{2,1,0:T(8,128)(2,1)}, bf16[2,128,512]{2,1,0:T(8,128)(2,1)S(1)}, u32[]{:S(2)}) copy-start(bf16[2,128,512]{2,1,0:T(8,128)(2,1)S(1)} %collective-permute-done.1.refs_1_.refs_6_) | copy-start | bytes 786436
  28.6 7.9 %collective-permute-start.3 = (bf16[2,128,512]{2,1,0:T(8,128)(2,1)S(1)}, bf16[2,128,512]{2,1,0:T(8,128)(2,1)S(1)}, u32[]{:S(2)}, u32[]{:S(2)}) collective-permute-start(bf16[2,128,512]{2,1,0:T(8,128)(2,1)S(1)} %collective-permute-done.1.refs_1_.refs_6_), channel_id=1, source_target_pairs={{0,1},{1,0},{2,3},{3,2},{4,5},{5,4},{6,7},{7,6},{8,9},{9,8},{10,11... | collective-permute-start | bytes 786440 | tf_op jit(solution)/shard_map/ppermute | solution.py:250
  33.6 12.7 %copy-start.3 = (bf16[8,2,24,512]{3,2,1,0:T(8,128)(2,1)}, bf16[8,2,24,512]{3,2,1,0:T(8,128)(2,1)S(1)}, u32[]{:S(2)}) copy-start(bf16[8,2,24,512]{3,2,1,0:T(8,128)(2,1)S(1)} %all-to-all-done.own_ref) | copy-start | bytes 1179652
  33.6 12.7 %collective-permute-start.4 = (bf16[8,2,24,512]{3,2,1,0:T(8,128)(2,1)S(1)}, bf16[8,2,24,512]{3,2,1,0:T(8,128)(2,1)S(1)}, u32[]{:S(2)}, u32[]{:S(2)}) collective-permute-start(bf16[8,2,24,512]{3,2,1,0:T(8,128)(2,1)S(1)} %all-to-all-done.own_ref), channel_id=1, source_target_pairs={{0,1},{1,0},{2,3},{3,2},{4,5},{5,4},{6,7},{7,6},{8,9},{9,8},{10,11... | collective-permute-start | bytes 1179656 | tf_op jit(solution)/shard_map/ppermute | solution.py:250
  36.4 0.7 copy-start.8
  37.2 0.7 copy-start.9
  46.4 0.8 copy-start.6
  54.9 4.5 %collective-permute-start.8 = (f32[8,2,24,512]{3,2,1,0:T(8,128)}, f32[8,2,24,512]{3,2,1,0:T(8,128)S(1)}, u32[]{:S(2)}, u32[]{:S(2)}) collective-permute-start(f32[8,2,24,512]{3,2,1,0:T(8,128)} %get-tuple-element.21), channel_id=1, source_target_pairs={{0,1},{1,0},{2,3},{3,2},{4,5},{5,4},{6,7},{7,6},{8,9},{9,8},{10,11... | collective-permute-start | bytes 2359304 | tf_op jit(solution)/shard_map/ppermute | solution.py:250
  61.4 25.4 %all-to-all-start.1 = ((bf16[8,2,24,512]{3,2,1,0:T(8,128)(2,1)}), bf16[8,2,24,512]{3,2,1,0:T(8,128)(2,1)S(1)}, u32[]{:S(2)}, u32[]{:S(2)}) async-start(bf16[8,2,24,512]{3,2,1,0:T(8,128)(2,1)} %add_convert_fusion), calls=%async_computation.1 | async-start | bytes 786432 | tf_op jit(solution)/shard_map/all_to_all | solution.py:253
  82.5 9.4 %copy-start = (f32[2,384,512]{2,1,0:T(8,128)S(1)}, f32[2,384,512]{2,1,0:T(8,128)}, u32[]{:S(2)}) copy-start(f32[2,384,512]{2,1,0:T(8,128)} %get-tuple-element.18) | copy-start | bytes 4718596
  82.5 4.1 %collective-permute-start.5 = (bf16[2,256,512]{2,1,0:T(8,128)(2,1)}, bf16[2,256,512]{2,1,0:T(8,128)(2,1)S(1)}, u32[]{:S(2)}, u32[]{:S(2)}) collective-permute-start(bf16[2,256,512]{2,1,0:T(8,128)(2,1)} %get-tuple-element.19), channel_id=1, source_target_pairs={{0,1},{1,0},{2,3},{3,2},{4,5},{5,4},{6,7},{7,6},{8,9},{9,8},{10,11... | collective-permute-start | bytes 1572872 | tf_op jit(solution)/shard_map/ppermute | solution.py:250
  87.6 12.7 %all-to-all-start.2 = ((f32[4,2,24,512]{3,2,1,0:T(8,128)}), f32[4,2,24,512]{3,2,1,0:T(8,128)S(1)}, u32[]{:S(2)}, u32[]{:S(2)}) async-start(f32[4,2,24,512]{3,2,1,0:T(8,128)} %broadcast_in_dim.88), calls=%async_computation.2 | async-start | bytes 786432 | tf_op jit(solution)/shard_map/all_to_all | solution.py:253
  93.0 16.6 %collective-permute-start.6 = (bf16[2,128,512]{2,1,0:T(8,128)(2,1)}, bf16[2,128,512]{2,1,0:T(8,128)(2,1)S(1)}, u32[]{:S(2)}, u32[]{:S(2)}) collective-permute-start(bf16[2,128,512]{2,1,0:T(8,128)(2,1)} %get-tuple-element.24), channel_id=1, source_target_pairs={{2,0},{3,1},{4,2},{5,3},{6,4},{7,5},{8,6},{9,7},{10,8},{11,9},{12,... | collective-permute-start | bytes 786440 | tf_op jit(solution)/shard_map/ppermute | solution.py:247
  94.9 16.4 %collective-permute-start.7 = (bf16[2,128,512]{2,1,0:T(8,128)(2,1)}, bf16[2,128,512]{2,1,0:T(8,128)(2,1)S(1)}, u32[]{:S(2)}, u32[]{:S(2)}) collective-permute-start(bf16[2,128,512]{2,1,0:T(8,128)(2,1)} %get-tuple-element.25), channel_id=1, source_target_pairs={{4,0},{5,1},{6,2},{7,3},{8,4},{9,5},{10,6},{11,7},{12,8},{13,9},{1... | collective-permute-start | bytes 786440 | tf_op jit(solution)/shard_map/ppermute | solution.py:247
  102.5 20.6 %all-to-all-start.3 = ((bf16[8,2,24,512]{3,2,1,0:T(8,128)(2,1)}), bf16[8,2,24,512]{3,2,1,0:T(8,128)(2,1)S(1)}, u32[]{:S(2)}, u32[]{:S(2)}) async-start(bf16[8,2,24,512]{3,2,1,0:T(8,128)(2,1)} %broadcast_in_dim.89), calls=%async_computation.3 | async-start | bytes 786432 | tf_op jit(solution)/shard_map/all_to_all | solution.py:253

commit v3 on v1

v3 whole, which is shorter than its diff:
```python
import functools
import math

import jax
import jax.numpy as jnp
from jax import lax
from jax.experimental import pallas as pl
from jax.experimental.pallas import tpu as pltpu
from jax.sharding import Mesh, PartitionSpec as P

HQ = 48
KVH = 4
HD = 128
PLEN = 64
NT = (((1,), (1,)), ((), ()))
NN = (((1,), (0,)), ((), ()))
SEQ = ("z", "core")
SCALE = 1.0 / math.sqrt(HD)
TO_LOG2 = SCALE * math.log2(math.e)
F32 = jnp.float32
BF16 = jnp.bfloat16


def stacked(ref, lead=()):
    count = ref.shape[-1] // HD
    return jnp.concatenate(
        [ref[(*lead, slice(None), slice(j * HD, (j + 1) * HD))] for j in range(count)], axis=0
    )


def joined(ref, chunk):
    return jnp.concatenate([ref[0, chunk, j : j + 1, :] for j in range(ref.shape[2])], axis=1)


def split(ref, chunk, row):
    for j in range(ref.shape[2]):
        ref[0, chunk, j : j + 1, :] = row[:, j * HD : (j + 1) * HD]


def windows(even, own, one, two, cross):
    last = jnp.where(even, own[0].astype(F32), two[0].astype(F32)).astype(BF16)
    far = jnp.where(even, cross[2, 0].astype(F32), cross[0, 0].astype(F32)).astype(BF16)
    return (
        jnp.concatenate([own[0], one[0], two[0], cross[1, 0], far], axis=0),
        jnp.concatenate([cross[0, 0], one[0], cross[1, 0], cross[2, 0], last], axis=0),
    )


def token_stats_kernel(core_ref, q_ref, g_ref, qo_ref, go_ref, *refs):
    bias_ref, top_ref, sum_ref, dot_ref = refs[8:]
    even = core_ref[0] == 0
    keys, values = windows(even, *refs[:4]), windows(even, *refs[4:8])
    toks = q_ref.shape[0]
    blocks = keys[0].shape[0] // toks
    for chunk in range(2):
        q, g = (stacked(qo_ref, (0,)), stacked(go_ref, (0,))) if chunk else (stacked(q_ref), stacked(g_ref))
        s_all = lax.dot_general(keys[chunk], q, NT, preferred_element_type=F32)
        dp_all = lax.dot_general(values[chunk], g, NT, preferred_element_type=F32)
        for j in range(q_ref.shape[1] // HD):
            cols = slice(j * toks, (j + 1) * toks)
            top = total = dot = None
            for b in range(blocks):
                rows = slice(b * toks, (b + 1) * toks)
                s = (s_all[rows, cols] + bias_ref[chunk, rows, :]).reshape(toks // 8, 8, toks)
                dp = dp_all[rows, cols].reshape(toks // 8, 8, toks)
                new = jnp.max(s, axis=0)
                new = new if top is None else jnp.maximum(top, new)
                e = jnp.exp2(s * TO_LOG2 - (new * TO_LOG2)[None])
                e_sum, e_dot = jnp.sum(e, axis=0), jnp.sum(e * dp, axis=0)
                if top is not None:
                    old = jnp.exp2(top * TO_LOG2 - new * TO_LOG2)
                    e_sum, e_dot = old * total + e_sum, old * dot + e_dot
                top, total, dot = new, e_sum, e_dot
            most = jnp.max(top, axis=0, keepdims=True)
            weight = jnp.exp2((top - most) * TO_LOG2)
            top_ref[0, chunk, j : j + 1, :] = most * TO_LOG2
            sum_ref[0, chunk, j : j + 1, :] = jnp.sum(total * weight, axis=0, keepdims=True)
            dot_ref[0, chunk, j : j + 1, :] = jnp.sum(dot * weight, axis=0, keepdims=True)


def prefix_kernel(
    core_ref, q_ref, g_ref, qo_ref, go_ref, pref_ref, slot_ref, top_ref, sum_ref, dot_ref,
    lse_ref, delta_ref, out_ref,
):
    count, _, each, _ = pref_ref.shape

    def gathered(which):
        rows = [pref_ref[part, which].astype(F32) for part in range(count)]
        return jnp.concatenate(rows, axis=0).astype(BF16)

    keys, values = gathered(0), gathered(1)
    heads = q_ref.shape[1] // HD
    slots = keys.shape[0] // PLEN
    grads = []
    for chunk in range(2):
        q, g = (stacked(qo_ref, (0,)), stacked(go_ref, (0,))) if chunk else (stacked(q_ref), stacked(g_ref))
        slot = jnp.concatenate([slot_ref[chunk]] * heads, axis=1)
        s_all = lax.dot_general(keys, q, NT, preferred_element_type=F32)
        dp_all = lax.dot_general(values, g, NT, preferred_element_type=F32)
        s, dp = s_all[:PLEN], dp_all[:PLEN]
        for k in range(1, slots):
            rows = slice(k * PLEN, (k + 1) * PLEN)
            s = jnp.where(slot == k, s_all[rows], s)
            dp = jnp.where(slot == k, dp_all[rows], dp)
        top = joined(top_ref, chunk)
        new = jnp.maximum(top, jnp.max(s, axis=0, keepdims=True) * TO_LOG2)
        e = jnp.exp2(s * TO_LOG2 - new)
        old = jnp.exp2(top - new)
        total = old * joined(sum_ref, chunk) + jnp.sum(e, axis=0, keepdims=True)
        dot = old * joined(dot_ref, chunk) + jnp.sum(e * dp, axis=0, keepdims=True)
        inverse = 1.0 / total
        delta = dot * inverse
        p = e * inverse
        ds = p * (dp - delta)
        split(lse_ref, chunk, new + jnp.log2(total))
        split(delta_ref, chunk, delta)
        zero = jnp.zeros_like(p)

        def spread(x, slot=slot, zero=zero):
            return jnp.concatenate(
                [jnp.where(slot == k, x, zero).astype(BF16) for k in range(slots)], axis=0
            )

        grads.append(
            (
                lax.dot_general(spread(ds), q, NN, preferred_element_type=F32),
                lax.dot_general(spread(p), g, NN, preferred_element_type=F32),
            )
        )
    dk, dv = (grads[0][0] + grads[1][0]) * SCALE, grads[0][1] + grads[1][1]
    for which, grad in enumerate((dk, dv)):
        for part in range(count):
            out_ref[part, which] = grad[part * each : (part + 1) * each].astype(BF16)


def token_grads_kernel(core_ref, q_ref, g_ref, qo_ref, go_ref, *refs):
    bias_ref, lse_ref, delta_ref, home_ref, one_ref, two_ref = refs[8:]
    even = core_ref[0] == 0
    keys, values = windows(even, *refs[:4]), windows(even, *refs[4:8])
    toks = q_ref.shape[0]
    heads = q_ref.shape[1] // HD
    found = []
    for chunk in range(2):
        q, g = (stacked(qo_ref, (0,)), stacked(go_ref, (0,))) if chunk else (stacked(q_ref), stacked(g_ref))
        bias = jnp.concatenate([bias_ref[chunk]] * heads, axis=1)
        s = lax.dot_general(keys[chunk], q, NT, preferred_element_type=F32) + bias
        dp = lax.dot_general(values[chunk], g, NT, preferred_element_type=F32)
        p = jnp.exp2(s * TO_LOG2 - joined(lse_ref, chunk))
        ds = (p * (dp - joined(delta_ref, chunk))).astype(BF16)
        dk = lax.dot_general(ds, q, NN, preferred_element_type=F32) * SCALE
        dv = lax.dot_general(p.astype(BF16), g, NN, preferred_element_type=F32)
        found.append((dk, dv))
    for which in range(2):
        a, b = (
            [found[chunk][which][n * toks : (n + 1) * toks] for n in range(5)] for chunk in range(2)
        )
        zero = jnp.zeros_like(a[4])
        home_ref[which, :toks] = a[0] + jnp.where(even, b[4], zero)
        home_ref[which, toks:] = b[0] + jnp.where(even, zero, a[4])
        one_ref[which, :toks] = (a[1] + b[1]).astype(BF16)
        one_ref[which, toks:] = (a[3] + b[2]).astype(BF16)
        two_ref[which, :toks] = (a[2] + jnp.where(even, zero, b[4])).astype(BF16)
        two_ref[which, toks:] = (b[3] + jnp.where(even, a[4], zero)).astype(BF16)


def planes(shape):
    lead = (0,) * (len(shape) - 1)
    return pl.BlockSpec((*shape[:-1], HD), lambda h, core: (*lead, h))


def whole(shape):
    return pl.BlockSpec(shape, lambda h, core: (0,) * len(shape))


def call(kernel, core, queries, others, flops, exps, ins, outs):
    q, g = queries
    toks, run, kept = q.shape[0], q.shape[1] // KVH, KVH // 2
    mine = pl.BlockSpec((toks, run), lambda h, core: (0, core[0] * kept + h))
    theirs = [
        pl.BlockSpec((1, toks, run), lambda h, core, which=which: (which, 0, h)) for which in range(2)
    ]
    return pl.pallas_call(
        kernel,
        grid_spec=pltpu.PrefetchScalarGridSpec(
            num_scalar_prefetch=1,
            grid=(kept,),
            in_specs=[mine, mine, *theirs] + [block for _, block in ins],
            out_specs=[block for _, block in outs],
        ),
        out_shape=[shape for shape, _ in outs],
        compiler_params=pltpu.CompilerParams(vmem_limit_bytes=56 << 20),
        cost_estimate=pl.CostEstimate(flops=flops, bytes_accessed=5 << 20, transcendentals=exps),
    )(core, q, g, others, others, *[array for array, _ in ins])


def stat(q):
    shape = (KVH // 2, 2, HQ // KVH, q.shape[0])
    block = pl.BlockSpec((1, *shape[1:]), lambda h, core: (h, 0, 0, 0))
    return jax.ShapeDtypeStruct(shape, F32), block


def window_ins(own, one, two, cross, bias):
    toks, kept = own.shape[1], KVH // 2
    ins = []
    for which in range(2):
        at = pl.BlockSpec((1, toks, HD), lambda h, core, which=which: (which, 0, core[0] * kept + h))
        far = pl.BlockSpec((3, 1, toks, HD), lambda h, core, which=which: (0, which, 0, h))
        ins += [(own, at), (one, at), (two, at), (cross, far)]
    return ins + [(bias, whole(bias.shape))]


def layout(lengths, tenants, slots, block, shards, toks):
    ends = jnp.cumsum(lengths)
    slot_of = jnp.sum(
        jnp.where(tenants[:, None] == jnp.arange(slots.shape[0])[None, :], slots[None, :], 0), axis=1
    )
    here = block * toks + jnp.arange(toks, dtype=jnp.int32)
    doc = jnp.sum((here[None, :] >= ends[:, None]).astype(jnp.int32), axis=0)
    pick = doc[None, :] == jnp.arange(lengths.shape[0])[:, None]
    first = jnp.sum(jnp.where(pick, (ends - lengths)[:, None], 0), axis=0)
    slot = jnp.sum(jnp.where(pick, slot_of[:, None], 0), axis=0)
    key = jnp.concatenate([s * toks + jnp.arange(toks, dtype=jnp.int32) for s in shards])
    ok = (key[:, None] >= first[None, :]) & (key[:, None] <= here[None, :])
    return jnp.where(ok, 0.0, -1e30).astype(F32), slot[None, :].astype(jnp.int32)


def per_device(
    queries, keys, values, grad_out, prefix_keys, prefix_values, doc_lengths, doc_tenants, tenant_slots
):
    toks, width = queries.shape
    parts = lax.axis_size("z")
    count = parts * 2
    index, core = lax.axis_index(SEQ), lax.axis_index("core").astype(jnp.int32)
    even = core == 0
    cores = core[None]

    def shift(x, steps):
        pairs = [(i, i + 2 * steps) for i in range(count) if 0 <= i + 2 * steps < count]
        return lax.ppermute(x, SEQ, pairs)

    def swap(x):
        return lax.ppermute(x, SEQ, [(i, i ^ 1) for i in range(count)])

    def exchange(x, axis):
        return lax.all_to_all(x, axis, split_axis=0, concat_axis=0, tiled=True)

    def to_all(x, axis):
        return exchange(jnp.broadcast_to(x[None], (lax.axis_size(axis), *x.shape)), axis)

    def other_half(x):
        half = x.shape[-1] // 2
        return jnp.where(even, x[..., half:], x[..., :half])

    own = jnp.stack([keys, values])
    one, two = shift(own, 1), shift(own, 2)
    pref = jnp.stack([prefix_keys, prefix_values])
    pref = pref.reshape(2, -1, 2, KVH * HD // 2).transpose(2, 0, 1, 3)
    pref = jnp.broadcast_to(pref[None], (parts, *pref.shape)).reshape(count, *pref.shape[1:])
    pref = exchange(pref, SEQ)
    others = swap(jnp.stack([other_half(queries), other_half(grad_out)]))
    cross = swap(jnp.stack([other_half(own), other_half(one), other_half(two)]))

    facing = index ^ 1
    near, far = jnp.where(even, index - 1, index - 3), jnp.where(even, index - 3, index - 1)
    docs = (doc_lengths[0], doc_tenants[0], tenant_slots)
    shards = [index, index - 2, index - 4, near, far]
    bias0, slot0 = layout(*docs, index, shards, toks)
    last = jnp.where(even, index, index - 4)
    shards = [facing, index - 2, facing - 2, facing - 4, last]
    bias1, slot1 = layout(*docs, facing, shards, toks)
    bias, slot = jnp.stack([bias0, bias1]), jnp.stack([slot0, slot1])

    run = functools.partial(call, core=cores, queries=(queries, grad_out), others=others)
    stats = stat(queries)
    work = queries.size // HD * bias.shape[1]
    window = window_ins(own, one, two, cross, bias)
    top, total, dot = run(
        token_stats_kernel, flops=4 * HD * work, exps=work, ins=window, outs=[stats] * 3
    )
    prefs = queries.size // HD * count * pref.shape[2]
    lse, delta, rows = run(
        prefix_kernel,
        flops=8 * HD * prefs,
        exps=prefs // 6,
        ins=[(pref, planes(pref.shape)), (slot, whole(slot.shape))]
        + [(x, stats[1]) for x in (top, total, dot)],
        outs=[stats, stats, (jax.ShapeDtypeStruct(pref.shape, BF16), planes(pref.shape))],
    )

    rows = exchange(rows, SEQ).astype(F32)
    rows = jnp.sum(rows.reshape(parts, 2, *rows.shape[1:]), axis=0)
    rows = jnp.sum(to_all(rows, "x"), axis=0)
    rows = jnp.sum(to_all(rows.astype(BF16), "y").astype(F32), axis=0)
    rows = rows.transpose(1, 2, 0, 3).reshape(2, prefix_keys.shape[0], KVH * HD)

    wide = (2, 2 * toks, KVH * HD // 2)
    home, back1, back2 = run(
        token_grads_kernel,
        flops=8 * HD * work,
        exps=work,
        ins=window + [(lse, stats[1]), (delta, stats[1])],
        outs=[
            (jax.ShapeDtypeStruct(wide, F32), planes(wide)),
            (jax.ShapeDtypeStruct(wide, BF16), planes(wide)),
            (jax.ShapeDtypeStruct(wide, BF16), planes(wide)),
        ],
    )
    back1, back2 = shift(back1, -1), shift(back2, -2)
    grads = (home + back1.astype(F32) + back2.astype(F32)).astype(BF16)
    mine, theirs = grads[:, :toks], swap(grads[:, toks:])
    grads = jnp.concatenate(
        [jnp.where(even, mine, theirs), jnp.where(even, theirs, mine)], axis=2
    )
    return grads[0], grads[1], rows[0], rows[1]


def solution(mesh):
    mesh = Mesh(mesh.devices.reshape(8, 4, 8, 2), ("y", "x", "z", "core"))
    rows, dp, seq = P(("y", "x", "z", "core"), None), P(("y", "x"), None), P(SEQ, None)
    return jax.shard_map(
        per_device,
        mesh=mesh,
        in_specs=(rows, rows, rows, rows, seq, seq, dp, dp, P()),
        out_specs=(rows, rows, seq, seq),
        check_vma=False,
    )
```

time: 155 us -> 117 us (0.75)
  waiting for transfers between devices: 27.1 us -> 12.7 us
  Pallas kernels: 36.3 us -> 27.9 us
  blocking collectives: 29.3 us -> 21.8 us
  starting transfers between devices: 42 us -> 39.5 us
  other arithmetic: 10.2 us -> 7.83 us
  local copies, waits for them, and re-layouts: 7.84 us -> 5.74 us
    all_gather x1 -> x0, blocking collectives: 29.3 us -> none  [per_device(): lax.all_gather(jnp.concatenate([prefix_keys, prefix_values], axis=1), SEQ...]
    all_to_all x0 -> x1, blocking collectives: none -> 21.8 us  [exchange(): return lax.all_to_all(x, axis, split_axis=0, concat_axis=0, tiled=True)]
    all_to_all x3, waiting for transfers between devices: 24.1 us -> 4.12 us  [exchange(): return lax.all_to_all(x, axis, split_axis=0, concat_axis=0, tiled=True)]
    pallas_call x1 -> x3, Pallas kernels: 36.3 us -> 27.9 us  [call(): pl.pallas_call(kernel, grid_spec=pltpu.PrefetchScalarGridSpec(num_scalar_...]
    another operation x1 -> x10, other arithmetic: 0.83 us -> 6.07 us  [the longest x2 3.3 us: per_device(): others = swap(jnp.stack([other_half(queries), other_half(grad_out)]))]
    ppermute x4, waiting for transfers between devices: 2.96 us -> 7.05 us  [shift(): return lax.ppermute(x, SEQ, pairs)]
    convert_element_type x4 -> x1, other arithmetic: 3.12 us -> 0.08 us  [per_device(): grads = (home + back1.astype(F32) + back2.astype(F32)).astype(BF16)]
    select_n x4 -> x3, other arithmetic: 2.53 us -> 0.32 us  [the longest x2 0.3 us: layout(): jnp.where(ok, 0.0, -1e+30).astype(F32)]
  transfers between devices with their start and end apart: 11 -> 10, of which waited for: 4 -> 5; matrix products, arithmetic and copies ran while one was open for 7% -> 7% of each run, Pallas kernels for 0% -> 17%
where the time goes in v3:
time: 117 us; the launch traced here: 116 us
  starting transfers between devices  39.5 us (34%)
  Pallas kernels  27.9 us (24%)
  blocking collectives  21.8 us (19%)
  waiting for transfers between devices  12.7 us (11%)
  other arithmetic  7.83 us (7%)
  local copies, waits for them, and re-layouts  5.74 us (5%)
    pallas_call x3, Pallas kernels, call(): pl.pallas_call(kernel, grid_spec=pltpu.PrefetchScalarGridSpec(num_scalar_...  27.9 us
    all_to_all x1, blocking collectives, exchange(): return lax.all_to_all(x, axis, split_axis=0, concat_axis=0, tiled=True)  21.8 us
    all_to_all x3, starting transfers between devices, exchange(): return lax.all_to_all(x, axis, split_axis=0, concat_axis=0, tiled=True)  18.5 us
    ppermute x4, starting transfers between devices, shift(): return lax.ppermute(x, SEQ, pairs)  13.4 us
    ppermute x3, starting transfers between devices, swap(): return lax.ppermute(x, SEQ, [(i, i ^ 1) for i in range(count)])  7.56 us
    ppermute x4, waiting for transfers between devices, shift(): return lax.ppermute(x, SEQ, pairs)  7.05 us
    all_to_all x3, waiting for transfers between devices, exchange(): return lax.all_to_all(x, axis, split_axis=0, concat_axis=0, tiled=True)  4.12 us
    unnamed x30, local copies, waits for them, and re-layouts  3.3 us
  transfers between devices with their start and end apart: 10, of which 5 were waited for; matrix products, arithmetic and copies ran while one was open for 7% of the time, Pallas kernels for 17%

profile of v3, /device:TPU:1, one launch (start us, length us, event | category | flops | bytes accessed | tf_op | source)
XLA Modules:
  0.0 116.4 jit_solution(3301415332968055404)
XLA Ops:
  0.6 1.0 pad_maximum_fusion.3.refs_0_.refs_4_
  1.6 0.0 copy-start.1
  1.6 4.8 %collective-permute-start.1 = (bf16[2,128,512]{2,1,0:T(8,128)(2,1)S(1)}, bf16[2,128,512]{2,1,0:T(8,128)(2,1)S(1)}, u32[]{:S(2)}, u32[]{:S(2)}) collective-permute-start(bf16[2,128,512]{2,1,0:T(8,128)(2,1)S(1)} %pad_maximum_fusion.3.refs_0_.refs_4_), channel_id=1, source_target_pairs={{0,2},{1,3},{2,4},{3,5},{4,6},{5,7},{6,8},{7,9},{8,10},{9,11},{10,... | collective-permute-start | bytes 786440 | tf_op jit(solution)/shard_map/ppermute | solution.py:239
  6.5 5.8 %collective-permute-start.2 = (bf16[2,128,512]{2,1,0:T(8,128)(2,1)S(1)}, bf16[2,128,512]{2,1,0:T(8,128)(2,1)S(1)}, u32[]{:S(2)}, u32[]{:S(2)}) collective-permute-start(bf16[2,128,512]{2,1,0:T(8,128)(2,1)S(1)} %pad_maximum_fusion.3.refs_0_.refs_4_), channel_id=1, source_target_pairs={{0,4},{1,5},{2,6},{3,7},{4,8},{5,9},{6,10},{7,11},{8,12},{9,13},{1... | collective-permute-start | bytes 786440 | tf_op jit(solution)/shard_map/ppermute | solution.py:239
  12.3 2.0 %select_bitcast_fusion = (bf16[1,128,3072]{2,1,0:T(8,128)(2,1)S(1)}, bf16[1,128,3072]{2,1,0:T(8,128)(2,1)S(1)}) fusion(bf16[128,6144]{1,0:T(8,128)(2,1)} %g_ref.5, pred[]{:T(512)S(6)} %eq.22, bf16[128,6144]{1,0:T(8,128)(2,1)} %q_ref.5), kind=kLoop, calls=%fused_computation.3 | loop fusion | flops 786432 | bytes 4718593 | tf_op jit(solution)/shard_map/stack | solution.py:260
  14.3 0.0 copy-done.1
  14.3 0.0 copy-start.9
  14.3 0.0 copy-start.10
  14.4 0.0 copy-start.11
  14.4 1.3 %pad_maximum_fusion = bf16[2,128,3072]{2,1,0:T(8,128)(2,1)} fusion(bf16[1,128,3072]{2,1,0:T(8,128)(2,1)S(1)} %get-tuple-element.34, bf16[1,128,3072]{2,1,0:T(8,128)(2,1)S(1)} %get-tuple-element.35), kind=kLoop, calls=%fused_computation | loop fusion | flops 786432 | bytes 3145728 | tf_op jit(solution)/shard_map/stack | solution.py:260
  15.7 3.3 %collective-permute-start = (bf16[2,128,3072]{2,1,0:T(8,128)(2,1)}, bf16[2,128,3072]{2,1,0:T(8,128)(2,1)S(1)}, u32[]{:S(2)}, u32[]{:S(2)}) collective-permute-start(bf16[2,128,3072]{2,1,0:T(8,128)(2,1)} %pad_maximum_fusion), channel_id=1, source_target_pairs={{0,1},{1,0},{2,3},{3,2},{4,5},{5,4},{6,7},{7,6},{8,9},{9,8},{10,11... | collective-permute-start | bytes 4718600 | tf_op jit(solution)/shard_map/ppermute | solution.py:242
  19.0 0.0 copy-done.9
  19.0 0.0 copy-done.10
  19.0 0.1 maximum_bitcast_fusion
  19.1 0.8 broadcast_in_dim.102
  19.9 7.7 %all-to-all-start = ((bf16[16,2,24,256]{3,2,1,0:T(8,128)(2,1)}), bf16[16,2,24,256]{3,2,1,0:T(8,128)(2,1)S(1)}, u32[]{:S(2)}, u32[]{:S(2)}) async-start(bf16[16,2,24,256]{3,2,1,0:T(8,128)(2,1)} %bitcast.12), calls=%async_computation | async-start | bytes 786432 | tf_op jit(solution)/shard_map/all_to_all | solution.py:245
  27.6 0.0 copy-done.11
  27.6 0.2 reduce-window.7
  27.9 0.0 copy-done.12
  27.9 0.0 copy-done.13
  27.9 0.2 select_reduce_fusion.2
  28.1 0.1 convert_reduce_fusion.3
  28.2 0.1 select_reduce_fusion.1
  28.3 0.6 pad_add_fusion.slot_ref
  28.9 0.1 and_select_fusion
  29.0 0.0 copy-done.6
  29.1 0.0 copy-done.7
  29.1 0.0 collective-permute-done.2.refs_2_.refs_6_
  29.2 0.0 collective-permute-done.1.refs_1_.refs_5_
  29.3 2.0 %collective-permute-start.3 = (bf16[3,2,128,256]{3,2,1,0:T(8,128)(2,1)S(1)}, bf16[3,2,128,256]{3,2,1,0:T(8,128)(2,1)S(1)}, u32[]{:S(2)}, u32[]{:S(2)}) collective-permute-start(bf16[3,2,128,256]{3,2,1,0:T(8,128)(2,1)S(1)} %pad_maximum_fusion.2), channel_id=1, source_target_pairs={{0,1},{1,0},{2,3},{3,2},{4,5},{5,4},{6,7},{7,6},{8,9},{9,8},{10,11... | collective-permute-start | bytes 1179656 | tf_op jit(solution)/shard_map/ppermute | solution.py:242
  31.3 0.2 and_select_fusion.1
  31.5 0.9 pad_maximum_fusion.1.refs_8_
  32.3 0.0 copy-done.3
  32.4 0.5 collective-permute-done.3.refs_3_.refs_7_
  32.9 0.0 collective-permute-done.qo_ref.go_ref
  32.9 0.0 copy-done.2
  32.9 0.7 copy-done.4
  33.6 0.5 copy-done
  34.2 8.8 %shard_map.120 = (f32[2,2,12,128]{3,2,1,0:T(8,128)}, f32[2,2,12,128]{3,2,1,0:T(8,128)}, f32[2,2,12,128]{3,2,1,0:T(8,128)}) custom-call(s32[1]{0:T(128)} %bitcast.core_ref, bf16[128,6144]{1,0:T(8,128)(2,1)} %q_ref.5, bf16[128,6144]{1,0:T(8,128)(2,1)} %g_ref.5, bf16[2,128,3072]{2,1,0:T(8,128)(2,1)} %copy-done, bf16[2,128,3072]{2,1,0:T(8,128)(2,1)} %copy-done, ...), custom_call_target="tpu_custom_call" | custom-call | flops 2013265920 | bytes 5242880 | tf_op jit(solution)/shard_map/pallas_call | solution.py:182
  42.9 0.0 all-to-all-done.pref_ref
  42.9 0.0 copy-start.8
  43.0 0.7 copy-done.8
  43.7 7.5 %shard_map.121 = (f32[2,2,12,128]{3,2,1,0:T(8,128)}, f32[2,2,12,128]{3,2,1,0:T(8,128)}, bf16[16,2,24,256]{3,2,1,0:T(8,128)(2,1)}) custom-call(s32[1]{0:T(128)} %bitcast.core_ref, bf16[128,6144]{1,0:T(8,128)(2,1)} %q_ref.5, bf16[128,6144]{1,0:T(8,128)(2,1)} %g_ref.5, bf16[2,128,3072]{2,1,0:T(8,128)(2,1)} %copy-done, bf16[2,128,3072]{2,1,0:T(8,128)(2,1)} %copy-done, ...), custom_call_target="tpu_custom_call" | custom-call | flops 2415919104 | bytes 5242880 | tf_op jit(solution)/shard_map/pallas_call | solution.py:182
  51.2 21.8 %all_to_all.20 = bf16[16,2,24,256]{3,2,1,0:T(8,128)(2,1)S(1)} all-to-all(bf16[16,2,24,256]{3,2,1,0:T(8,128)(2,1)} %get-tuple-element.21), channel_id=1, replica_groups=mesh['y'=8,'x'=4,'z'=8,'core'=2] {'z','core'}, dimensions={0} | all-to-all | bytes 786432 | tf_op jit(solution)/shard_map/all_to_all | solution.py:245
  73.0 0.1 convert_reduce_fusion
  73.1 0.8 broadcast_in_dim.106
  73.8 4.0 %all-to-all-start.2 = ((f32[4,2,2,24,256]{4,3,2,1,0:T(8,128)}), f32[4,2,2,24,256]{4,3,2,1,0:T(8,128)S(1)}, u32[]{:S(2)}, u32[]{:S(2)}) async-start(f32[4,2,2,24,256]{4,3,2,1,0:T(8,128)} %broadcast_in_dim.106), calls=%async_computation.2 | async-start | bytes 786432 | tf_op jit(solution)/shard_map/all_to_all | solution.py:245
  77.9 11.6 %shard_map.122 = (f32[2,256,256]{2,1,0:T(8,128)}, bf16[2,256,256]{2,1,0:T(8,128)(2,1)}, bf16[2,256,256]{2,1,0:T(8,128)(2,1)}) custom-call(s32[1]{0:T(128)} %bitcast.core_ref, bf16[128,6144]{1,0:T(8,128)(2,1)} %q_ref.5, bf16[128,6144]{1,0:T(8,128)(2,1)} %g_ref.5, bf16[2,128,3072]{2,1,0:T(8,128)(2,1)} %copy-done, bf16[2,128,3072]{2,1,0:T(8,128)(2,1)} %copy-done, ...), custom_call_target="tpu_custom_call" | custom-call | flops 4026531840 | bytes 5242880 | tf_op jit(solution)/shard_map/pallas_call | solution.py:182
  89.4 0.0 copy-start.5
  89.4 1.4 %collective-permute-start.5 = (bf16[2,256,256]{2,1,0:T(8,128)(2,1)}, bf16[2,256,256]{2,1,0:T(8,128)(2,1)S(1)}, u32[]{:S(2)}, u32[]{:S(2)}) collective-permute-start(bf16[2,256,256]{2,1,0:T(8,128)(2,1)} %get-tuple-element.20), channel_id=1, source_target_pairs={{4,0},{5,1},{6,2},{7,3},{8,4},{9,5},{10,6},{11,7},{12,8},{13,9},{1... | collective-permute-start | bytes 786440 | tf_op jit(solution)/shard_map/ppermute | solution.py:239
  90.9 1.3 %collective-permute-start.4 = (bf16[2,256,256]{2,1,0:T(8,128)(2,1)}, bf16[2,256,256]{2,1,0:T(8,128)(2,1)S(1)}, u32[]{:S(2)}, u32[]{:S(2)}) collective-permute-start(bf16[2,256,256]{2,1,0:T(8,128)(2,1)} %get-tuple-element.19), channel_id=1, source_target_pairs={{2,0},{3,1},{4,2},{5,3},{6,4},{7,5},{8,6},{9,7},{10,8},{11,9},{12,... | collective-permute-start | bytes 786440 | tf_op jit(solution)/shard_map/ppermute | solution.py:239
  92.2 0.0 all-to-all-done.2
  92.2 0.8 broadcast_in_dim.107
  93.0 6.8 %all-to-all-start.3 = ((bf16[8,2,2,24,256]{4,3,2,1,0:T(8,128)(2,1)}), bf16[8,2,2,24,256]{4,3,2,1,0:T(8,128)(2,1)S(1)}, u32[]{:S(2)}, u32[]{:S(2)}) async-start(bf16[8,2,2,24,256]{4,3,2,1,0:T(8,128)(2,1)} %broadcast_in_dim.107), calls=%async_computation.3 | async-start | bytes 786432 | tf_op jit(solution)/shard_map/all_to_all | solution.py:245
  99.8 5.5 %collective-permute-done.5 = bf16[2,256,256]{2,1,0:T(8,128)(2,1)S(1)} collective-permute-done((bf16[2,256,256]{2,1,0:T(8,128)(2,1)}, bf16[2,256,256]{2,1,0:T(8,128)(2,1)S(1)}, u32[]{:S(2)}, u32[]{:S(2)}) %collective-permute-start.5) | collective-permute-done | bytes 262176 | tf_op jit(solution)/shard_map/ppermute | solution.py:239
  105.3 1.5 %collective-permute-done.4 = bf16[2,256,256]{2,1,0:T(8,128)(2,1)S(1)} collective-permute-done((bf16[2,256,256]{2,1,0:T(8,128)(2,1)}, bf16[2,256,256]{2,1,0:T(8,128)(2,1)S(1)}, u32[]{:S(2)}, u32[]{:S(2)}) %collective-permute-start.4) | collective-permute-done | bytes 262176 | tf_op jit(solution)/shard_map/ppermute | solution.py:239
  106.8 0.1 add_convert_fusion
  106.9 2.3 %collective-permute-start.6 = (bf16[2,128,256]{2,1,0:T(8,128)(2,1)S(1)}, bf16[2,128,256]{2,1,0:T(8,128)(2,1)S(1)}, u32[]{:S(2)}, u32[]{:S(2)}) collective-permute-start(bf16[2,128,256]{2,1,0:T(8,128)(2,1)S(1)} %slice.75), channel_id=1, source_target_pairs={{0,1},{1,0},{2,3},{3,2},{4,5},{5,4},{6,7},{7,6},{8,9},{9,8},{10,11... | collective-permute-start | bytes 393224 | tf_op jit(solution)/shard_map/ppermute | solution.py:242
  109.2 1.0 collective-permute-done.6
  110.2 0.7 fusion.6
  110.9 4.1 %all-to-all-done.3 = bf16[8,2,2,24,256]{4,3,2,1,0:T(8,128)(2,1)S(1)} async-done(((bf16[8,2,2,24,256]{4,3,2,1,0:T(8,128)(2,1)}), bf16[8,2,2,24,256]{4,3,2,1,0:T(8,128)(2,1)S(1)}, u32[]{:S(2)}, u32[]{:S(2)}) %all-to-all-start.3) | async-done | bytes 393248 | tf_op jit(solution)/shard_map/all_to_all | solution.py:245
  115.0 0.1 convert_reduce_fusion.1
  115.2 0.6 copy.18
  115.8 0.6 copy.19
  (35 shorter events, 0.4 us)
Async XLA Ops:
  1.6 12.7 %copy-start.1 = (bf16[2,128,512]{2,1,0:T(8,128)(2,1)}, bf16[2,128,512]{2,1,0:T(8,128)(2,1)S(1)}, u32[]{:S(2)}) copy-start(bf16[2,128,512]{2,1,0:T(8,128)(2,1)S(1)} %pad_maximum_fusion.3.refs_0_.refs_4_) | copy-start | bytes 786436
  1.6 27.5 %collective-permute-start.1 = (bf16[2,128,512]{2,1,0:T(8,128)(2,1)S(1)}, bf16[2,128,512]{2,1,0:T(8,128)(2,1)S(1)}, u32[]{:S(2)}, u32[]{:S(2)}) collective-permute-start(bf16[2,128,512]{2,1,0:T(8,128)(2,1)S(1)} %pad_maximum_fusion.3.refs_0_.refs_4_), channel_id=1, source_target_pairs={{0,2},{1,3},{2,4},{3,5},{4,6},{5,7},{6,8},{7,9},{8,10},{9,11},{10,... | collective-permute-start | bytes 786440 | tf_op jit(solution)/shard_map/ppermute | solution.py:239
  6.5 22.6 %collective-permute-start.2 = (bf16[2,128,512]{2,1,0:T(8,128)(2,1)S(1)}, bf16[2,128,512]{2,1,0:T(8,128)(2,1)S(1)}, u32[]{:S(2)}, u32[]{:S(2)}) collective-permute-start(bf16[2,128,512]{2,1,0:T(8,128)(2,1)S(1)} %pad_maximum_fusion.3.refs_0_.refs_4_), channel_id=1, source_target_pairs={{0,4},{1,5},{2,6},{3,7},{4,8},{5,9},{6,10},{7,11},{8,12},{9,13},{1... | collective-permute-start | bytes 786440 | tf_op jit(solution)/shard_map/ppermute | solution.py:239
  14.3 4.6 %copy-start.9 = (bf16[24,512]{1,0:T(8,128)(2,1)S(1)}, bf16[24,512]{1,0:T(8,128)(2,1)}, u32[]{:S(2)}) copy-start(bf16[24,512]{1,0:T(8,128)(2,1)} %param.14) | copy-start | bytes 73732
  14.3 4.6 %copy-start.10 = (bf16[24,512]{1,0:T(8,128)(2,1)S(1)}, bf16[24,512]{1,0:T(8,128)(2,1)}, u32[]{:S(2)}) copy-start(bf16[24,512]{1,0:T(8,128)(2,1)} %param.13) | copy-start | bytes 73732
  14.4 13.3 %copy-start.11 = (s32[1,8]{1,0:T(1,128)S(1)}, s32[1,8]{1,0:T(1,128)}, u32[]{:S(2)}) copy-start(s32[1,8]{1,0:T(1,128)} %param.15) | copy-start | bytes 100
  15.7 12.2 %copy-start.12 = (s32[6]{0:T(128)S(1)}, s32[6]{0:T(128)}, u32[]{:S(2)}) copy-start(s32[6]{0:T(128)} %param.17) | copy-start | bytes 76
  15.7 12.2 %copy-start.13 = (s32[1,8]{1,0:T(1,128)S(1)}, s32[1,8]{1,0:T(1,128)}, u32[]{:S(2)}) copy-start(s32[1,8]{1,0:T(1,128)} %param.16) | copy-start | bytes 100
  15.7 13.4 %copy-start.6 = (bf16[128,512]{1,0:T(8,128)(2,1)S(1)}, bf16[128,512]{1,0:T(8,128)(2,1)}, u32[]{:S(2)}) copy-start(bf16[128,512]{1,0:T(8,128)(2,1)} %param.11) | copy-start | bytes 393220
  15.7 13.4 %copy-start.7 = (bf16[128,512]{1,0:T(8,128)(2,1)S(1)}, bf16[128,512]{1,0:T(8,128)(2,1)}, u32[]{:S(2)}) copy-start(bf16[128,512]{1,0:T(8,128)(2,1)} %param.10) | copy-start | bytes 393220
  15.7 17.2 %collective-permute-start = (bf16[2,128,3072]{2,1,0:T(8,128)(2,1)}, bf16[2,128,3072]{2,1,0:T(8,128)(2,1)S(1)}, u32[]{:S(2)}, u32[]{:S(2)}) collective-permute-start(bf16[2,128,3072]{2,1,0:T(8,128)(2,1)} %pad_maximum_fusion), channel_id=1, source_target_pairs={{0,1},{1,0},{2,3},{3,2},{4,5},{5,4},{6,7},{7,6},{8,9},{9,8},{10,11... | collective-permute-start | bytes 4718600 | tf_op jit(solution)/shard_map/ppermute | solution.py:242
  19.9 23.1 %all-to-all-start = ((bf16[16,2,24,256]{3,2,1,0:T(8,128)(2,1)}), bf16[16,2,24,256]{3,2,1,0:T(8,128)(2,1)S(1)}, u32[]{:S(2)}, u32[]{:S(2)}) async-start(bf16[16,2,24,256]{3,2,1,0:T(8,128)(2,1)} %bitcast.12), calls=%async_computation | async-start | bytes 786432 | tf_op jit(solution)/shard_map/all_to_all | solution.py:245
  29.1 3.2 %copy-start.3 = (bf16[2,128,512]{2,1,0:T(8,128)(2,1)}, bf16[2,128,512]{2,1,0:T(8,128)(2,1)S(1)}, u32[]{:S(2)}) copy-start(bf16[2,128,512]{2,1,0:T(8,128)(2,1)S(1)} %collective-permute-done.2.refs_2_.refs_6_) | copy-start | bytes 786436
  29.2 3.7 %copy-start.2 = (bf16[2,128,512]{2,1,0:T(8,128)(2,1)}, bf16[2,128,512]{2,1,0:T(8,128)(2,1)S(1)}, u32[]{:S(2)}) copy-start(bf16[2,128,512]{2,1,0:T(8,128)(2,1)S(1)} %collective-permute-done.1.refs_1_.refs_5_) | copy-start | bytes 786436
  29.3 3.6 %collective-permute-start.3 = (bf16[3,2,128,256]{3,2,1,0:T(8,128)(2,1)S(1)}, bf16[3,2,128,256]{3,2,1,0:T(8,128)(2,1)S(1)}, u32[]{:S(2)}, u32[]{:S(2)}) collective-permute-start(bf16[3,2,128,256]{3,2,1,0:T(8,128)(2,1)S(1)} %pad_maximum_fusion.2), channel_id=1, source_target_pairs={{0,1},{1,0},{2,3},{3,2},{4,5},{5,4},{6,7},{7,6},{8,9},{9,8},{10,11... | collective-permute-start | bytes 1179656 | tf_op jit(solution)/shard_map/ppermute | solution.py:242
  32.9 0.8 copy-start.4
  32.9 1.3 %copy-start = (bf16[2,128,3072]{2,1,0:T(8,128)(2,1)}, bf16[2,128,3072]{2,1,0:T(8,128)(2,1)S(1)}, u32[]{:S(2)}) copy-start(bf16[2,128,3072]{2,1,0:T(8,128)(2,1)S(1)} %collective-permute-done.qo_ref.go_ref) | copy-start | bytes 4718596
  42.9 0.7 copy-start.8
  73.8 18.3 %all-to-all-start.2 = ((f32[4,2,2,24,256]{4,3,2,1,0:T(8,128)}), f32[4,2,2,24,256]{4,3,2,1,0:T(8,128)S(1)}, u32[]{:S(2)}, u32[]{:S(2)}) async-start(f32[4,2,2,24,256]{4,3,2,1,0:T(8,128)} %broadcast_in_dim.106), calls=%async_computation.2 | async-start | bytes 786432 | tf_op jit(solution)/shard_map/all_to_all | solution.py:245
  89.4 17.4 %copy-start.5 = (f32[2,256,256]{2,1,0:T(8,128)S(1)}, f32[2,256,256]{2,1,0:T(8,128)}, u32[]{:S(2)}) copy-start(f32[2,256,256]{2,1,0:T(8,128)} %get-tuple-element.18) | copy-start | bytes 1572868
  89.4 15.9 %collective-permute-start.5 = (bf16[2,256,256]{2,1,0:T(8,128)(2,1)}, bf16[2,256,256]{2,1,0:T(8,128)(2,1)S(1)}, u32[]{:S(2)}, u32[]{:S(2)}) collective-permute-start(bf16[2,256,256]{2,1,0:T(8,128)(2,1)} %get-tuple-element.20), channel_id=1, source_target_pairs={{4,0},{5,1},{6,2},{7,3},{8,4},{9,5},{10,6},{11,7},{12,8},{13,9},{1... | collective-permute-start | bytes 786440 | tf_op jit(solution)/shard_map/ppermute | solution.py:239
  90.9 16.0 %collective-permute-start.4 = (bf16[2,256,256]{2,1,0:T(8,128)(2,1)}, bf16[2,256,256]{2,1,0:T(8,128)(2,1)S(1)}, u32[]{:S(2)}, u32[]{:S(2)}) collective-permute-start(bf16[2,256,256]{2,1,0:T(8,128)(2,1)} %get-tuple-element.19), channel_id=1, source_target_pairs={{2,0},{3,1},{4,2},{5,3},{6,4},{7,5},{8,6},{9,7},{10,8},{11,9},{12,... | collective-permute-start | bytes 786440 | tf_op jit(solution)/shard_map/ppermute | solution.py:239
  93.0 22.1 %all-to-all-start.3 = ((bf16[8,2,2,24,256]{4,3,2,1,0:T(8,128)(2,1)}), bf16[8,2,2,24,256]{4,3,2,1,0:T(8,128)(2,1)S(1)}, u32[]{:S(2)}, u32[]{:S(2)}) async-start(bf16[8,2,2,24,256]{4,3,2,1,0:T(8,128)(2,1)} %broadcast_in_dim.107), calls=%async_computation.3 | async-start | bytes 786432 | tf_op jit(solution)/shard_map/all_to_all | solution.py:245
  106.9 3.2 %collective-permute-start.6 = (bf16[2,128,256]{2,1,0:T(8,128)(2,1)S(1)}, bf16[2,128,256]{2,1,0:T(8,128)(2,1)S(1)}, u32[]{:S(2)}, u32[]{:S(2)}) collective-permute-start(bf16[2,128,256]{2,1,0:T(8,128)(2,1)S(1)} %slice.75), channel_id=1, source_target_pairs={{0,1},{1,0},{2,3},{3,2},{4,5},{5,4},{6,7},{7,6},{8,9},{9,8},{10,11... | collective-permute-start | bytes 393224 | tf_op jit(solution)/shard_map/ppermute | solution.py:242

commit v4 on v3

v4 whole, which is shorter than its diff:
```python
import math

import jax
import jax.numpy as jnp
from jax import lax
from jax.experimental import pallas as pl
from jax.experimental.pallas import tpu as pltpu
from jax.sharding import Mesh, PartitionSpec as P

HQ = 48
KVH = 4
HD = 128
PLEN = 64
NT = (((1,), (1,)), ((), ()))
NN = (((1,), (0,)), ((), ()))
SEQ = ("z", "core")
SCALE = 1.0 / math.sqrt(HD)
TO_LOG2 = SCALE * math.log2(math.e)
F32 = jnp.float32
BF16 = jnp.bfloat16
VMEM_BYTES = 20 << 20


def heads_of(ref, start, count, lead=()):
    columns = [slice(start + j * HD, start + (j + 1) * HD) for j in range(count)]
    return jnp.concatenate([ref[(*lead, slice(None), c)] for c in columns], axis=0)


def joined(ref, kind, h, chunk):
    return jnp.concatenate([ref[kind, h, chunk, j : j + 1, :] for j in range(ref.shape[3])], axis=1)


def split(ref, kind, h, chunk, row):
    for j in range(ref.shape[3]):
        ref[kind, h, chunk, j : j + 1, :] = row[:, j * HD : (j + 1) * HD]


def units(mine_ref, others_ref):
    kept = KVH // 2
    run = mine_ref.shape[2] // kept
    found = []
    for h in range(kept):
        for chunk, ref in enumerate((mine_ref, others_ref)):

            def read(which, first, count, h=h, ref=ref):
                return heads_of(ref, h * run + first * HD, count, (which,))

            found.append((h, chunk, read))
    return found, run // HD


def windows(core, h, which, own_ref, one_ref, two_ref, cross_ref):
    at = pl.ds(pl.multiple_of((core * (KVH // 2) + h) * HD, HD), HD)
    own, one, two = (ref[which, :, at] for ref in (own_ref, one_ref, two_ref))
    cross = [cross_ref[n, which, :, h * HD : (h + 1) * HD] for n in range(3)]
    even = core == 0
    last = jnp.where(even, own.astype(F32), two.astype(F32)).astype(BF16)
    far = jnp.where(even, cross[2].astype(F32), cross[0].astype(F32)).astype(BF16)
    return (
        jnp.concatenate([own, one, two, cross[1], far], axis=0),
        jnp.concatenate([cross[0], one, cross[1], cross[2], last], axis=0),
    )


def token_stats_kernel(core_ref, mine_ref, others_ref, *refs):
    window, (bias_ref, stat_ref) = refs[:4], refs[4:]
    core = core_ref[0]
    toks = mine_ref.shape[1]
    blocks = bias_ref.shape[1] // toks
    found, heads = units(mine_ref, others_ref)
    for h, chunk, read in found:
        keys, values = (windows(core, h, which, *window)[chunk] for which in range(2))

        def dots(j, keys=keys, values=values, read=read):
            return (
                lax.dot_general(keys, read(0, j, 1), NT, preferred_element_type=F32),
                lax.dot_general(values, read(1, j, 1), NT, preferred_element_type=F32),
            )

        ahead = dots(0)
        for j in range(heads):
            s_all, dp_all = ahead
            if j + 1 < heads:
                ahead = dots(j + 1)
            top = total = dot = None
            for b in range(blocks):
                rows = slice(b * toks, (b + 1) * toks)
                s = (s_all[rows] + bias_ref[chunk, rows, :]).reshape(toks // 8, 8, toks)
                dp = dp_all[rows].reshape(toks // 8, 8, toks)
                new = jnp.max(s, axis=0)
                new = new if top is None else jnp.maximum(top, new)
                e = jnp.exp2(s * TO_LOG2 - (new * TO_LOG2)[None])
                e_sum, e_dot = jnp.sum(e, axis=0), jnp.sum(e * dp, axis=0)
                if top is not None:
                    old = jnp.exp2(top * TO_LOG2 - new * TO_LOG2)
                    e_sum, e_dot = old * total + e_sum, old * dot + e_dot
                top, total, dot = new, e_sum, e_dot
            most = jnp.max(top, axis=0, keepdims=True)
            weight = jnp.exp2((top - most) * TO_LOG2)
            stat_ref[0, h, chunk, j : j + 1, :] = most * TO_LOG2
            stat_ref[1, h, chunk, j : j + 1, :] = jnp.sum(total * weight, axis=0, keepdims=True)
            stat_ref[2, h, chunk, j : j + 1, :] = jnp.sum(dot * weight, axis=0, keepdims=True)


def prefix_kernel(mine_ref, others_ref, pref_ref, slot_ref, stat_ref, full_ref, out_ref):
    count, _, each, _ = pref_ref.shape
    found, heads = units(mine_ref, others_ref)
    slots = count * each // PLEN
    grads = {}
    for h, chunk, read in found:
        columns = slice(h * HD, (h + 1) * HD)
        keys, values = (
            jnp.concatenate(
                [pref_ref[part, which, :, columns].astype(F32) for part in range(count)], axis=0
            ).astype(BF16)
            for which in range(2)
        )
        q, g = read(0, 0, heads), read(1, 0, heads)
        slot = jnp.concatenate([slot_ref[chunk]] * heads, axis=1)
        s_all = lax.dot_general(keys, q, NT, preferred_element_type=F32)
        dp_all = lax.dot_general(values, g, NT, preferred_element_type=F32)
        s, dp = s_all[:PLEN], dp_all[:PLEN]
        for k in range(1, slots):
            rows = slice(k * PLEN, (k + 1) * PLEN)
            s = jnp.where(slot == k, s_all[rows], s)
            dp = jnp.where(slot == k, dp_all[rows], dp)
        top = joined(stat_ref, 0, h, chunk)
        new = jnp.maximum(top, jnp.max(s, axis=0, keepdims=True) * TO_LOG2)
        e = jnp.exp2(s * TO_LOG2 - new)
        old = jnp.exp2(top - new)
        total = old * joined(stat_ref, 1, h, chunk) + jnp.sum(e, axis=0, keepdims=True)
        dot = old * joined(stat_ref, 2, h, chunk) + jnp.sum(e * dp, axis=0, keepdims=True)
        inverse = 1.0 / total
        delta = dot * inverse
        p = e * inverse
        ds = p * (dp - delta)
        split(full_ref, 0, h, chunk, new + jnp.log2(total))
        split(full_ref, 1, h, chunk, delta)
        zero = jnp.zeros_like(p)

        def spread(x, slot=slot, zero=zero):
            return jnp.concatenate(
                [jnp.where(slot == k, x, zero).astype(BF16) for k in range(slots)], axis=0
            )

        grads[chunk] = (
            lax.dot_general(spread(ds), q, NN, preferred_element_type=F32),
            lax.dot_general(spread(p), g, NN, preferred_element_type=F32),
        )
        if chunk:
            dk, dv = (grads[0][0] + grads[1][0]) * SCALE, grads[0][1] + grads[1][1]
            for which, grad in enumerate((dk, dv)):
                for part in range(count):
                    rows = grad[part * each : (part + 1) * each]
                    out_ref[part, which, :, columns] = rows.astype(BF16)


def token_grads_kernel(core_ref, mine_ref, others_ref, *refs):
    window, (bias_ref, full_ref, home_ref, one_ref, two_ref) = refs[:4], refs[4:]
    core = core_ref[0]
    even = core == 0
    toks = mine_ref.shape[1]
    found, heads = units(mine_ref, others_ref)
    grads = {}
    for h, chunk, read in found:
        keys, values = (windows(core, h, which, *window)[chunk] for which in range(2))
        q, g = read(0, 0, heads), read(1, 0, heads)
        bias = jnp.concatenate([bias_ref[chunk]] * heads, axis=1)
        s = lax.dot_general(keys, q, NT, preferred_element_type=F32) + bias
        dp = lax.dot_general(values, g, NT, preferred_element_type=F32)
        p = jnp.exp2(s * TO_LOG2 - joined(full_ref, 0, h, chunk))
        ds = (p * (dp - joined(full_ref, 1, h, chunk))).astype(BF16)
        dk = lax.dot_general(ds, q, NN, preferred_element_type=F32) * SCALE
        dv = lax.dot_general(p.astype(BF16), g, NN, preferred_element_type=F32)
        grads[chunk] = (dk, dv)
        if not chunk:
            continue
        columns = slice(h * HD, (h + 1) * HD)
        for which in range(2):
            a, b = (
                [grads[c][which][n * toks : (n + 1) * toks] for n in range(5)] for c in range(2)
            )
            zero = jnp.zeros_like(a[4])
            home_ref[which, :toks, columns] = a[0] + jnp.where(even, b[4], zero)
            home_ref[which, toks:, columns] = b[0] + jnp.where(even, zero, a[4])
            one_ref[which, :toks, columns] = (a[1] + b[1]).astype(BF16)
            one_ref[which, toks:, columns] = (a[3] + b[2]).astype(BF16)
            two_ref[which, :toks, columns] = (a[2] + jnp.where(even, zero, b[4])).astype(BF16)
            two_ref[which, toks:, columns] = (b[3] + jnp.where(even, a[4], zero)).astype(BF16)


def call(kernel, flops, exps, ins, outs):
    space = pl.BlockSpec(memory_space=pltpu.VMEM)
    scalar = pl.BlockSpec(memory_space=pltpu.SMEM)
    return pl.pallas_call(
        kernel,
        in_specs=[scalar if x.ndim == 1 else space for x in ins],
        out_specs=[space] * len(outs),
        out_shape=outs,
        compiler_params=pltpu.CompilerParams(vmem_limit_bytes=VMEM_BYTES),
        cost_estimate=pl.CostEstimate(flops=flops, bytes_accessed=6 << 20, transcendentals=exps),
    )(*ins)


def layout(lengths, tenants, slots, block, shards, toks):
    ends = jnp.cumsum(lengths)
    slot_of = jnp.sum(
        jnp.where(tenants[:, None] == jnp.arange(slots.shape[0])[None, :], slots[None, :], 0), axis=1
    )
    here = block * toks + jnp.arange(toks, dtype=jnp.int32)
    doc = jnp.sum((here[None, :] >= ends[:, None]).astype(jnp.int32), axis=0)
    pick = doc[None, :] == jnp.arange(lengths.shape[0])[:, None]
    first = jnp.sum(jnp.where(pick, (ends - lengths)[:, None], 0), axis=0)
    slot = jnp.sum(jnp.where(pick, slot_of[:, None], 0), axis=0)
    key = jnp.concatenate([s * toks + jnp.arange(toks, dtype=jnp.int32) for s in shards])
    ok = (key[:, None] >= first[None, :]) & (key[:, None] <= here[None, :])
    return jnp.where(ok, 0.0, -1e30).astype(F32), slot[None, :].astype(jnp.int32)


def per_device(
    queries, keys, values, grad_out, prefix_keys, prefix_values, doc_lengths, doc_tenants, tenant_slots
):
    toks, width = queries.shape
    parts = lax.axis_size("z")
    count = parts * 2
    index, core = lax.axis_index(SEQ), lax.axis_index("core").astype(jnp.int32)
    even = core == 0
    cores = core[None]

    def shift(x, steps):
        pairs = [(i, i + 2 * steps) for i in range(count) if 0 <= i + 2 * steps < count]
        return lax.ppermute(x, SEQ, pairs)

    def swap(x):
        return lax.ppermute(x, SEQ, [(i, i ^ 1) for i in range(count)])

    def exchange(x, axis):
        return lax.all_to_all(x, axis, split_axis=0, concat_axis=0, tiled=True)

    def to_all(x, axis):
        return exchange(jnp.broadcast_to(x[None], (lax.axis_size(axis), *x.shape)), axis)

    def half(x, which):
        size = x.shape[-1] // 2
        return lax.dynamic_slice_in_dim(x, which * size, size, x.ndim - 1)

    def other_half(x):
        return half(x, 1 - core)

    own = jnp.stack([keys, values])
    one, two = shift(own, 1), shift(own, 2)
    pref = jnp.stack([prefix_keys, prefix_values])
    pref = pref.reshape(2, -1, 2, KVH * HD // 2).transpose(2, 0, 1, 3)
    pref = jnp.broadcast_to(pref[None], (parts, *pref.shape)).reshape(count, *pref.shape[1:])
    pref = exchange(pref, SEQ)
    others = swap(jnp.stack([other_half(queries), other_half(grad_out)]))
    cross = swap(jnp.stack([other_half(own), other_half(one), other_half(two)]))

    facing = index ^ 1
    near, far = jnp.where(even, index - 1, index - 3), jnp.where(even, index - 3, index - 1)
    docs = (doc_lengths[0], doc_tenants[0], tenant_slots)
    shards = [index, index - 2, index - 4, near, far]
    bias0, slot0 = layout(*docs, index, shards, toks)
    last = jnp.where(even, index, index - 4)
    shards = [facing, index - 2, facing - 2, facing - 4, last]
    bias1, slot1 = layout(*docs, facing, shards, toks)
    bias, slot = jnp.stack([bias0, bias1]), jnp.stack([slot0, slot1])

    heads = [jnp.stack([half(queries, core), half(grad_out, core)]), others]
    shape = (KVH // 2, 2, HQ // KVH, toks)
    work = queries.size // HD * bias.shape[1]
    window = [cores, *heads, own, one, two, cross, bias]
    (stats,) = call(
        token_stats_kernel,
        flops=4 * HD * work,
        exps=work,
        ins=window,
        outs=[jax.ShapeDtypeStruct((3, *shape), F32)],
    )
    prefs = queries.size // HD * count * pref.shape[2]
    full, rows = call(
        prefix_kernel,
        flops=8 * HD * prefs,
        exps=prefs // 6,
        ins=[*heads, pref, slot, stats],
        outs=[jax.ShapeDtypeStruct((2, *shape), F32), jax.ShapeDtypeStruct(pref.shape, BF16)],
    )
    wide = (2, 2 * toks, KVH * HD // 2)
    home, back1, back2 = call(
        token_grads_kernel,
        flops=8 * HD * work,
        exps=work,
        ins=window + [full],
        outs=[jax.ShapeDtypeStruct(wide, kind) for kind in (F32, BF16, BF16)],
    )

    rows = exchange(rows, SEQ).astype(F32)
    rows = rows.reshape(parts, 2, *rows.shape[1:])
    rows = jnp.concatenate([jnp.sum(rows[:, n], axis=0) for n in range(2)], axis=2)
    rows, home, back1, back2 = lax.optimization_barrier((rows.astype(BF16), home, back1, back2))
    rows = jnp.sum(to_all(rows, "x").astype(F32), axis=0)
    rows = to_all(rows.astype(BF16), "y").astype(F32)

    back1, back2 = shift(back1, -1), shift(back2, -2)
    grads = (home + back1.astype(F32) + back2.astype(F32)).astype(BF16)
    mine, theirs = grads[:, :toks], swap(grads[:, toks:])
    grads = jnp.concatenate(
        [jnp.where(even, mine, theirs), jnp.where(even, theirs, mine)], axis=2
    )
    return grads[0], grads[1], jnp.sum(rows[:, 0], axis=0), jnp.sum(rows[:, 1], axis=0)


def solution(mesh):
    mesh = Mesh(mesh.devices.reshape(8, 4, 8, 2), ("y", "x", "z", "core"))
    rows, dp, seq = P(("y", "x", "z", "core"), None), P(("y", "x"), None), P(SEQ, None)
    return jax.shard_map(
        per_device,
        mesh=mesh,
        in_specs=(rows, rows, rows, rows, seq, seq, dp, dp, P()),
        out_specs=(rows, rows, seq, seq),
        check_vma=False,
    )
```

time: 117 us -> 110 us (0.940)
  blocking collectives: 21.8 us -> 10.3 us
  local copies, waits for them, and re-layouts: 5.74 us -> 9.57 us
  Pallas kernels: 27.9 us -> 24.8 us
  waiting for transfers between devices: 12.7 us -> 14.6 us
  starting transfers between devices: 39.5 us -> 41.2 us
    all_to_all x1, blocking collectives: 21.8 us -> 10.3 us  [exchange(): return lax.all_to_all(x, axis, split_axis=0, concat_axis=0, tiled=True)]
    all_to_all x3, waiting for transfers between devices: 4.12 us -> 13.6 us  [exchange(): return lax.all_to_all(x, axis, split_axis=0, concat_axis=0, tiled=True)]
    ppermute x4, waiting for transfers between devices: 7.05 us -> 0.01 us  [shift(): return lax.ppermute(x, SEQ, pairs)]
    another operation x0 -> x3, local copies, waits for them, and re-layouts: none -> 3.33 us  [the longest x1 3.3 us: per_device(): others = swap(jnp.stack([other_half(queries), other_half(grad_out)]))]
    pallas_call x3, Pallas kernels: 27.9 us -> 24.8 us  [call(): pl.pallas_call(kernel, in_specs=[scalar if x.ndim == 1 else space for x i...]
    another operation x2 -> x1, other arithmetic: 3.3 us -> 1.29 us  [per_device(): others = swap(jnp.stack([other_half(queries), other_half(grad_out)]))]
    another operation x1 -> x2, other arithmetic: 0.18 us -> 1.7 us  [the longest x1 1.52 us: per_device(): heads = [jnp.stack([half(queries, core), half(grad_out, core)]), others]]
    all_to_all x3, starting transfers between devices: 18.5 us -> 20.1 us  [exchange(): return lax.all_to_all(x, axis, split_axis=0, concat_axis=0, tiled=True)]
  transfers between devices with their start and end apart: 10 -> 10, of which waited for: 5 -> 5; matrix products, arithmetic and copies ran while one was open for 7% -> 9% of each run, Pallas kernels for 17% -> 16%
where the time goes in v4:
time: 110 us; the launch traced here: 109 us
  starting transfers between devices  41.2 us (37%)
  Pallas kernels  24.8 us (23%)
  waiting for transfers between devices  14.6 us (13%)
  blocking collectives  10.3 us (9%)
  local copies, waits for them, and re-layouts  9.57 us (9%)
  other arithmetic  7.72 us (7%)
    pallas_call x3, Pallas kernels, call(): pl.pallas_call(kernel, in_specs=[scalar if x.ndim == 1 else space for x i...  24.8 us
    all_to_all x3, starting transfers between devices, exchange(): return lax.all_to_all(x, axis, split_axis=0, concat_axis=0, tiled=True)  20.1 us
    all_to_all x3, waiting for transfers between devices, exchange(): return lax.all_to_all(x, axis, split_axis=0, concat_axis=0, tiled=True)  13.6 us
    ppermute x4, starting transfers between devices, shift(): return lax.ppermute(x, SEQ, pairs)  13.2 us
    all_to_all x1, blocking collectives, exchange(): return lax.all_to_all(x, axis, split_axis=0, concat_axis=0, tiled=True)  10.3 us
    ppermute x3, starting transfers between devices, swap(): return lax.ppermute(x, SEQ, [(i, i ^ 1) for i in range(count)])  7.87 us
    unnamed x30, local copies, waits for them, and re-layouts  4.62 us
    another operation x1, local copies, waits for them, and re-layouts, per_device(): others = swap(jnp.stack([other_half(queries), other_half(grad_out)]))  3.3 us
  transfers between devices with their start and end apart: 10, of which 5 were waited for; matrix products, arithmetic and copies ran while one was open for 9% of the time, Pallas kernels for 16%

profile of v4, /device:TPU:1, one launch (start us, length us, event | category | flops | bytes accessed | tf_op | source)
XLA Modules:
  0.0 109.2 jit_solution(1410622891540630349)
XLA Ops:
  0.6 1.0 pad_maximum_fusion.4.refs_0_
  1.6 4.8 %collective-permute-start.1 = (bf16[2,128,512]{2,1,0:T(8,128)(2,1)S(1)}, bf16[2,128,512]{2,1,0:T(8,128)(2,1)S(1)}, u32[]{:S(2)}, u32[]{:S(2)}) collective-permute-start(bf16[2,128,512]{2,1,0:T(8,128)(2,1)S(1)} %pad_maximum_fusion.4.refs_0_), channel_id=1, source_target_pairs={{0,2},{1,3},{2,4},{3,5},{4,6},{5,7},{6,8},{7,9},{8,10},{9,11},{10,... | collective-permute-start | bytes 786440 | tf_op jit(solution)/shard_map/ppermute | solution.py:232
  6.5 5.8 %collective-permute-start.2 = (bf16[2,128,512]{2,1,0:T(8,128)(2,1)S(1)}, bf16[2,128,512]{2,1,0:T(8,128)(2,1)S(1)}, u32[]{:S(2)}, u32[]{:S(2)}) collective-permute-start(bf16[2,128,512]{2,1,0:T(8,128)(2,1)S(1)} %pad_maximum_fusion.4.refs_0_), channel_id=1, source_target_pairs={{0,4},{1,5},{2,6},{3,7},{4,8},{5,9},{6,10},{7,11},{8,12},{9,13},{1... | collective-permute-start | bytes 786440 | tf_op jit(solution)/shard_map/ppermute | solution.py:232
  12.3 3.3 %dynamic-slice_bitcast_fusion = (bf16[1,128,3072]{2,1,0:T(8,128)(2,1)S(1)}, bf16[1,128,3072]{2,1,0:T(8,128)(2,1)}, bf16[1,128,3072]{2,1,0:T(8,128)(2,1)}, bf16[1,128,3072]{2,1,0:T(8,128)(2,1)S(1)}) fusion(bf16[128,6144]{1,0:T(8,128)(2,1)} %param.12, s32[]{:T(128)S(6)} %select_n.76, s32[]{:T(128)S(6)} %select_n.75, bf16[128,6144]{1,0:T(8,128)(2,1)} %param.9), kind=kLoop, calls=%fused_computation.2 | loop fusion | bytes 6291464 | tf_op jit(solution)/shard_map/stack | solution.py:256
  15.6 0.0 copy-start.10
  15.6 0.0 copy-start.11
  15.6 0.0 copy-start.12
  15.6 1.3 %pad_maximum_fusion.1 = bf16[2,128,3072]{2,1,0:T(8,128)(2,1)} fusion(bf16[1,128,3072]{2,1,0:T(8,128)(2,1)S(1)} %get-tuple-element.34, bf16[1,128,3072]{2,1,0:T(8,128)(2,1)S(1)} %get-tuple-element.41), kind=kLoop, calls=%fused_computation.1 | loop fusion | flops 786432 | bytes 3145728 | tf_op jit(solution)/shard_map/stack | solution.py:256
  16.9 0.0 copy-start.13
  16.9 0.0 copy-start.14
  16.9 0.0 copy-start.8
  16.9 3.3 %collective-permute-start = (bf16[2,128,3072]{2,1,0:T(8,128)(2,1)}, bf16[2,128,3072]{2,1,0:T(8,128)(2,1)}, u32[]{:S(2)}, u32[]{:S(2)}) collective-permute-start(bf16[2,128,3072]{2,1,0:T(8,128)(2,1)} %pad_maximum_fusion.1), channel_id=1, source_target_pairs={{0,1},{1,0},{2,3},{3,2},{4,5},{5,4},{6,7},{7,6},{8,9},{9,8},{10,11... | collective-permute-start | bytes 4718600 | tf_op jit(solution)/shard_map/ppermute | solution.py:235
  20.2 0.0 copy-done.10
  20.2 0.0 copy-done.11
  20.3 0.1 maximum_bitcast_fusion
  20.3 0.8 broadcast_in_dim.97
  21.1 7.7 %all-to-all-start = ((bf16[16,2,24,256]{3,2,1,0:T(8,128)(2,1)}), bf16[16,2,24,256]{3,2,1,0:T(8,128)(2,1)S(1)}, u32[]{:S(2)}, u32[]{:S(2)}) async-start(bf16[16,2,24,256]{3,2,1,0:T(8,128)(2,1)} %bitcast.5), calls=%async_computation | async-start | bytes 786432 | tf_op jit(solution)/shard_map/all_to_all | solution.py:238
  28.9 0.0 copy-done.12
  28.9 0.2 reduce-window.7
  29.1 0.0 copy-done.13
  29.1 0.0 copy-done.14
  29.1 0.2 select_reduce_fusion.4
  29.4 0.1 convert_reduce_fusion.1
  29.5 0.1 select_reduce_fusion.1
  29.6 0.1 and_select_fusion
  29.7 0.2 and_select_fusion.1
  29.9 0.0 copy-done.8
  29.9 0.0 copy-done.9
  30.0 0.0 collective-permute-done.2.refs_2_
  30.0 0.0 collective-permute-done.1.refs_1_
  30.1 2.0 %collective-permute-start.3 = (bf16[3,2,128,256]{3,2,1,0:T(8,128)(2,1)S(1)}, bf16[3,2,128,256]{3,2,1,0:T(8,128)(2,1)S(1)}, u32[]{:S(2)}, u32[]{:S(2)}) collective-permute-start(bf16[3,2,128,256]{3,2,1,0:T(8,128)(2,1)S(1)} %pad_maximum_fusion.3), channel_id=1, source_target_pairs={{0,1},{1,0},{2,3},{3,2},{4,5},{5,4},{6,7},{7,6},{8,9},{9,8},{10,11... | collective-permute-start | bytes 1179656 | tf_op jit(solution)/shard_map/ppermute | solution.py:235
  32.2 1.5 %pad_maximum_fusion.mine_ref = bf16[2,128,3072]{2,1,0:T(8,128)(2,1)S(1)} fusion(bf16[1,128,3072]{2,1,0:T(8,128)(2,1)} %get-tuple-element.35, bf16[1,128,3072]{2,1,0:T(8,128)(2,1)} %get-tuple-element.40), kind=kLoop, calls=%fused_computation | loop fusion | flops 786432 | bytes 3145728 | tf_op jit(solution)/shard_map/stack | solution.py:269
  33.7 0.1 collective-permute-done.3.refs_3_
  33.7 0.0 collective-permute-done.others_ref
  33.7 7.2 %shard_map.120.stat_ref = f32[3,2,2,12,128]{4,3,2,1,0:T(8,128)S(1)} custom-call(s32[1]{0:T(128)} %bitcast.11.core_ref, bf16[2,128,3072]{2,1,0:T(8,128)(2,1)S(1)} %pad_maximum_fusion.mine_ref, bf16[2,128,3072]{2,1,0:T(8,128)(2,1)} %collective-permute-done.others_ref, bf16[2,128,512]{2,1,0:T(8,128)(2,1)S(1)} %pad_maximum_fusion.4.refs_0_, ...), custom_call_target="tpu_custom_call" | custom-call | flops 2013265920 | bytes 6291456 | tf_op jit(solution)/shard_map/pallas_call | solution.py:195
  41.0 0.7 copy-done
  41.7 1.7 %all-to-all-done.pref_ref = bf16[16,2,24,256]{3,2,1,0:T(8,128)(2,1)S(1)} async-done(((bf16[16,2,24,256]{3,2,1,0:T(8,128)(2,1)}), bf16[16,2,24,256]{3,2,1,0:T(8,128)(2,1)S(1)}, u32[]{:S(2)}, u32[]{:S(2)}) %all-to-all-start) | async-done | bytes 393248 | tf_op jit(solution)/shard_map/all_to_all | solution.py:238
  43.4 7.3 %shard_map.121 = (f32[2,2,2,12,128]{4,3,2,1,0:T(8,128)S(1)}, bf16[16,2,24,256]{3,2,1,0:T(8,128)(2,1)}) custom-call(bf16[2,128,3072]{2,1,0:T(8,128)(2,1)S(1)} %pad_maximum_fusion.mine_ref, bf16[2,128,3072]{2,1,0:T(8,128)(2,1)} %collective-permute-done.others_ref, bf16[16,2,24,256]{3,2,1,0:T(8,128)(2,1)S(1)} %all-to-all-done.pref_ref, ...), custom_call_target="tpu_custom_call" | custom-call | flops 2415919104 | bytes 6291456 | tf_op jit(solution)/shard_map/pallas_call | solution.py:195
  50.7 0.6 copy-done.6
  51.3 5.5 %all-to-all-start.1 = ((bf16[16,2,24,256]{3,2,1,0:T(8,128)(2,1)}), bf16[16,2,24,256]{3,2,1,0:T(8,128)(2,1)}, u32[]{:S(2)}, u32[]{:S(2)}) async-start(bf16[16,2,24,256]{3,2,1,0:T(8,128)(2,1)} %get-tuple-element.13), calls=%async_computation.1 | async-start | bytes 786432 | tf_op jit(solution)/shard_map/all_to_all | solution.py:238
  56.9 1.0 copy-done.1
  57.9 0.8 copy-done.7
  58.7 10.2 %shard_map.122 = (f32[2,256,256]{2,1,0:T(8,128)S(1)}, bf16[2,256,256]{2,1,0:T(8,128)(2,1)S(1)}, bf16[2,256,256]{2,1,0:T(8,128)(2,1)S(1)}) custom-call(s32[1]{0:T(128)} %bitcast.11.core_ref, bf16[2,128,3072]{2,1,0:T(8,128)(2,1)S(1)} %pad_maximum_fusion.mine_ref, bf16[2,128,3072]{2,1,0:T(8,128)(2,1)} %collective-permute-done.others_ref, ...), custom_call_target="tpu_custom_call" | custom-call | flops 4026531840 | bytes 6291456 | tf_op jit(solution)/shard_map/pallas_call | solution.py:195
  68.9 0.0 copy-start.2
  69.0 0.7 copy-done.2
  69.6 0.7 copy-done.4
  70.3 1.2 %all-to-all-done.1 = bf16[16,2,24,256]{3,2,1,0:T(8,128)(2,1)} async-done(((bf16[16,2,24,256]{3,2,1,0:T(8,128)(2,1)}), bf16[16,2,24,256]{3,2,1,0:T(8,128)(2,1)}, u32[]{:S(2)}, u32[]{:S(2)}) %all-to-all-start.1) | async-done | bytes 393248 | tf_op jit(solution)/shard_map/all_to_all | solution.py:238
  71.5 1.1 %bitcast_convert_fusion = f32[8,2,2,24,256]{4,3,2,1,0:T(8,128)S(1)} fusion(bf16[16,2,24,256]{3,2,1,0:T(8,128)(2,1)} %all-to-all-done.1), kind=kLoop, calls=%fused_computation.57 | loop fusion | flops 196608 | bytes 1179648 | tf_op jit(solution)/shard_map/reshape | solution.py:298
  72.7 0.0 copy-done.5
  72.7 1.3 %collective-permute-start.5 = (bf16[2,256,256]{2,1,0:T(8,128)(2,1)S(1)}, bf16[2,256,256]{2,1,0:T(8,128)(2,1)S(1)}, u32[]{:S(2)}, u32[]{:S(2)}) collective-permute-start(bf16[2,256,256]{2,1,0:T(8,128)(2,1)S(1)} %copy-done.5), channel_id=1, source_target_pairs={{4,0},{5,1},{6,2},{7,3},{8,4},{9,5},{10,6},{11,7},{12,8},{13,9},{1... | collective-permute-start | bytes 786440 | tf_op jit(solution)/shard_map/ppermute | solution.py:232
  74.0 0.0 copy-done.3
  74.0 1.3 %collective-permute-start.4 = (bf16[2,256,256]{2,1,0:T(8,128)(2,1)S(1)}, bf16[2,256,256]{2,1,0:T(8,128)(2,1)S(1)}, u32[]{:S(2)}, u32[]{:S(2)}) collective-permute-start(bf16[2,256,256]{2,1,0:T(8,128)(2,1)S(1)} %copy-done.3), channel_id=1, source_target_pairs={{2,0},{3,1},{4,2},{5,3},{6,4},{7,5},{8,6},{9,7},{10,8},{11,9},{12,... | collective-permute-start | bytes 786440 | tf_op jit(solution)/shard_map/ppermute | solution.py:232
  75.4 10.3 %all_to_all.20 = bf16[4,2,24,512]{3,2,1,0:T(8,128)(2,1)S(1)} all-to-all(bf16[4,2,24,512]{3,2,1,0:T(8,128)(2,1)S(1)} %broadcast_in_dim.106), channel_id=1, replica_groups=mesh['y'=8,'x'=4,'z'=8,'core'=2] {'x'}, dimensions={0} | all-to-all | bytes 393216 | tf_op jit(solution)/shard_map/all_to_all | solution.py:238
  85.7 0.8 broadcast_in_dim.107
  86.5 6.8 %all-to-all-start.3 = ((bf16[8,2,24,512]{3,2,1,0:T(8,128)(2,1)}), bf16[8,2,24,512]{3,2,1,0:T(8,128)(2,1)S(1)}, u32[]{:S(2)}, u32[]{:S(2)}) async-start(bf16[8,2,24,512]{3,2,1,0:T(8,128)(2,1)} %broadcast_in_dim.107), calls=%async_computation.3 | async-start | bytes 786432 | tf_op jit(solution)/shard_map/all_to_all | solution.py:238
  93.3 0.0 collective-permute-done.5
  93.3 0.0 collective-permute-done.4
  93.3 0.1 add_convert_fusion
  93.4 2.6 %collective-permute-start.6 = (bf16[2,128,256]{2,1,0:T(8,128)(2,1)S(1)}, bf16[2,128,256]{2,1,0:T(8,128)(2,1)S(1)}, u32[]{:S(2)}, u32[]{:S(2)}) collective-permute-start(bf16[2,128,256]{2,1,0:T(8,128)(2,1)S(1)} %slice.35), channel_id=1, source_target_pairs={{0,1},{1,0},{2,3},{3,2},{4,5},{5,4},{6,7},{7,6},{8,9},{9,8},{10,11... | collective-permute-start | bytes 393224 | tf_op jit(solution)/shard_map/ppermute | solution.py:235
  96.0 1.0 collective-permute-done.6
  97.0 0.7 fusion.4
  97.7 10.7 %all-to-all-done.3 = bf16[8,2,24,512]{3,2,1,0:T(8,128)(2,1)S(1)} async-done(((bf16[8,2,24,512]{3,2,1,0:T(8,128)(2,1)}), bf16[8,2,24,512]{3,2,1,0:T(8,128)(2,1)S(1)}, u32[]{:S(2)}, u32[]{:S(2)}) %all-to-all-start.3) | async-done | bytes 393248 | tf_op jit(solution)/shard_map/all_to_all | solution.py:238
  108.4 0.1 convert_element_type.27
  108.5 0.7 slice_reduce_fusion
  (36 shorter events, 0.4 us)
Async XLA Ops:
  1.6 28.4 %collective-permute-start.1 = (bf16[2,128,512]{2,1,0:T(8,128)(2,1)S(1)}, bf16[2,128,512]{2,1,0:T(8,128)(2,1)S(1)}, u32[]{:S(2)}, u32[]{:S(2)}) collective-permute-start(bf16[2,128,512]{2,1,0:T(8,128)(2,1)S(1)} %pad_maximum_fusion.4.refs_0_), channel_id=1, source_target_pairs={{0,2},{1,3},{2,4},{3,5},{4,6},{5,7},{6,8},{7,9},{8,10},{9,11},{10,... | collective-permute-start | bytes 786440 | tf_op jit(solution)/shard_map/ppermute | solution.py:232
  6.5 23.5 %collective-permute-start.2 = (bf16[2,128,512]{2,1,0:T(8,128)(2,1)S(1)}, bf16[2,128,512]{2,1,0:T(8,128)(2,1)S(1)}, u32[]{:S(2)}, u32[]{:S(2)}) collective-permute-start(bf16[2,128,512]{2,1,0:T(8,128)(2,1)S(1)} %pad_maximum_fusion.4.refs_0_), channel_id=1, source_target_pairs={{0,4},{1,5},{2,6},{3,7},{4,8},{5,9},{6,10},{7,11},{8,12},{9,13},{1... | collective-permute-start | bytes 786440 | tf_op jit(solution)/shard_map/ppermute | solution.py:232
  15.6 4.6 %copy-start.10 = (bf16[24,512]{1,0:T(8,128)(2,1)S(1)}, bf16[24,512]{1,0:T(8,128)(2,1)}, u32[]{:S(2)}) copy-start(bf16[24,512]{1,0:T(8,128)(2,1)} %param.14) | copy-start | bytes 73732
  15.6 4.6 %copy-start.11 = (bf16[24,512]{1,0:T(8,128)(2,1)S(1)}, bf16[24,512]{1,0:T(8,128)(2,1)}, u32[]{:S(2)}) copy-start(bf16[24,512]{1,0:T(8,128)(2,1)} %param.13) | copy-start | bytes 73732
  15.6 13.3 %copy-start.12 = (s32[1,8]{1,0:T(1,128)S(1)}, s32[1,8]{1,0:T(1,128)}, u32[]{:S(2)}) copy-start(s32[1,8]{1,0:T(1,128)} %param.15) | copy-start | bytes 100
  16.9 12.2 %copy-start.13 = (s32[6]{0:T(128)S(1)}, s32[6]{0:T(128)}, u32[]{:S(2)}) copy-start(s32[6]{0:T(128)} %param.17) | copy-start | bytes 76
  16.9 12.2 %copy-start.14 = (s32[1,8]{1,0:T(1,128)S(1)}, s32[1,8]{1,0:T(1,128)}, u32[]{:S(2)}) copy-start(s32[1,8]{1,0:T(1,128)} %param.16) | copy-start | bytes 100
  16.9 13.0 %copy-start.8 = (bf16[128,512]{1,0:T(8,128)(2,1)S(1)}, bf16[128,512]{1,0:T(8,128)(2,1)}, u32[]{:S(2)}) copy-start(bf16[128,512]{1,0:T(8,128)(2,1)} %param.11) | copy-start | bytes 393220
  16.9 13.0 %copy-start.9 = (bf16[128,512]{1,0:T(8,128)(2,1)S(1)}, bf16[128,512]{1,0:T(8,128)(2,1)}, u32[]{:S(2)}) copy-start(bf16[128,512]{1,0:T(8,128)(2,1)} %param.10) | copy-start | bytes 393220
  16.9 16.8 %collective-permute-start = (bf16[2,128,3072]{2,1,0:T(8,128)(2,1)}, bf16[2,128,3072]{2,1,0:T(8,128)(2,1)}, u32[]{:S(2)}, u32[]{:S(2)}) collective-permute-start(bf16[2,128,3072]{2,1,0:T(8,128)(2,1)} %pad_maximum_fusion.1), channel_id=1, source_target_pairs={{0,1},{1,0},{2,3},{3,2},{4,5},{5,4},{6,7},{7,6},{8,9},{9,8},{10,11... | collective-permute-start | bytes 4718600 | tf_op jit(solution)/shard_map/ppermute | solution.py:235
  21.1 22.3 %all-to-all-start = ((bf16[16,2,24,256]{3,2,1,0:T(8,128)(2,1)}), bf16[16,2,24,256]{3,2,1,0:T(8,128)(2,1)S(1)}, u32[]{:S(2)}, u32[]{:S(2)}) async-start(bf16[16,2,24,256]{3,2,1,0:T(8,128)(2,1)} %bitcast.5), calls=%async_computation | async-start | bytes 786432 | tf_op jit(solution)/shard_map/all_to_all | solution.py:238
  30.1 3.6 %collective-permute-start.3 = (bf16[3,2,128,256]{3,2,1,0:T(8,128)(2,1)S(1)}, bf16[3,2,128,256]{3,2,1,0:T(8,128)(2,1)S(1)}, u32[]{:S(2)}, u32[]{:S(2)}) collective-permute-start(bf16[3,2,128,256]{3,2,1,0:T(8,128)(2,1)S(1)} %pad_maximum_fusion.3), channel_id=1, source_target_pairs={{0,1},{1,0},{2,3},{3,2},{4,5},{5,4},{6,7},{7,6},{8,9},{9,8},{10,11... | collective-permute-start | bytes 1179656 | tf_op jit(solution)/shard_map/ppermute | solution.py:235
  41.0 0.8 copy-start
  50.7 0.6 copy-start.6
  51.3 20.2 %all-to-all-start.1 = ((bf16[16,2,24,256]{3,2,1,0:T(8,128)(2,1)}), bf16[16,2,24,256]{3,2,1,0:T(8,128)(2,1)}, u32[]{:S(2)}, u32[]{:S(2)}) async-start(bf16[16,2,24,256]{3,2,1,0:T(8,128)(2,1)} %get-tuple-element.13), calls=%async_computation.1 | async-start | bytes 786432 | tf_op jit(solution)/shard_map/all_to_all | solution.py:238
  56.9 1.0 copy-start.1
  57.9 0.8 copy-start.7
  68.9 0.7 copy-start.2
  69.6 0.7 copy-start.4
  71.5 1.2 %copy-start.5 = (bf16[2,256,256]{2,1,0:T(8,128)(2,1)S(1)}, bf16[2,256,256]{2,1,0:T(8,128)(2,1)}, u32[]{:S(2)}) copy-start(bf16[2,256,256]{2,1,0:T(8,128)(2,1)} %copy-done.4) | copy-start | bytes 786436
  71.5 2.5 %copy-start.3 = (bf16[2,256,256]{2,1,0:T(8,128)(2,1)S(1)}, bf16[2,256,256]{2,1,0:T(8,128)(2,1)}, u32[]{:S(2)}) copy-start(bf16[2,256,256]{2,1,0:T(8,128)(2,1)} %copy-done.2) | copy-start | bytes 786436
  72.7 20.5 %collective-permute-start.5 = (bf16[2,256,256]{2,1,0:T(8,128)(2,1)S(1)}, bf16[2,256,256]{2,1,0:T(8,128)(2,1)S(1)}, u32[]{:S(2)}, u32[]{:S(2)}) collective-permute-start(bf16[2,256,256]{2,1,0:T(8,128)(2,1)S(1)} %copy-done.5), channel_id=1, source_target_pairs={{4,0},{5,1},{6,2},{7,3},{8,4},{9,5},{10,6},{11,7},{12,8},{13,9},{1... | collective-permute-start | bytes 786440 | tf_op jit(solution)/shard_map/ppermute | solution.py:232
  74.0 19.2 %collective-permute-start.4 = (bf16[2,256,256]{2,1,0:T(8,128)(2,1)S(1)}, bf16[2,256,256]{2,1,0:T(8,128)(2,1)S(1)}, u32[]{:S(2)}, u32[]{:S(2)}) collective-permute-start(bf16[2,256,256]{2,1,0:T(8,128)(2,1)S(1)} %copy-done.3), channel_id=1, source_target_pairs={{2,0},{3,1},{4,2},{5,3},{6,4},{7,5},{8,6},{9,7},{10,8},{11,9},{12,... | collective-permute-start | bytes 786440 | tf_op jit(solution)/shard_map/ppermute | solution.py:232
  86.5 22.0 %all-to-all-start.3 = ((bf16[8,2,24,512]{3,2,1,0:T(8,128)(2,1)}), bf16[8,2,24,512]{3,2,1,0:T(8,128)(2,1)S(1)}, u32[]{:S(2)}, u32[]{:S(2)}) async-start(bf16[8,2,24,512]{3,2,1,0:T(8,128)(2,1)} %broadcast_in_dim.107), calls=%async_computation.3 | async-start | bytes 786432 | tf_op jit(solution)/shard_map/all_to_all | solution.py:238
  93.4 3.6 %collective-permute-start.6 = (bf16[2,128,256]{2,1,0:T(8,128)(2,1)S(1)}, bf16[2,128,256]{2,1,0:T(8,128)(2,1)S(1)}, u32[]{:S(2)}, u32[]{:S(2)}) collective-permute-start(bf16[2,128,256]{2,1,0:T(8,128)(2,1)S(1)} %slice.35), channel_id=1, source_target_pairs={{0,1},{1,0},{2,3},{3,2},{4,5},{5,4},{6,7},{7,6},{8,9},{9,8},{10,11... | collective-permute-start | bytes 393224 | tf_op jit(solution)/shard_map/ppermute | solution.py:235

commit v5 on v4

--- a/solution.py
+++ b/solution.py
@@ -14,6 +14,7 @@
 NT = (((1,), (1,)), ((), ()))
 NN = (((1,), (0,)), ((), ()))
 SEQ = ("z", "core")
+DP = ("y", "x")
 SCALE = 1.0 / math.sqrt(HD)
 TO_LOG2 = SCALE * math.log2(math.e)
 F32 = jnp.float32
@@ -108,13 +109,14 @@
     slots = count * each // PLEN
     grads = {}
     for h, chunk, read in found:
-        columns = slice(h * HD, (h + 1) * HD)
-        keys, values = (
-            jnp.concatenate(
-                [pref_ref[part, which, :, columns].astype(F32) for part in range(count)], axis=0
-            ).astype(BF16)
-            for which in range(2)
-        )
+        if not chunk:
+            columns = slice(h * HD, (h + 1) * HD)
+            keys, values = (
+                jnp.concatenate(
+                    [pref_ref[part, which, :, columns].astype(F32) for part in range(count)], axis=0
+                ).astype(BF16)
+                for which in range(2)
+            )
         q, g = read(0, 0, heads), read(1, 0, heads)
         slot = jnp.concatenate([slot_ref[chunk]] * heads, axis=1)
         s_all = lax.dot_general(keys, q, NT, preferred_element_type=F32)
@@ -152,7 +154,7 @@
             for which, grad in enumerate((dk, dv)):
                 for part in range(count):
                     rows = grad[part * each : (part + 1) * each]
-                    out_ref[part, which, :, columns] = rows.astype(BF16)
+                    out_ref[2 * which + h, part] = rows.astype(BF16)
 
 
 def token_grads_kernel(core_ref, mine_ref, others_ref, *refs):
@@ -189,6 +191,57 @@
             two_ref[which, toks:, columns] = (b[3] + jnp.where(even, a[4], zero)).astype(BF16)
 
 
+def halves_kernel(core_ref, q_ref, g_ref, mine_ref, theirs_ref, sems):
+    width = mine_ref.shape[2]
+    copies = []
+    for which, ref in enumerate((q_ref, g_ref)):
+        for n, (out, side) in enumerate(((theirs_ref, 1 - core_ref[0]), (mine_ref, core_ref[0]))):
+            columns = pl.ds(pl.multiple_of(side * width, HD), width)
+            copies.append(
+                pltpu.make_async_copy(ref.at[:, columns], out.at[which], sems.at[which, n])
+            )
+    for copy in copies:
+        copy.start()
+    for copy in copies:
+        copy.wait()
+
+
+def halves(cores, q, g):
+    half = jax.ShapeDtypeStruct((2, q.shape[0], q.shape[1] // 2), q.dtype)
+    anywhere = pl.BlockSpec(memory_space=pl.ANY)
+    return pl.pallas_call(
+        halves_kernel,
+        in_specs=[pl.BlockSpec(memory_space=pltpu.SMEM), anywhere, anywhere],
+        out_specs=[pl.BlockSpec(memory_space=pltpu.VMEM), anywhere],
+        out_shape=[half, half],
+        scratch_shapes=[pltpu.SemaphoreType.DMA((2, 2))],
+        cost_estimate=pl.CostEstimate(flops=0, bytes_accessed=4 * q.size * 2, transcendentals=0),
+    )(cores, q, g)
+
+
+def spread_kernel(got_ref, out_ref):
+    count, cores = out_ref.shape[:2]
+    for c in range(cores):
+        total = got_ref[c].astype(F32)
+        for n in range(c + cores, got_ref.shape[0], cores):
+            total = total + got_ref[n].astype(F32)
+        total = total.astype(BF16)
+        for n in range(count):
+            out_ref[n, c] = total
+
+
+def finish_kernel(got_ref, keys_ref, values_ref):
+    heads, cores = got_ref.shape[2:4]
+    for which, out_ref in enumerate((keys_ref, values_ref)):
+        for h in range(heads):
+            for c in range(cores):
+                total = got_ref[0, which, h, c].astype(F32)
+                for y in range(1, got_ref.shape[0]):
+                    total = total + got_ref[y, which, h, c].astype(F32)
+                at = (c * heads + h) * HD
+                out_ref[:, at : at + HD] = total
+
+
 def call(kernel, flops, exps, ins, outs):
     space = pl.BlockSpec(memory_space=pltpu.VMEM)
     scalar = pl.BlockSpec(memory_space=pltpu.SMEM)
@@ -237,15 +290,9 @@
     def exchange(x, axis):
         return lax.all_to_all(x, axis, split_axis=0, concat_axis=0, tiled=True)
 
-    def to_all(x, axis):
-        return exchange(jnp.broadcast_to(x[None], (lax.axis_size(axis), *x.shape)), axis)
-
-    def half(x, which):
+    def other_half(x):
         size = x.shape[-1] // 2
-        return lax.dynamic_slice_in_dim(x, which * size, size, x.ndim - 1)
-
-    def other_half(x):
-        return half(x, 1 - core)
+        return lax.dynamic_slice_in_dim(x, (1 - core) * size, size, x.ndim - 1)
 
     own = jnp.stack([keys, values])
     one, two = shift(own, 1), shift(own, 2)
@@ -253,7 +300,8 @@
     pref = pref.reshape(2, -1, 2, KVH * HD // 2).transpose(2, 0, 1, 3)
     pref = jnp.broadcast_to(pref[None], (parts, *pref.shape)).reshape(count, *pref.shape[1:])
     pref = exchange(pref, SEQ)
-    others = swap(jnp.stack([other_half(queries), other_half(grad_out)]))
+    mine, theirs = halves(cores, queries, grad_out)
+    others = swap(theirs)
     cross = swap(jnp.stack([other_half(own), other_half(one), other_half(two)]))
 
     facing = index ^ 1
@@ -266,7 +314,7 @@
     bias1, slot1 = layout(*docs, facing, shards, toks)
     bias, slot = jnp.stack([bias0, bias1]), jnp.stack([slot0, slot1])
 
-    heads = [jnp.stack([half(queries, core), half(grad_out, core)]), others]
+    heads = [mine, others]
     shape = (KVH // 2, 2, HQ // KVH, toks)
     work = queries.size // HD * bias.shape[1]
     window = [cores, *heads, own, one, two, cross, bias]
@@ -283,7 +331,10 @@
         flops=8 * HD * prefs,
         exps=prefs // 6,
         ins=[*heads, pref, slot, stats],
-        outs=[jax.ShapeDtypeStruct((2, *shape), F32), jax.ShapeDtypeStruct(pref.shape, BF16)],
+        outs=[
+            jax.ShapeDtypeStruct((2, *shape), F32),
+            jax.ShapeDtypeStruct((KVH, count, pref.shape[2], HD), BF16),
+        ],
     )
     wide = (2, 2 * toks, KVH * HD // 2)
     home, back1, back2 = call(
@@ -294,12 +345,15 @@
         outs=[jax.ShapeDtypeStruct(wide, kind) for kind in (F32, BF16, BF16)],
     )
 
-    rows = exchange(rows, SEQ).astype(F32)
-    rows = rows.reshape(parts, 2, *rows.shape[1:])
-    rows = jnp.concatenate([jnp.sum(rows[:, n], axis=0) for n in range(2)], axis=2)
-    rows, home, back1, back2 = lax.optimization_barrier((rows.astype(BF16), home, back1, back2))
-    rows = jnp.sum(to_all(rows, "x").astype(F32), axis=0)
-    rows = to_all(rows.astype(BF16), "y").astype(F32)
+    rows = exchange(rows.reshape(-1, *rows.shape[2:]), ("x", *SEQ))
+    spread = jax.ShapeDtypeStruct((lax.axis_size(DP), 2, *rows.shape[1:]), BF16)
+    (rows,) = call(spread_kernel, flops=rows.size, exps=0, ins=[rows], outs=[spread])
+    rows, home, _, _ = lax.optimization_barrier((rows, home, back1, back2))
+    rows = exchange(rows, DP).reshape(lax.axis_size("y"), 2, 2, *rows.shape[1:])
+    full = jax.ShapeDtypeStruct((prefix_keys.shape[0], KVH * HD), F32)
+    pref_key_grads, pref_value_grads = call(
+        finish_kernel, flops=rows.size, exps=0, ins=[rows], outs=[full, full]
+    )
 
     back1, back2 = shift(back1, -1), shift(back2, -2)
     grads = (home + back1.astype(F32) + back2.astype(F32)).astype(BF16)
@@ -307,12 +361,12 @@
     grads = jnp.concatenate(
         [jnp.where(even, mine, theirs), jnp.where(even, theirs, mine)], axis=2
     )
-    return grads[0], grads[1], jnp.sum(rows[:, 0], axis=0), jnp.sum(rows[:, 1], axis=0)
+    return grads[0], grads[1], pref_key_grads, pref_value_grads
 
 
 def solution(mesh):
     mesh = Mesh(mesh.devices.reshape(8, 4, 8, 2), ("y", "x", "z", "core"))
-    rows, dp, seq = P(("y", "x", "z", "core"), None), P(("y", "x"), None), P(SEQ, None)
+    rows, dp, seq = P(("y", "x", "z", "core"), None), P(DP, None), P(SEQ, None)
     return jax.shard_map(
         per_device,
         mesh=mesh,

time: 110 us -> 147 us (1.34)
  Pallas kernels: 24.8 us -> 76.5 us
  blocking collectives: 10.3 us -> 0 us
  starting transfers between devices: 41.2 us -> 48 us
  local copies, waits for them, and re-layouts: 9.57 us -> 3.73 us
  other arithmetic: 7.72 us -> 2.91 us
  waiting for transfers between devices: 14.6 us -> 12.9 us
    pallas_call x0 -> x1, Pallas kernels: none -> 49.9 us  [halves(): pl.pallas_call(halves_kernel, in_specs=[pl.BlockSpec(memory_space=pltpu.S...]
    all_to_all x1 -> x0, blocking collectives: 10.3 us -> none  [exchange(): return lax.all_to_all(x, axis, split_axis=0, concat_axis=0, tiled=True)]
    all_to_all x3, waiting for transfers between devices: 13.6 us -> 8.08 us  [exchange(): return lax.all_to_all(x, axis, split_axis=0, concat_axis=0, tiled=True)]
    all_to_all x3, starting transfers between devices: 20.1 us -> 25.3 us  [exchange(): return lax.all_to_all(x, axis, split_axis=0, concat_axis=0, tiled=True)]
    another operation x1 -> x0, local copies, waits for them, and re-layouts: 3.3 us -> none  [per_device(): others = swap(jnp.stack([other_half(queries), other_half(grad_out)]))]
    another operation x3 -> x1, other arithmetic: 2.99 us -> 0.18 us  [the longest x1 1.52 us: per_device(): heads = [jnp.stack([half(queries, core), half(grad_out, core)]), others]]
    ppermute x4, waiting for transfers between devices: 0.01 us -> 2.51 us  [shift(): return lax.ppermute(x, SEQ, pairs)]
    pallas_call x3 -> x5, Pallas kernels: 24.8 us -> 26.5 us  [call(): pl.pallas_call(kernel, in_specs=[scalar if x.ndim == 1 else space for x i...]
  transfers between devices with their start and end apart: 10 -> 10, of which waited for: 5 -> 6; matrix products, arithmetic and copies ran while one was open for 9% -> 2% of each run, Pallas kernels for 16% -> 47%
where the time goes in v5:
time: 147 us; the launch traced here: 145 us
  Pallas kernels  76.5 us (52%)
  starting transfers between devices  48 us (33%)
  waiting for transfers between devices  12.9 us (9%)
  local copies, waits for them, and re-layouts  3.73 us (3%)
  other arithmetic  2.91 us (2%)
    pallas_call x1, Pallas kernels, halves(): pl.pallas_call(halves_kernel, in_specs=[pl.BlockSpec(memory_space=pltpu.S...  49.9 us
    pallas_call x5, Pallas kernels, call(): pl.pallas_call(kernel, in_specs=[scalar if x.ndim == 1 else space for x i...  26.5 us
    all_to_all x3, starting transfers between devices, exchange(): return lax.all_to_all(x, axis, split_axis=0, concat_axis=0, tiled=True)  25.3 us
    ppermute x4, starting transfers between devices, shift(): return lax.ppermute(x, SEQ, pairs)  13.2 us
    ppermute x3, starting transfers between devices, swap(): return lax.ppermute(x, SEQ, [(i, i ^ 1) for i in range(count)])  9.5 us
    all_to_all x3, waiting for transfers between devices, exchange(): return lax.all_to_all(x, axis, split_axis=0, concat_axis=0, tiled=True)  8.08 us
  transfers between devices with their start and end apart: 10, of which 6 were waited for; matrix products, arithmetic and copies ran while one was open for 2% of the time, Pallas kernels for 47%

profile of v5, /device:TPU:1, one launch (start us, length us, event | category | flops | bytes accessed | tf_op | source)
XLA Modules:
  0.0 145.1 jit_solution(6375068162079257774)
XLA Ops:
  0.6 1.0 pad_maximum_fusion.2.refs_0_
  1.6 4.8 %collective-permute-start.1 = (bf16[2,128,512]{2,1,0:T(8,128)(2,1)S(1)}, bf16[2,128,512]{2,1,0:T(8,128)(2,1)S(1)}, u32[]{:S(2)}, u32[]{:S(2)}) collective-permute-start(bf16[2,128,512]{2,1,0:T(8,128)(2,1)S(1)} %pad_maximum_fusion.2.refs_0_), channel_id=1, source_target_pairs={{0,2},{1,3},{2,4},{3,5},{4,6},{5,7},{6,8},{7,9},{8,10},{9,11},{10,... | collective-permute-start | bytes 786440 | tf_op jit(solution)/shard_map/ppermute | solution.py:285
  6.5 5.8 %collective-permute-start.2 = (bf16[2,128,512]{2,1,0:T(8,128)(2,1)S(1)}, bf16[2,128,512]{2,1,0:T(8,128)(2,1)S(1)}, u32[]{:S(2)}, u32[]{:S(2)}) collective-permute-start(bf16[2,128,512]{2,1,0:T(8,128)(2,1)S(1)} %pad_maximum_fusion.2.refs_0_), channel_id=1, source_target_pairs={{0,4},{1,5},{2,6},{3,7},{4,8},{5,9},{6,10},{7,11},{8,12},{9,13},{1... | collective-permute-start | bytes 786440 | tf_op jit(solution)/shard_map/ppermute | solution.py:285
  12.3 0.0 copy-start.5
  12.3 0.0 copy-start.6
  12.3 0.0 copy-start.7
  12.3 49.9 %shard_map.120 = (bf16[2,128,3072]{2,1,0:T(8,128)(2,1)}, bf16[2,128,3072]{2,1,0:T(8,128)(2,1)}) custom-call(s32[1]{0:T(128)} %bitcast.core_ref, bf16[128,6144]{1,0:T(8,128)(2,1)} %q_ref.1, bf16[128,6144]{1,0:T(8,128)(2,1)} %g_ref.1), custom_call_target="tpu_custom_call" | custom-call | bytes 6291456 | tf_op jit(solution)/shard_map/pallas_call | solution.py:212
  62.3 0.0 copy-start.8
  62.3 0.0 copy-start.9
  62.3 0.0 copy-start.3
  62.3 0.0 copy-start.4
  62.3 3.3 %collective-permute-start = (bf16[2,128,3072]{2,1,0:T(8,128)(2,1)}, bf16[2,128,3072]{2,1,0:T(8,128)(2,1)}, u32[]{:S(2)}, u32[]{:S(2)}) collective-permute-start(bf16[2,128,3072]{2,1,0:T(8,128)(2,1)} %get-tuple-element.16), channel_id=1, source_target_pairs={{0,1},{1,0},{2,3},{3,2},{4,5},{5,4},{6,7},{7,6},{8,9},{9,8},{10,11... | collective-permute-start | bytes 4718600 | tf_op jit(solution)/shard_map/ppermute | solution.py:288
  65.6 0.0 copy-done.5
  65.6 0.0 copy-done.6
  65.7 0.1 maximum_bitcast_fusion
  65.8 0.8 broadcast_in_dim.86
  66.6 7.7 %all-to-all-start = ((bf16[16,2,24,256]{3,2,1,0:T(8,128)(2,1)}), bf16[16,2,24,256]{3,2,1,0:T(8,128)(2,1)S(1)}, u32[]{:S(2)}, u32[]{:S(2)}) async-start(bf16[16,2,24,256]{3,2,1,0:T(8,128)(2,1)} %bitcast.2), calls=%async_computation | async-start | bytes 786432 | tf_op jit(solution)/shard_map/all_to_all | solution.py:291
  74.3 0.0 copy-done.7
  74.3 0.2 reduce-window.7
  74.5 0.0 copy-done.8
  74.5 0.0 copy-done.9
  74.5 0.2 select_reduce_fusion.4
  74.7 0.1 convert_reduce_fusion.1
  74.8 0.1 select_reduce_fusion.3
  74.9 0.2 and_select_fusion
  75.1 0.0 copy-done.3
  75.1 0.0 copy-done.4
  75.2 0.0 copy-start
  75.2 0.0 collective-permute-done.2.refs_2_
  75.2 0.0 collective-permute-done.1.refs_1_
  75.3 2.1 %collective-permute-start.3 = (bf16[3,2,128,256]{3,2,1,0:T(8,128)(2,1)S(1)}, bf16[3,2,128,256]{3,2,1,0:T(8,128)(2,1)S(1)}, u32[]{:S(2)}, u32[]{:S(2)}) collective-permute-start(bf16[3,2,128,256]{3,2,1,0:T(8,128)(2,1)S(1)} %pad_maximum_fusion.1), channel_id=1, source_target_pairs={{0,1},{1,0},{2,3},{3,2},{4,5},{5,4},{6,7},{7,6},{8,9},{9,8},{10,11... | collective-permute-start | bytes 1179656 | tf_op jit(solution)/shard_map/ppermute | solution.py:288
  77.5 0.2 and_select_fusion.1
  77.7 1.4 collective-permute-done.3.refs_3_
  79.1 0.0 collective-permute-done.others_ref
  79.1 0.0 copy-done
  79.1 7.5 %shard_map.121.stat_ref = f32[3,2,2,12,128]{4,3,2,1,0:T(8,128)S(1)} custom-call(s32[1]{0:T(128)} %bitcast.core_ref, bf16[2,128,3072]{2,1,0:T(8,128)(2,1)S(1)} %copy-done, bf16[2,128,3072]{2,1,0:T(8,128)(2,1)} %collective-permute-done.others_ref, bf16[2,128,512]{2,1,0:T(8,128)(2,1)S(1)} %pad_maximum_fusion.2.refs_0_, ...), custom_call_target="tpu_custom_call" | custom-call | flops 2013265920 | bytes 6291456 | tf_op jit(solution)/shard_map/pallas_call | solution.py:248
  86.6 2.3 %all-to-all-done.pref_ref = bf16[16,2,24,256]{3,2,1,0:T(8,128)(2,1)S(1)} async-done(((bf16[16,2,24,256]{3,2,1,0:T(8,128)(2,1)}), bf16[16,2,24,256]{3,2,1,0:T(8,128)(2,1)S(1)}, u32[]{:S(2)}, u32[]{:S(2)}) %all-to-all-start) | async-done | bytes 393248 | tf_op jit(solution)/shard_map/all_to_all | solution.py:291
  88.8 0.0 copy-start.1
  88.8 1.4 copy-done.1
  90.2 7.3 %shard_map.122 = (f32[2,2,2,12,128]{4,3,2,1,0:T(8,128)S(1)}, bf16[4,16,24,128]{3,2,1,0:T(8,128)(2,1)}) custom-call(bf16[2,128,3072]{2,1,0:T(8,128)(2,1)S(1)} %copy-done.1, bf16[2,128,3072]{2,1,0:T(8,128)(2,1)} %collective-permute-done.others_ref, bf16[16,2,24,256]{3,2,1,0:T(8,128)(2,1)S(1)} %all-to-all-done.pref_ref, s32[2,1,128]{2,1,0:T(1,128)S(1)} %pad_add_fusion.slot_ref, ...), custom_call_target="tpu_custom_call" | custom-call | flops 2415919104 | bytes 6291456 | tf_op jit(solution)/shard_map/pallas_call | solution.py:248
  97.5 7.9 %all-to-all-start.1 = ((bf16[64,24,128]{2,1,0:T(8,128)(2,1)}), bf16[64,24,128]{2,1,0:T(8,128)(2,1)S(1)}, u32[]{:S(2)}, u32[]{:S(2)}) async-start(bf16[64,24,128]{2,1,0:T(8,128)(2,1)} %bitcast.14), calls=%async_computation.1 | async-start | bytes 786432 | tf_op jit(solution)/shard_map/all_to_all | solution.py:291
  105.4 0.0 copy-start.2
  105.4 1.4 copy-done.2
  106.8 10.3 %shard_map.124 = (f32[2,256,256]{2,1,0:T(8,128)S(1)}, bf16[2,256,256]{2,1,0:T(8,128)(2,1)S(1)}, bf16[2,256,256]{2,1,0:T(8,128)(2,1)S(1)}) custom-call(s32[1]{0:T(128)} %bitcast.core_ref, bf16[2,128,3072]{2,1,0:T(8,128)(2,1)S(1)} %copy-done.2, bf16[2,128,3072]{2,1,0:T(8,128)(2,1)} %collective-permute-done.others_ref, ...), custom_call_target="tpu_custom_call" | custom-call | flops 4026531840 | bytes 6291456 | tf_op jit(solution)/shard_map/pallas_call | solution.py:248
  117.1 1.3 collective-permute-start.5
  118.4 1.3 collective-permute-start.4
  119.7 0.3 all-to-all-done.1.got_ref
  120.0 0.8 shard_map.123
  120.8 9.7 %all-to-all-start.2 = ((bf16[32,2,24,128]{3,2,1,0:T(8,128)(2,1)}), bf16[32,2,24,128]{3,2,1,0:T(8,128)(2,1)S(1)}, u32[]{:S(2)}, u32[]{:S(2)}) async-start(bf16[32,2,24,128]{3,2,1,0:T(8,128)(2,1)} %shard_map.123), calls=%async_computation.2 | async-start | bytes 786432 | tf_op jit(solution)/shard_map/all_to_all | solution.py:291
  130.5 2.5 %collective-permute-done.5 = bf16[2,256,256]{2,1,0:T(8,128)(2,1)S(1)} collective-permute-done((bf16[2,256,256]{2,1,0:T(8,128)(2,1)S(1)}, bf16[2,256,256]{2,1,0:T(8,128)(2,1)S(1)}, u32[]{:S(2)}, u32[]{:S(2)}) %collective-permute-start.5) | collective-permute-done | bytes 262176 | tf_op jit(solution)/shard_map/ppermute | solution.py:285
  133.0 0.0 collective-permute-done.4
  133.0 0.1 add_convert_fusion
  133.1 4.1 %collective-permute-start.6 = (bf16[2,128,256]{2,1,0:T(8,128)(2,1)S(1)}, bf16[2,128,256]{2,1,0:T(8,128)(2,1)S(1)}, u32[]{:S(2)}, u32[]{:S(2)}) collective-permute-start(bf16[2,128,256]{2,1,0:T(8,128)(2,1)S(1)} %slice.17), channel_id=1, source_target_pairs={{0,1},{1,0},{2,3},{3,2},{4,5},{5,4},{6,7},{7,6},{8,9},{9,8},{10,11... | collective-permute-start | bytes 393224 | tf_op jit(solution)/shard_map/ppermute | solution.py:288
  137.2 1.0 collective-permute-done.6
  138.2 0.7 fusion.4
  138.9 5.6 %all-to-all-done.2 = bf16[32,2,24,128]{3,2,1,0:T(8,128)(2,1)S(1)} async-done(((bf16[32,2,24,128]{3,2,1,0:T(8,128)(2,1)}), bf16[32,2,24,128]{3,2,1,0:T(8,128)(2,1)S(1)}, u32[]{:S(2)}, u32[]{:S(2)}) %all-to-all-start.2) | async-done | bytes 393248 | tf_op jit(solution)/shard_map/all_to_all | solution.py:291
  144.4 0.7 shard_map.125
  (24 shorter events, 0.3 us)
Async XLA Ops:
  1.6 73.6 %collective-permute-start.1 = (bf16[2,128,512]{2,1,0:T(8,128)(2,1)S(1)}, bf16[2,128,512]{2,1,0:T(8,128)(2,1)S(1)}, u32[]{:S(2)}, u32[]{:S(2)}) collective-permute-start(bf16[2,128,512]{2,1,0:T(8,128)(2,1)S(1)} %pad_maximum_fusion.2.refs_0_), channel_id=1, source_target_pairs={{0,2},{1,3},{2,4},{3,5},{4,6},{5,7},{6,8},{7,9},{8,10},{9,11},{10,... | collective-permute-start | bytes 786440 | tf_op jit(solution)/shard_map/ppermute | solution.py:285
  6.5 68.7 %collective-permute-start.2 = (bf16[2,128,512]{2,1,0:T(8,128)(2,1)S(1)}, bf16[2,128,512]{2,1,0:T(8,128)(2,1)S(1)}, u32[]{:S(2)}, u32[]{:S(2)}) collective-permute-start(bf16[2,128,512]{2,1,0:T(8,128)(2,1)S(1)} %pad_maximum_fusion.2.refs_0_), channel_id=1, source_target_pairs={{0,4},{1,5},{2,6},{3,7},{4,8},{5,9},{6,10},{7,11},{8,12},{9,13},{1... | collective-permute-start | bytes 786440 | tf_op jit(solution)/shard_map/ppermute | solution.py:285
  12.3 53.3 %copy-start.5 = (bf16[24,512]{1,0:T(8,128)(2,1)S(1)}, bf16[24,512]{1,0:T(8,128)(2,1)}, u32[]{:S(2)}) copy-start(bf16[24,512]{1,0:T(8,128)(2,1)} %param.14) | copy-start | bytes 73732
  12.3 53.3 %copy-start.6 = (bf16[24,512]{1,0:T(8,128)(2,1)S(1)}, bf16[24,512]{1,0:T(8,128)(2,1)}, u32[]{:S(2)}) copy-start(bf16[24,512]{1,0:T(8,128)(2,1)} %param.13) | copy-start | bytes 73732
  12.3 62.0 %copy-start.7 = (s32[1,8]{1,0:T(1,128)S(1)}, s32[1,8]{1,0:T(1,128)}, u32[]{:S(2)}) copy-start(s32[1,8]{1,0:T(1,128)} %param.15) | copy-start | bytes 100
  62.3 12.2 %copy-start.8 = (s32[6]{0:T(128)S(1)}, s32[6]{0:T(128)}, u32[]{:S(2)}) copy-start(s32[6]{0:T(128)} %param.17) | copy-start | bytes 76
  62.3 12.2 %copy-start.9 = (s32[1,8]{1,0:T(1,128)S(1)}, s32[1,8]{1,0:T(1,128)}, u32[]{:S(2)}) copy-start(s32[1,8]{1,0:T(1,128)} %param.16) | copy-start | bytes 100
  62.3 12.8 %copy-start.3 = (bf16[128,512]{1,0:T(8,128)(2,1)S(1)}, bf16[128,512]{1,0:T(8,128)(2,1)}, u32[]{:S(2)}) copy-start(bf16[128,512]{1,0:T(8,128)(2,1)} %param.11) | copy-start | bytes 393220
  62.3 12.8 %copy-start.4 = (bf16[128,512]{1,0:T(8,128)(2,1)S(1)}, bf16[128,512]{1,0:T(8,128)(2,1)}, u32[]{:S(2)}) copy-start(bf16[128,512]{1,0:T(8,128)(2,1)} %param.10) | copy-start | bytes 393220
  62.3 16.7 %collective-permute-start = (bf16[2,128,3072]{2,1,0:T(8,128)(2,1)}, bf16[2,128,3072]{2,1,0:T(8,128)(2,1)}, u32[]{:S(2)}, u32[]{:S(2)}) collective-permute-start(bf16[2,128,3072]{2,1,0:T(8,128)(2,1)} %get-tuple-element.16), channel_id=1, source_target_pairs={{0,1},{1,0},{2,3},{3,2},{4,5},{5,4},{6,7},{7,6},{8,9},{9,8},{10,11... | collective-permute-start | bytes 4718600 | tf_op jit(solution)/shard_map/ppermute | solution.py:288
  66.6 22.3 %all-to-all-start = ((bf16[16,2,24,256]{3,2,1,0:T(8,128)(2,1)}), bf16[16,2,24,256]{3,2,1,0:T(8,128)(2,1)S(1)}, u32[]{:S(2)}, u32[]{:S(2)}) async-start(bf16[16,2,24,256]{3,2,1,0:T(8,128)(2,1)} %bitcast.2), calls=%async_computation | async-start | bytes 786432 | tf_op jit(solution)/shard_map/all_to_all | solution.py:291
  75.2 3.9 %copy-start = (bf16[2,128,3072]{2,1,0:T(8,128)(2,1)S(1)}, bf16[2,128,3072]{2,1,0:T(8,128)(2,1)}, u32[]{:S(2)}) copy-start(bf16[2,128,3072]{2,1,0:T(8,128)(2,1)} %get-tuple-element.15.mine_ref) | copy-start | bytes 4718596
  75.3 3.7 %collective-permute-start.3 = (bf16[3,2,128,256]{3,2,1,0:T(8,128)(2,1)S(1)}, bf16[3,2,128,256]{3,2,1,0:T(8,128)(2,1)S(1)}, u32[]{:S(2)}, u32[]{:S(2)}) collective-permute-start(bf16[3,2,128,256]{3,2,1,0:T(8,128)(2,1)S(1)} %pad_maximum_fusion.1), channel_id=1, source_target_pairs={{0,1},{1,0},{2,3},{3,2},{4,5},{5,4},{6,7},{7,6},{8,9},{9,8},{10,11... | collective-permute-start | bytes 1179656 | tf_op jit(solution)/shard_map/ppermute | solution.py:288
  88.8 1.4 copy-start.1
  97.5 22.5 %all-to-all-start.1 = ((bf16[64,24,128]{2,1,0:T(8,128)(2,1)}), bf16[64,24,128]{2,1,0:T(8,128)(2,1)S(1)}, u32[]{:S(2)}, u32[]{:S(2)}) async-start(bf16[64,24,128]{2,1,0:T(8,128)(2,1)} %bitcast.14), calls=%async_computation.1 | async-start | bytes 786432 | tf_op jit(solution)/shard_map/all_to_all | solution.py:291
  105.4 1.4 copy-start.2
  117.1 15.8 %collective-permute-start.5 = (bf16[2,256,256]{2,1,0:T(8,128)(2,1)S(1)}, bf16[2,256,256]{2,1,0:T(8,128)(2,1)S(1)}, u32[]{:S(2)}, u32[]{:S(2)}) collective-permute-start(bf16[2,256,256]{2,1,0:T(8,128)(2,1)S(1)} %get-tuple-element.21), channel_id=1, source_target_pairs={{4,0},{5,1},{6,2},{7,3},{8,4},{9,5},{10,6},{11,7},{12,8},{13,9},{1... | collective-permute-start | bytes 786440 | tf_op jit(solution)/shard_map/ppermute | solution.py:285
  118.4 14.6 %collective-permute-start.4 = (bf16[2,256,256]{2,1,0:T(8,128)(2,1)S(1)}, bf16[2,256,256]{2,1,0:T(8,128)(2,1)S(1)}, u32[]{:S(2)}, u32[]{:S(2)}) collective-permute-start(bf16[2,256,256]{2,1,0:T(8,128)(2,1)S(1)} %get-tuple-element.20), channel_id=1, source_target_pairs={{2,0},{3,1},{4,2},{5,3},{6,4},{7,5},{8,6},{9,7},{10,8},{11,9},{12,... | collective-permute-start | bytes 786440 | tf_op jit(solution)/shard_map/ppermute | solution.py:285
  120.8 23.6 %all-to-all-start.2 = ((bf16[32,2,24,128]{3,2,1,0:T(8,128)(2,1)}), bf16[32,2,24,128]{3,2,1,0:T(8,128)(2,1)S(1)}, u32[]{:S(2)}, u32[]{:S(2)}) async-start(bf16[32,2,24,128]{3,2,1,0:T(8,128)(2,1)} %shard_map.123), calls=%async_computation.2 | async-start | bytes 786432 | tf_op jit(solution)/shard_map/all_to_all | solution.py:291
  133.1 5.0 %collective-permute-start.6 = (bf16[2,128,256]{2,1,0:T(8,128)(2,1)S(1)}, bf16[2,128,256]{2,1,0:T(8,128)(2,1)S(1)}, u32[]{:S(2)}, u32[]{:S(2)}) collective-permute-start(bf16[2,128,256]{2,1,0:T(8,128)(2,1)S(1)} %slice.17), channel_id=1, source_target_pairs={{0,1},{1,0},{2,3},{3,2},{4,5},{5,4},{6,7},{7,6},{8,9},{9,8},{10,11... | collective-permute-start | bytes 393224 | tf_op jit(solution)/shard_map/ppermute | solution.py:288

commit v6 on v5

--- a/solution.py
+++ b/solution.py
@@ -19,7 +19,6 @@
 TO_LOG2 = SCALE * math.log2(math.e)
 F32 = jnp.float32
 BF16 = jnp.bfloat16
-VMEM_BYTES = 20 << 20
 
 
 def heads_of(ref, start, count, lead=()):
@@ -36,17 +35,33 @@
         ref[kind, h, chunk, j : j + 1, :] = row[:, j * HD : (j + 1) * HD]
 
 
-def units(mine_ref, others_ref):
+def units(core, q_ref, g_ref, others_ref, rows_ref, sems):
     kept = KVH // 2
-    run = mine_ref.shape[2] // kept
-    found = []
+    run = q_ref.shape[1] // KVH
+    copies, found = {}, []
     for h in range(kept):
-        for chunk, ref in enumerate((mine_ref, others_ref)):
-
-            def read(which, first, count, h=h, ref=ref):
-                return heads_of(ref, h * run + first * HD, count, (which,))
-
-            found.append((h, chunk, read))
+        for chunk in range(2):
+            for which, ref in enumerate((q_ref, g_ref)):
+                start = h * run if chunk else pl.multiple_of((core * kept + h) * run, HD)
+                source = others_ref.at[which] if chunk else ref
+                copies[h, chunk, which] = pltpu.make_async_copy(
+                    source.at[:, pl.ds(start, run)],
+                    rows_ref.at[h, chunk, which],
+                    sems.at[h, chunk, which],
+                )
+    for copy in copies.values():
+        copy.start()
+    for h in range(kept):
+        for chunk in range(2):
+
+            def ready(h=h, chunk=chunk):
+                copies[h, chunk, 0].wait()
+                copies[h, chunk, 1].wait()
+
+            def read(which, first, count, h=h, chunk=chunk):
+                return heads_of(rows_ref, first * HD, count, (h, chunk, which))
+
+            found.append((h, chunk, ready, read))
     return found, run // HD
 
 
@@ -63,14 +78,16 @@
     )
 
 
-def token_stats_kernel(core_ref, mine_ref, others_ref, *refs):
-    window, (bias_ref, stat_ref) = refs[:4], refs[4:]
+def token_stats_kernel(core_ref, q_ref, g_ref, others_ref, *refs):
+    window, (bias_ref, stat_ref, rows_ref, sems) = refs[:4], refs[4:]
     core = core_ref[0]
-    toks = mine_ref.shape[1]
+    toks = q_ref.shape[0]
     blocks = bias_ref.shape[1] // toks
-    found, heads = units(mine_ref, others_ref)
-    for h, chunk, read in found:
+    found, heads = units(core, q_ref, g_ref, others_ref, rows_ref, sems)
+    for h, chunk, ready, read in found:
         keys, values = (windows(core, h, which, *window)[chunk] for which in range(2))
+
+        ready()
 
         def dots(j, keys=keys, values=values, read=read):
             return (
@@ -103,12 +120,14 @@
             stat_ref[2, h, chunk, j : j + 1, :] = jnp.sum(dot * weight, axis=0, keepdims=True)
 
 
-def prefix_kernel(mine_ref, others_ref, pref_ref, slot_ref, stat_ref, full_ref, out_ref):
+def prefix_kernel(
+    core_ref, q_ref, g_ref, others_ref, pref_ref, slot_ref, stat_ref, full_ref, out_ref, rows_ref, sems
+):
     count, _, each, _ = pref_ref.shape
-    found, heads = units(mine_ref, others_ref)
+    found, heads = units(core_ref[0], q_ref, g_ref, others_ref, rows_ref, sems)
     slots = count * each // PLEN
     grads = {}
-    for h, chunk, read in found:
+    for h, chunk, ready, read in found:
         if not chunk:
             columns = slice(h * HD, (h + 1) * HD)
             keys, values = (
@@ -117,6 +136,7 @@
                 ).astype(BF16)
                 for which in range(2)
             )
+        ready()
         q, g = read(0, 0, heads), read(1, 0, heads)
         slot = jnp.concatenate([slot_ref[chunk]] * heads, axis=1)
         s_all = lax.dot_general(keys, q, NT, preferred_element_type=F32)
@@ -157,14 +177,15 @@
                     out_ref[2 * which + h, part] = rows.astype(BF16)
 
 
-def token_grads_kernel(core_ref, mine_ref, others_ref, *refs):
-    window, (bias_ref, full_ref, home_ref, one_ref, two_ref) = refs[:4], refs[4:]
+def token_grads_kernel(core_ref, q_ref, g_ref, others_ref, *refs):
+    window, (bias_ref, full_ref, home_ref, one_ref, two_ref, rows_ref, sems) = refs[:4], refs[4:]
     core = core_ref[0]
     even = core == 0
-    toks = mine_ref.shape[1]
-    found, heads = units(mine_ref, others_ref)
+    toks = q_ref.shape[0]
+    found, heads = units(core, q_ref, g_ref, others_ref, rows_ref, sems)
     grads = {}
-    for h, chunk, read in found:
+    for h, chunk, ready, read in found:
+        ready()
         keys, values = (windows(core, h, which, *window)[chunk] for which in range(2))
         q, g = read(0, 0, heads), read(1, 0, heads)
         bias = jnp.concatenate([bias_ref[chunk]] * heads, axis=1)
@@ -191,34 +212,6 @@
             two_ref[which, toks:, columns] = (b[3] + jnp.where(even, a[4], zero)).astype(BF16)
 
 
-def halves_kernel(core_ref, q_ref, g_ref, mine_ref, theirs_ref, sems):
-    width = mine_ref.shape[2]
-    copies = []
-    for which, ref in enumerate((q_ref, g_ref)):
-        for n, (out, side) in enumerate(((theirs_ref, 1 - core_ref[0]), (mine_ref, core_ref[0]))):
-            columns = pl.ds(pl.multiple_of(side * width, HD), width)
-            copies.append(
-                pltpu.make_async_copy(ref.at[:, columns], out.at[which], sems.at[which, n])
-            )
-    for copy in copies:
-        copy.start()
-    for copy in copies:
-        copy.wait()
-
-
-def halves(cores, q, g):
-    half = jax.ShapeDtypeStruct((2, q.shape[0], q.shape[1] // 2), q.dtype)
-    anywhere = pl.BlockSpec(memory_space=pl.ANY)
-    return pl.pallas_call(
-        halves_kernel,
-        in_specs=[pl.BlockSpec(memory_space=pltpu.SMEM), anywhere, anywhere],
-        out_specs=[pl.BlockSpec(memory_space=pltpu.VMEM), anywhere],
-        out_shape=[half, half],
-        scratch_shapes=[pltpu.SemaphoreType.DMA((2, 2))],
-        cost_estimate=pl.CostEstimate(flops=0, bytes_accessed=4 * q.size * 2, transcendentals=0),
-    )(cores, q, g)
-
-
 def spread_kernel(got_ref, out_ref):
     count, cores = out_ref.shape[:2]
     for c in range(cores):
@@ -242,17 +235,28 @@
                 out_ref[:, at : at + HD] = total
 
 
-def call(kernel, flops, exps, ins, outs):
+def call(kernel, flops, exps, ins, outs, rows=()):
     space = pl.BlockSpec(memory_space=pltpu.VMEM)
-    scalar = pl.BlockSpec(memory_space=pltpu.SMEM)
+    specs = [space] * len(ins)
+    scratch = []
+    if rows:
+        far = pl.BlockSpec(memory_space=pl.ANY)
+        specs = [pl.BlockSpec(memory_space=pltpu.SMEM)] + [far] * 3 + specs
+        toks, width = rows[1].shape
+        lead = (KVH // 2, 2, 2)
+        scratch = [
+            pltpu.VMEM((*lead, toks, width // KVH), BF16),
+            pltpu.SemaphoreType.DMA(lead),
+        ]
     return pl.pallas_call(
         kernel,
-        in_specs=[scalar if x.ndim == 1 else space for x in ins],
+        in_specs=specs,
         out_specs=[space] * len(outs),
         out_shape=outs,
-        compiler_params=pltpu.CompilerParams(vmem_limit_bytes=VMEM_BYTES),
+        scratch_shapes=scratch,
+        compiler_params=pltpu.CompilerParams(vmem_limit_bytes=(60 if rows else 16) << 20),
         cost_estimate=pl.CostEstimate(flops=flops, bytes_accessed=6 << 20, transcendentals=exps),
-    )(*ins)
+    )(*rows, *ins)
 
 
 def layout(lengths, tenants, slots, block, shards, toks):
@@ -300,8 +304,7 @@
     pref = pref.reshape(2, -1, 2, KVH * HD // 2).transpose(2, 0, 1, 3)
     pref = jnp.broadcast_to(pref[None], (parts, *pref.shape)).reshape(count, *pref.shape[1:])
     pref = exchange(pref, SEQ)
-    mine, theirs = halves(cores, queries, grad_out)
-    others = swap(theirs)
+    others = swap(jnp.stack([other_half(queries), other_half(grad_out)]))
     cross = swap(jnp.stack([other_half(own), other_half(one), other_half(two)]))
 
     facing = index ^ 1
@@ -314,23 +317,25 @@
     bias1, slot1 = layout(*docs, facing, shards, toks)
     bias, slot = jnp.stack([bias0, bias1]), jnp.stack([slot0, slot1])
 
-    heads = [mine, others]
+    rows_in = (cores, queries, grad_out, others)
     shape = (KVH // 2, 2, HQ // KVH, toks)
     work = queries.size // HD * bias.shape[1]
-    window = [cores, *heads, own, one, two, cross, bias]
+    window = [own, one, two, cross, bias]
     (stats,) = call(
         token_stats_kernel,
         flops=4 * HD * work,
         exps=work,
         ins=window,
         outs=[jax.ShapeDtypeStruct((3, *shape), F32)],
+        rows=rows_in,
     )
     prefs = queries.size // HD * count * pref.shape[2]
     full, rows = call(
         prefix_kernel,
         flops=8 * HD * prefs,
         exps=prefs // 6,
-        ins=[*heads, pref, slot, stats],
+        ins=[pref, slot, stats],
+        rows=rows_in,
         outs=[
             jax.ShapeDtypeStruct((2, *shape), F32),
             jax.ShapeDtypeStruct((KVH, count, pref.shape[2], HD), BF16),
@@ -342,6 +347,7 @@
         flops=8 * HD * work,
         exps=work,
         ins=window + [full],
+        rows=rows_in,
         outs=[jax.ShapeDtypeStruct(wide, kind) for kind in (F32, BF16, BF16)],
     )
 

time: 147 us -> 108 us (0.73)
  Pallas kernels: 76.5 us -> 32 us
  starting transfers between devices: 48 us -> 55.6 us
  waiting for transfers between devices: 12.9 us -> 9.37 us
  other arithmetic: 2.91 us -> 4.48 us
    pallas_call x6 -> x5, Pallas kernels: 76.5 us -> 32 us  [call(): pl.pallas_call(kernel, in_specs=specs, out_specs=[space] * len(outs), out...]
    all_to_all x3, starting transfers between devices: 25.3 us -> 32.6 us  [exchange(): return lax.all_to_all(x, axis, split_axis=0, concat_axis=0, tiled=True)]
    all_to_all x3, waiting for transfers between devices: 8.08 us -> 5.3 us  [exchange(): return lax.all_to_all(x, axis, split_axis=0, concat_axis=0, tiled=True)]
    another operation x0 -> x1, local copies, waits for them, and re-layouts: none -> 1.48 us  [per_device(): others = swap(jnp.stack([other_half(queries), other_half(grad_out)]))]
  transfers between devices with their start and end apart: 10 -> 10, of which waited for: 6 -> 4; matrix products, arithmetic and copies ran while one was open for 2% -> 5% of each run, Pallas kernels for 47% -> 21%
where the time goes in v6:
time: 108 us; the launch traced here: 107 us
  starting transfers between devices  55.6 us (51%)
  Pallas kernels  32 us (30%)
  waiting for transfers between devices  9.37 us (9%)
  other arithmetic  4.48 us (4%)
  local copies, waits for them, and re-layouts  3.92 us (4%)
  between operations  1.13 us (1%)
    all_to_all x3, starting transfers between devices, exchange(): return lax.all_to_all(x, axis, split_axis=0, concat_axis=0, tiled=True)  32.6 us
    pallas_call x5, Pallas kernels, call(): pl.pallas_call(kernel, in_specs=specs, out_specs=[space] * len(outs), out...  32 us
    ppermute x4, starting transfers between devices, shift(): return lax.ppermute(x, SEQ, pairs)  13.4 us
    ppermute x3, starting transfers between devices, swap(): return lax.ppermute(x, SEQ, [(i, i ^ 1) for i in range(count)])  9.63 us
    all_to_all x3, waiting for transfers between devices, exchange(): return lax.all_to_all(x, axis, split_axis=0, concat_axis=0, tiled=True)  5.3 us
    ppermute x4, waiting for transfers between devices, shift(): return lax.ppermute(x, SEQ, pairs)  2.59 us
  transfers between devices with their start and end apart: 10, of which 4 were waited for; matrix products, arithmetic and copies ran while one was open for 5% of the time, Pallas kernels for 21%

profile of v6, /device:TPU:1, one launch (start us, length us, event | category | flops | bytes accessed | tf_op | source)
XLA Modules:
  0.0 106.5 jit_solution(14627971424248122564)
XLA Ops:
  0.6 1.0 pad_maximum_fusion.3.refs_0_
  1.6 0.0 copy-start.4
  1.6 4.8 %collective-permute-start.1 = (bf16[2,128,512]{2,1,0:T(8,128)(2,1)S(1)}, bf16[2,128,512]{2,1,0:T(8,128)(2,1)S(1)}, u32[]{:S(2)}, u32[]{:S(2)}) collective-permute-start(bf16[2,128,512]{2,1,0:T(8,128)(2,1)S(1)} %pad_maximum_fusion.3.refs_0_), channel_id=1, source_target_pairs={{0,2},{1,3},{2,4},{3,5},{4,6},{5,7},{6,8},{7,9},{8,10},{9,11},{10,... | collective-permute-start | bytes 786440 | tf_op jit(solution)/shard_map/ppermute | solution.py:289
  6.5 5.8 %collective-permute-start.2 = (bf16[2,128,512]{2,1,0:T(8,128)(2,1)S(1)}, bf16[2,128,512]{2,1,0:T(8,128)(2,1)S(1)}, u32[]{:S(2)}, u32[]{:S(2)}) collective-permute-start(bf16[2,128,512]{2,1,0:T(8,128)(2,1)S(1)} %pad_maximum_fusion.3.refs_0_), channel_id=1, source_target_pairs={{0,4},{1,5},{2,6},{3,7},{4,8},{5,9},{6,10},{7,11},{8,12},{9,13},{1... | collective-permute-start | bytes 786440 | tf_op jit(solution)/shard_map/ppermute | solution.py:289
  12.3 1.5 %dynamic-slice_bitcast_fusion = (bf16[1,128,3072]{2,1,0:T(8,128)(2,1)S(1)}, bf16[1,128,3072]{2,1,0:T(8,128)(2,1)S(1)}) fusion(bf16[128,6144]{1,0:T(8,128)(2,1)} %g_ref.5, s32[]{:T(128)S(6)} %select_n.71, bf16[128,6144]{1,0:T(8,128)(2,1)} %q_ref.5), kind=kLoop, calls=%fused_computation.1 | loop fusion | bytes 3145732 | tf_op jit(solution)/shard_map/stack | solution.py:307
  13.8 0.0 copy-done.4
  13.8 0.0 copy-start.7
  13.8 0.0 copy-start.8
  13.8 0.0 copy-start.10
  13.8 0.1 pad_maximum_fusion
  14.0 0.0 copy-start.11
  14.0 0.0 copy-start.12
  14.0 0.0 copy-start.1
  14.0 0.0 copy-start.2
  14.0 3.3 %collective-permute-start = (bf16[2,128,3072]{2,1,0:T(8,128)(2,1)S(1)}, bf16[2,128,3072]{2,1,0:T(8,128)(2,1)}, u32[]{:S(2)}, u32[]{:S(2)}) collective-permute-start(bf16[2,128,3072]{2,1,0:T(8,128)(2,1)S(1)} %pad_maximum_fusion), channel_id=1, source_target_pairs={{0,1},{1,0},{2,3},{3,2},{4,5},{5,4},{6,7},{7,6},{8,9},{9,8},{10,11... | collective-permute-start | bytes 4718600 | tf_op jit(solution)/shard_map/ppermute | solution.py:292
  17.3 0.0 copy-done.7
  17.4 0.0 copy-done.8
  17.4 0.1 maximum_bitcast_fusion
  17.5 0.8 broadcast_in_dim.86
  18.3 7.7 %all-to-all-start = ((bf16[16,2,24,256]{3,2,1,0:T(8,128)(2,1)}), bf16[16,2,24,256]{3,2,1,0:T(8,128)(2,1)S(1)}, u32[]{:S(2)}, u32[]{:S(2)}) async-start(bf16[16,2,24,256]{3,2,1,0:T(8,128)(2,1)} %bitcast.4), calls=%async_computation | async-start | bytes 786432 | tf_op jit(solution)/shard_map/all_to_all | solution.py:295
  26.0 0.0 copy-done.10
  26.0 0.2 reduce-window.7
  26.2 0.0 copy-done.11
  26.2 0.0 copy-done.12
  26.3 0.2 select_reduce_fusion.4
  26.5 0.1 convert_reduce_fusion.1
  26.5 0.1 select_reduce_fusion.3
  26.6 0.6 pad_add_fusion.slot_ref
  27.2 0.1 and_select_fusion
  27.4 0.0 copy-done.1
  27.4 0.0 copy-done.2
  27.4 0.0 collective-permute-done.2.refs_2_
  27.5 0.0 copy-start.6
  27.5 0.0 collective-permute-done.1.refs_1_
  27.5 0.0 copy-start.5
  27.6 2.0 %collective-permute-start.3 = (bf16[3,2,128,256]{3,2,1,0:T(8,128)(2,1)S(1)}, bf16[3,2,128,256]{3,2,1,0:T(8,128)(2,1)S(1)}, u32[]{:S(2)}, u32[]{:S(2)}) collective-permute-start(bf16[3,2,128,256]{3,2,1,0:T(8,128)(2,1)S(1)} %pad_maximum_fusion.2), channel_id=1, source_target_pairs={{0,1},{1,0},{2,3},{3,2},{4,5},{5,4},{6,7},{7,6},{8,9},{9,8},{10,11... | collective-permute-start | bytes 1179656 | tf_op jit(solution)/shard_map/ppermute | solution.py:292
  29.6 0.2 and_select_fusion.1
  29.8 0.9 pad_maximum_fusion.1.refs_4_
  30.7 0.5 collective-permute-done.3.refs_3_
  31.2 0.0 collective-permute-done.others_ref
  31.2 0.0 copy-done.6
  31.2 0.8 copy-done.9
  32.0 9.1 %shard_map.120.stat_ref = f32[3,2,2,12,128]{4,3,2,1,0:T(8,128)} custom-call(s32[1]{0:T(128)} %bitcast.core_ref, bf16[128,6144]{1,0:T(8,128)(2,1)} %q_ref.5, bf16[128,6144]{1,0:T(8,128)(2,1)} %g_ref.5, bf16[2,128,3072]{2,1,0:T(8,128)(2,1)} %collective-permute-done.others_ref, bf16[2,128,512]{2,1,0:T(8,128)(2,1)} %copy-done.4, bf16[2,128,512]{2,1,0:T(8,128)(2,1)} %copy-done.5, ...), custom_call_target="tpu_custom_call" | custom-call | flops 2013265920 | bytes 6291456 | tf_op jit(solution)/shard_map/pallas_call | solution.py:251
  41.1 0.0 all-to-all-done.pref_ref
  41.1 0.0 copy-start.3
  41.1 0.7 copy-done.3
  41.9 8.6 %shard_map.121 = (f32[2,2,2,12,128]{4,3,2,1,0:T(8,128)}, bf16[4,16,24,128]{3,2,1,0:T(8,128)(2,1)}) custom-call(s32[1]{0:T(128)} %bitcast.core_ref, bf16[128,6144]{1,0:T(8,128)(2,1)} %q_ref.5, bf16[128,6144]{1,0:T(8,128)(2,1)} %g_ref.5, bf16[2,128,3072]{2,1,0:T(8,128)(2,1)} %collective-permute-done.others_ref, bf16[16,2,24,256]{3,2,1,0:T(8,128)(2,1)} %copy-done.3, ...), custom_call_target="tpu_custom_call" | custom-call | flops 2415919104 | bytes 6291456 | tf_op jit(solution)/shard_map/pallas_call | solution.py:251
  50.5 15.0 %all-to-all-start.1 = ((bf16[64,24,128]{2,1,0:T(8,128)(2,1)}), bf16[64,24,128]{2,1,0:T(8,128)(2,1)S(1)}, u32[]{:S(2)}, u32[]{:S(2)}) async-start(bf16[64,24,128]{2,1,0:T(8,128)(2,1)} %bitcast.35), calls=%async_computation.1 | async-start | bytes 786432 | tf_op jit(solution)/shard_map/all_to_all | solution.py:295
  65.5 12.8 %shard_map.123 = (f32[2,256,256]{2,1,0:T(8,128)}, bf16[2,256,256]{2,1,0:T(8,128)(2,1)}, bf16[2,256,256]{2,1,0:T(8,128)(2,1)}) custom-call(s32[1]{0:T(128)} %bitcast.core_ref, bf16[128,6144]{1,0:T(8,128)(2,1)} %q_ref.5, bf16[128,6144]{1,0:T(8,128)(2,1)} %g_ref.5, bf16[2,128,3072]{2,1,0:T(8,128)(2,1)} %collective-permute-done.others_ref, ...), custom_call_target="tpu_custom_call" | custom-call | flops 4026531840 | bytes 6291456 | tf_op jit(solution)/shard_map/pallas_call | solution.py:251
  78.3 0.0 copy-start
  78.3 1.4 %collective-permute-start.5 = (bf16[2,256,256]{2,1,0:T(8,128)(2,1)}, bf16[2,256,256]{2,1,0:T(8,128)(2,1)S(1)}, u32[]{:S(2)}, u32[]{:S(2)}) collective-permute-start(bf16[2,256,256]{2,1,0:T(8,128)(2,1)} %get-tuple-element.17), channel_id=1, source_target_pairs={{4,0},{5,1},{6,2},{7,3},{8,4},{9,5},{10,6},{11,7},{12,8},{13,9},{1... | collective-permute-start | bytes 786440 | tf_op jit(solution)/shard_map/ppermute | solution.py:289
  79.7 1.3 %collective-permute-start.4 = (bf16[2,256,256]{2,1,0:T(8,128)(2,1)}, bf16[2,256,256]{2,1,0:T(8,128)(2,1)S(1)}, u32[]{:S(2)}, u32[]{:S(2)}) collective-permute-start(bf16[2,256,256]{2,1,0:T(8,128)(2,1)} %get-tuple-element.16), channel_id=1, source_target_pairs={{2,0},{3,1},{4,2},{5,3},{6,4},{7,5},{8,6},{9,7},{10,8},{11,9},{12,... | collective-permute-start | bytes 786440 | tf_op jit(solution)/shard_map/ppermute | solution.py:289
  81.0 0.0 all-to-all-done.1.got_ref
  81.1 0.8 shard_map.122
  81.9 9.9 %all-to-all-start.2 = ((bf16[32,2,24,128]{3,2,1,0:T(8,128)(2,1)}), bf16[32,2,24,128]{3,2,1,0:T(8,128)(2,1)S(1)}, u32[]{:S(2)}, u32[]{:S(2)}) async-start(bf16[32,2,24,128]{3,2,1,0:T(8,128)(2,1)} %shard_map.122), calls=%async_computation.2 | async-start | bytes 786432 | tf_op jit(solution)/shard_map/all_to_all | solution.py:295
  91.8 2.6 %collective-permute-done.5 = bf16[2,256,256]{2,1,0:T(8,128)(2,1)S(1)} collective-permute-done((bf16[2,256,256]{2,1,0:T(8,128)(2,1)}, bf16[2,256,256]{2,1,0:T(8,128)(2,1)S(1)}, u32[]{:S(2)}, u32[]{:S(2)}) %collective-permute-start.5) | collective-permute-done | bytes 262176 | tf_op jit(solution)/shard_map/ppermute | solution.py:289
  94.4 0.0 collective-permute-done.4
  94.4 0.0 copy-done
  94.4 0.1 add_convert_fusion
  94.5 4.3 %collective-permute-start.6 = (bf16[2,128,256]{2,1,0:T(8,128)(2,1)S(1)}, bf16[2,128,256]{2,1,0:T(8,128)(2,1)S(1)}, u32[]{:S(2)}, u32[]{:S(2)}) collective-permute-start(bf16[2,128,256]{2,1,0:T(8,128)(2,1)S(1)} %slice.17), channel_id=1, source_target_pairs={{0,1},{1,0},{2,3},{3,2},{4,5},{5,4},{6,7},{7,6},{8,9},{9,8},{10,11... | collective-permute-start | bytes 393224 | tf_op jit(solution)/shard_map/ppermute | solution.py:292
  98.8 1.0 collective-permute-done.6
  99.8 0.7 fusion.4
  100.5 5.3 %all-to-all-done.2 = bf16[32,2,24,128]{3,2,1,0:T(8,128)(2,1)S(1)} async-done(((bf16[32,2,24,128]{3,2,1,0:T(8,128)(2,1)}), bf16[32,2,24,128]{3,2,1,0:T(8,128)(2,1)S(1)}, u32[]{:S(2)}, u32[]{:S(2)}) %all-to-all-start.2) | async-done | bytes 393248 | tf_op jit(solution)/shard_map/all_to_all | solution.py:295
  105.8 0.7 shard_map.124
  (24 shorter events, 0.2 us)
Async XLA Ops:
  1.6 12.2 %copy-start.4 = (bf16[2,128,512]{2,1,0:T(8,128)(2,1)}, bf16[2,128,512]{2,1,0:T(8,128)(2,1)S(1)}, u32[]{:S(2)}) copy-start(bf16[2,128,512]{2,1,0:T(8,128)(2,1)S(1)} %pad_maximum_fusion.3.refs_0_) | copy-start | bytes 786436
  1.6 25.9 %collective-permute-start.1 = (bf16[2,128,512]{2,1,0:T(8,128)(2,1)S(1)}, bf16[2,128,512]{2,1,0:T(8,128)(2,1)S(1)}, u32[]{:S(2)}, u32[]{:S(2)}) collective-permute-start(bf16[2,128,512]{2,1,0:T(8,128)(2,1)S(1)} %pad_maximum_fusion.3.refs_0_), channel_id=1, source_target_pairs={{0,2},{1,3},{2,4},{3,5},{4,6},{5,7},{6,8},{7,9},{8,10},{9,11},{10,... | collective-permute-start | bytes 786440 | tf_op jit(solution)/shard_map/ppermute | solution.py:289
  6.5 21.0 %collective-permute-start.2 = (bf16[2,128,512]{2,1,0:T(8,128)(2,1)S(1)}, bf16[2,128,512]{2,1,0:T(8,128)(2,1)S(1)}, u32[]{:S(2)}, u32[]{:S(2)}) collective-permute-start(bf16[2,128,512]{2,1,0:T(8,128)(2,1)S(1)} %pad_maximum_fusion.3.refs_0_), channel_id=1, source_target_pairs={{0,4},{1,5},{2,6},{3,7},{4,8},{5,9},{6,10},{7,11},{8,12},{9,13},{1... | collective-permute-start | bytes 786440 | tf_op jit(solution)/shard_map/ppermute | solution.py:289
  13.8 3.5 %copy-start.7 = (bf16[24,512]{1,0:T(8,128)(2,1)S(1)}, bf16[24,512]{1,0:T(8,128)(2,1)}, u32[]{:S(2)}) copy-start(bf16[24,512]{1,0:T(8,128)(2,1)} %param.14) | copy-start | bytes 73732
  13.8 3.5 %copy-start.8 = (bf16[24,512]{1,0:T(8,128)(2,1)S(1)}, bf16[24,512]{1,0:T(8,128)(2,1)}, u32[]{:S(2)}) copy-start(bf16[24,512]{1,0:T(8,128)(2,1)} %param.13) | copy-start | bytes 73732
  13.8 12.2 %copy-start.10 = (s32[1,8]{1,0:T(1,128)S(1)}, s32[1,8]{1,0:T(1,128)}, u32[]{:S(2)}) copy-start(s32[1,8]{1,0:T(1,128)} %param.15) | copy-start | bytes 100
  14.0 12.2 %copy-start.11 = (s32[6]{0:T(128)S(1)}, s32[6]{0:T(128)}, u32[]{:S(2)}) copy-start(s32[6]{0:T(128)} %param.17) | copy-start | bytes 76
  14.0 12.2 %copy-start.12 = (s32[1,8]{1,0:T(1,128)S(1)}, s32[1,8]{1,0:T(1,128)}, u32[]{:S(2)}) copy-start(s32[1,8]{1,0:T(1,128)} %param.16) | copy-start | bytes 100
  14.0 13.4 %copy-start.1 = (bf16[128,512]{1,0:T(8,128)(2,1)S(1)}, bf16[128,512]{1,0:T(8,128)(2,1)}, u32[]{:S(2)}) copy-start(bf16[128,512]{1,0:T(8,128)(2,1)} %param.11) | copy-start | bytes 393220
  14.0 13.4 %copy-start.2 = (bf16[128,512]{1,0:T(8,128)(2,1)S(1)}, bf16[128,512]{1,0:T(8,128)(2,1)}, u32[]{:S(2)}) copy-start(bf16[128,512]{1,0:T(8,128)(2,1)} %param.10) | copy-start | bytes 393220
  14.0 17.2 %collective-permute-start = (bf16[2,128,3072]{2,1,0:T(8,128)(2,1)S(1)}, bf16[2,128,3072]{2,1,0:T(8,128)(2,1)}, u32[]{:S(2)}, u32[]{:S(2)}) collective-permute-start(bf16[2,128,3072]{2,1,0:T(8,128)(2,1)S(1)} %pad_maximum_fusion), channel_id=1, source_target_pairs={{0,1},{1,0},{2,3},{3,2},{4,5},{5,4},{6,7},{7,6},{8,9},{9,8},{10,11... | collective-permute-start | bytes 4718600 | tf_op jit(solution)/shard_map/ppermute | solution.py:292
  18.3 22.9 %all-to-all-start = ((bf16[16,2,24,256]{3,2,1,0:T(8,128)(2,1)}), bf16[16,2,24,256]{3,2,1,0:T(8,128)(2,1)S(1)}, u32[]{:S(2)}, u32[]{:S(2)}) async-start(bf16[16,2,24,256]{3,2,1,0:T(8,128)(2,1)} %bitcast.4), calls=%async_computation | async-start | bytes 786432 | tf_op jit(solution)/shard_map/all_to_all | solution.py:295
  27.5 3.8 %copy-start.6 = (bf16[2,128,512]{2,1,0:T(8,128)(2,1)}, bf16[2,128,512]{2,1,0:T(8,128)(2,1)S(1)}, u32[]{:S(2)}) copy-start(bf16[2,128,512]{2,1,0:T(8,128)(2,1)S(1)} %collective-permute-done.2.refs_2_) | copy-start | bytes 786436
  27.5 3.7 %copy-start.5 = (bf16[2,128,512]{2,1,0:T(8,128)(2,1)}, bf16[2,128,512]{2,1,0:T(8,128)(2,1)S(1)}, u32[]{:S(2)}) copy-start(bf16[2,128,512]{2,1,0:T(8,128)(2,1)S(1)} %collective-permute-done.1.refs_1_) | copy-start | bytes 786436
  27.6 3.6 %collective-permute-start.3 = (bf16[3,2,128,256]{3,2,1,0:T(8,128)(2,1)S(1)}, bf16[3,2,128,256]{3,2,1,0:T(8,128)(2,1)S(1)}, u32[]{:S(2)}, u32[]{:S(2)}) collective-permute-start(bf16[3,2,128,256]{3,2,1,0:T(8,128)(2,1)S(1)} %pad_maximum_fusion.2), channel_id=1, source_target_pairs={{0,1},{1,0},{2,3},{3,2},{4,5},{5,4},{6,7},{7,6},{8,9},{9,8},{10,11... | collective-permute-start | bytes 1179656 | tf_op jit(solution)/shard_map/ppermute | solution.py:292
  31.2 0.8 copy-start.9
  41.1 0.8 copy-start.3
  50.5 30.5 %all-to-all-start.1 = ((bf16[64,24,128]{2,1,0:T(8,128)(2,1)}), bf16[64,24,128]{2,1,0:T(8,128)(2,1)S(1)}, u32[]{:S(2)}, u32[]{:S(2)}) async-start(bf16[64,24,128]{2,1,0:T(8,128)(2,1)} %bitcast.35), calls=%async_computation.1 | async-start | bytes 786432 | tf_op jit(solution)/shard_map/all_to_all | solution.py:295
  78.3 16.1 %copy-start = (f32[2,256,256]{2,1,0:T(8,128)S(1)}, f32[2,256,256]{2,1,0:T(8,128)}, u32[]{:S(2)}) copy-start(f32[2,256,256]{2,1,0:T(8,128)} %get-tuple-element.18) | copy-start | bytes 1572868
  78.3 16.1 %collective-permute-start.5 = (bf16[2,256,256]{2,1,0:T(8,128)(2,1)}, bf16[2,256,256]{2,1,0:T(8,128)(2,1)S(1)}, u32[]{:S(2)}, u32[]{:S(2)}) collective-permute-start(bf16[2,256,256]{2,1,0:T(8,128)(2,1)} %get-tuple-element.17), channel_id=1, source_target_pairs={{4,0},{5,1},{6,2},{7,3},{8,4},{9,5},{10,6},{11,7},{12,8},{13,9},{1... | collective-permute-start | bytes 786440 | tf_op jit(solution)/shard_map/ppermute | solution.py:289
  79.7 14.6 %collective-permute-start.4 = (bf16[2,256,256]{2,1,0:T(8,128)(2,1)}, bf16[2,256,256]{2,1,0:T(8,128)(2,1)S(1)}, u32[]{:S(2)}, u32[]{:S(2)}) collective-permute-start(bf16[2,256,256]{2,1,0:T(8,128)(2,1)} %get-tuple-element.16), channel_id=1, source_target_pairs={{2,0},{3,1},{4,2},{5,3},{6,4},{7,5},{8,6},{9,7},{10,8},{11,9},{12,... | collective-permute-start | bytes 786440 | tf_op jit(solution)/shard_map/ppermute | solution.py:289
  81.9 24.0 %all-to-all-start.2 = ((bf16[32,2,24,128]{3,2,1,0:T(8,128)(2,1)}), bf16[32,2,24,128]{3,2,1,0:T(8,128)(2,1)S(1)}, u32[]{:S(2)}, u32[]{:S(2)}) async-start(bf16[32,2,24,128]{3,2,1,0:T(8,128)(2,1)} %shard_map.122), calls=%async_computation.2 | async-start | bytes 786432 | tf_op jit(solution)/shard_map/all_to_all | solution.py:295
  94.5 5.3 %collective-permute-start.6 = (bf16[2,128,256]{2,1,0:T(8,128)(2,1)S(1)}, bf16[2,128,256]{2,1,0:T(8,128)(2,1)S(1)}, u32[]{:S(2)}, u32[]{:S(2)}) collective-permute-start(bf16[2,128,256]{2,1,0:T(8,128)(2,1)S(1)} %slice.17), channel_id=1, source_target_pairs={{0,1},{1,0},{2,3},{3,2},{4,5},{5,4},{6,7},{7,6},{8,9},{9,8},{10,11... | collective-permute-start | bytes 393224 | tf_op jit(solution)/shard_map/ppermute | solution.py:292

commit v7 on v5

--- a/solution.py
+++ b/solution.py
@@ -63,11 +63,27 @@
     )
 
 
-def token_stats_kernel(core_ref, mine_ref, others_ref, *refs):
-    window, (bias_ref, stat_ref) = refs[:4], refs[4:]
-    core = core_ref[0]
+def masks(where_ref, first_ref, toks):
+    down = lax.broadcasted_iota(jnp.int32, (toks, toks), 0)
+    along = lax.broadcasted_iota(jnp.int32, (toks, toks), 1)
+    found = []
+    for chunk in range(2):
+        at = 1 + chunk * 6
+        here = along + where_ref[at] * toks
+        found.append([])
+        for b in range(5):
+            key = down + where_ref[at + 1 + b] * toks
+            seen = (key >= first_ref[chunk]) & (key <= here)
+            found[-1].append(jnp.where(seen, 0.0, -1e30).astype(F32))
+    return found
+
+
+def token_stats_kernel(where_ref, mine_ref, others_ref, *refs):
+    window, (first_ref, stat_ref) = refs[:4], refs[4:]
+    core = where_ref[0]
     toks = mine_ref.shape[1]
-    blocks = bias_ref.shape[1] // toks
+    hidden = masks(where_ref, first_ref, toks)
+    blocks = len(hidden[0])
     found, heads = units(mine_ref, others_ref)
     for h, chunk, read in found:
         keys, values = (windows(core, h, which, *window)[chunk] for which in range(2))
@@ -86,7 +102,7 @@
             top = total = dot = None
             for b in range(blocks):
                 rows = slice(b * toks, (b + 1) * toks)
-                s = (s_all[rows] + bias_ref[chunk, rows, :]).reshape(toks // 8, 8, toks)
+                s = (s_all[rows] + hidden[chunk][b]).reshape(toks // 8, 8, toks)
                 dp = dp_all[rows].reshape(toks // 8, 8, toks)
                 new = jnp.max(s, axis=0)
                 new = new if top is None else jnp.maximum(top, new)
@@ -157,17 +173,18 @@
                     out_ref[2 * which + h, part] = rows.astype(BF16)
 
 
-def token_grads_kernel(core_ref, mine_ref, others_ref, *refs):
-    window, (bias_ref, full_ref, home_ref, one_ref, two_ref) = refs[:4], refs[4:]
-    core = core_ref[0]
+def token_grads_kernel(where_ref, mine_ref, others_ref, *refs):
+    window, (first_ref, full_ref, home_ref, one_ref, two_ref) = refs[:4], refs[4:]
+    core = where_ref[0]
     even = core == 0
     toks = mine_ref.shape[1]
+    hidden = masks(where_ref, first_ref, toks)
     found, heads = units(mine_ref, others_ref)
     grads = {}
     for h, chunk, read in found:
         keys, values = (windows(core, h, which, *window)[chunk] for which in range(2))
         q, g = read(0, 0, heads), read(1, 0, heads)
-        bias = jnp.concatenate([bias_ref[chunk]] * heads, axis=1)
+        bias = jnp.concatenate([jnp.concatenate(hidden[chunk], axis=0)] * heads, axis=1)
         s = lax.dot_general(keys, q, NT, preferred_element_type=F32) + bias
         dp = lax.dot_general(values, g, NT, preferred_element_type=F32)
         p = jnp.exp2(s * TO_LOG2 - joined(full_ref, 0, h, chunk))
@@ -191,34 +208,6 @@
             two_ref[which, toks:, columns] = (b[3] + jnp.where(even, a[4], zero)).astype(BF16)
 
 
-def halves_kernel(core_ref, q_ref, g_ref, mine_ref, theirs_ref, sems):
-    width = mine_ref.shape[2]
-    copies = []
-    for which, ref in enumerate((q_ref, g_ref)):
-        for n, (out, side) in enumerate(((theirs_ref, 1 - core_ref[0]), (mine_ref, core_ref[0]))):
-            columns = pl.ds(pl.multiple_of(side * width, HD), width)
-            copies.append(
-                pltpu.make_async_copy(ref.at[:, columns], out.at[which], sems.at[which, n])
-            )
-    for copy in copies:
-        copy.start()
-    for copy in copies:
-        copy.wait()
-
-
-def halves(cores, q, g):
-    half = jax.ShapeDtypeStruct((2, q.shape[0], q.shape[1] // 2), q.dtype)
-    anywhere = pl.BlockSpec(memory_space=pl.ANY)
-    return pl.pallas_call(
-        halves_kernel,
-        in_specs=[pl.BlockSpec(memory_space=pltpu.SMEM), anywhere, anywhere],
-        out_specs=[pl.BlockSpec(memory_space=pltpu.VMEM), anywhere],
-        out_shape=[half, half],
-        scratch_shapes=[pltpu.SemaphoreType.DMA((2, 2))],
-        cost_estimate=pl.CostEstimate(flops=0, bytes_accessed=4 * q.size * 2, transcendentals=0),
-    )(cores, q, g)
-
-
 def spread_kernel(got_ref, out_ref):
     count, cores = out_ref.shape[:2]
     for c in range(cores):
@@ -255,7 +244,7 @@
     )(*ins)
 
 
-def layout(lengths, tenants, slots, block, shards, toks):
+def layout(lengths, tenants, slots, block, toks):
     ends = jnp.cumsum(lengths)
     slot_of = jnp.sum(
         jnp.where(tenants[:, None] == jnp.arange(slots.shape[0])[None, :], slots[None, :], 0), axis=1
@@ -265,9 +254,7 @@
     pick = doc[None, :] == jnp.arange(lengths.shape[0])[:, None]
     first = jnp.sum(jnp.where(pick, (ends - lengths)[:, None], 0), axis=0)
     slot = jnp.sum(jnp.where(pick, slot_of[:, None], 0), axis=0)
-    key = jnp.concatenate([s * toks + jnp.arange(toks, dtype=jnp.int32) for s in shards])
-    ok = (key[:, None] >= first[None, :]) & (key[:, None] <= here[None, :])
-    return jnp.where(ok, 0.0, -1e30).astype(F32), slot[None, :].astype(jnp.int32)
+    return first[None, :].astype(jnp.int32), slot[None, :].astype(jnp.int32)
 
 
 def per_device(
@@ -278,7 +265,6 @@
     count = parts * 2
     index, core = lax.axis_index(SEQ), lax.axis_index("core").astype(jnp.int32)
     even = core == 0
-    cores = core[None]
 
     def shift(x, steps):
         pairs = [(i, i + 2 * steps) for i in range(count) if 0 <= i + 2 * steps < count]
@@ -290,9 +276,9 @@
     def exchange(x, axis):
         return lax.all_to_all(x, axis, split_axis=0, concat_axis=0, tiled=True)
 
-    def other_half(x):
+    def half(x, which):
         size = x.shape[-1] // 2
-        return lax.dynamic_slice_in_dim(x, (1 - core) * size, size, x.ndim - 1)
+        return lax.dynamic_slice_in_dim(x, which * size, size, x.ndim - 1)
 
     own = jnp.stack([keys, values])
     one, two = shift(own, 1), shift(own, 2)
@@ -300,24 +286,24 @@
     pref = pref.reshape(2, -1, 2, KVH * HD // 2).transpose(2, 0, 1, 3)
     pref = jnp.broadcast_to(pref[None], (parts, *pref.shape)).reshape(count, *pref.shape[1:])
     pref = exchange(pref, SEQ)
-    mine, theirs = halves(cores, queries, grad_out)
-    others = swap(theirs)
-    cross = swap(jnp.stack([other_half(own), other_half(one), other_half(two)]))
+    others = swap(jnp.stack([half(queries, 1 - core), half(grad_out, 1 - core)]))
+    cross = swap(jnp.stack([half(x, 1 - core) for x in (own, one, two)]))
 
     facing = index ^ 1
     near, far = jnp.where(even, index - 1, index - 3), jnp.where(even, index - 3, index - 1)
     docs = (doc_lengths[0], doc_tenants[0], tenant_slots)
-    shards = [index, index - 2, index - 4, near, far]
-    bias0, slot0 = layout(*docs, index, shards, toks)
+    first0, slot0 = layout(*docs, index, toks)
+    first1, slot1 = layout(*docs, facing, toks)
+    first, slot = jnp.stack([first0, first1]), jnp.stack([slot0, slot1])
     last = jnp.where(even, index, index - 4)
-    shards = [facing, index - 2, facing - 2, facing - 4, last]
-    bias1, slot1 = layout(*docs, facing, shards, toks)
-    bias, slot = jnp.stack([bias0, bias1]), jnp.stack([slot0, slot1])
-
-    heads = [mine, others]
+    where = [core, index, index, index - 2, index - 4, near, far]
+    where += [facing, facing, index - 2, facing - 2, facing - 4, last]
+    where = jnp.stack(where).astype(jnp.int32)
+
+    heads = [jnp.stack([half(queries, core), half(grad_out, core)]), others]
     shape = (KVH // 2, 2, HQ // KVH, toks)
-    work = queries.size // HD * bias.shape[1]
-    window = [cores, *heads, own, one, two, cross, bias]
+    work = queries.size // HD * 5 * toks
+    window = [where, *heads, own, one, two, cross, first]
     (stats,) = call(
         token_stats_kernel,
         flops=4 * HD * work,
@@ -345,17 +331,18 @@
         outs=[jax.ShapeDtypeStruct(wide, kind) for kind in (F32, BF16, BF16)],
     )
 
+    back1, back2 = shift(back1, -1), shift(back2, -2)
+
     rows = exchange(rows.reshape(-1, *rows.shape[2:]), ("x", *SEQ))
     spread = jax.ShapeDtypeStruct((lax.axis_size(DP), 2, *rows.shape[1:]), BF16)
     (rows,) = call(spread_kernel, flops=rows.size, exps=0, ins=[rows], outs=[spread])
-    rows, home, _, _ = lax.optimization_barrier((rows, home, back1, back2))
+    rows, home = lax.optimization_barrier((rows, home))
     rows = exchange(rows, DP).reshape(lax.axis_size("y"), 2, 2, *rows.shape[1:])
     full = jax.ShapeDtypeStruct((prefix_keys.shape[0], KVH * HD), F32)
     pref_key_grads, pref_value_grads = call(
         finish_kernel, flops=rows.size, exps=0, ins=[rows], outs=[full, full]
     )
 
-    back1, back2 = shift(back1, -1), shift(back2, -2)
     grads = (home + back1.astype(F32) + back2.astype(F32)).astype(BF16)
     mine, theirs = grads[:, :toks], swap(grads[:, toks:])
     grads = jnp.concatenate(

time: 147 us -> 101 us (0.69)
  Pallas kernels: 76.5 us -> 27.2 us
  other arithmetic: 2.91 us -> 5.32 us
  local copies, waits for them, and re-layouts: 3.73 us -> 6.13 us
    pallas_call x1 -> x0, Pallas kernels: 49.9 us -> none  [halves(): pl.pallas_call(halves_kernel, in_specs=[pl.BlockSpec(memory_space=pltpu.S...]
    ppermute x4, waiting for transfers between devices: 2.51 us -> 8.67 us  [shift(): return lax.ppermute(x, SEQ, pairs)]
    all_to_all x3, waiting for transfers between devices: 8.08 us -> 3.03 us  [exchange(): return lax.all_to_all(x, axis, split_axis=0, concat_axis=0, tiled=True)]
    another operation x2 -> x4, local copies, waits for them, and re-layouts: 0.04 us -> 3.43 us  [the longest x1 3.3 us: per_device(): jnp.stack([half(queries, 1 - core), half(grad_out, 1 - core)])]
    another operation x5 -> x6, other arithmetic: 0.29 us -> 3.05 us  [the longest x1 1.52 us: per_device(): heads = [jnp.stack([half(queries, core), half(grad_out, core)]), others]]
  transfers between devices with their start and end apart: 10 -> 10, of which waited for: 6 -> 4; matrix products, arithmetic and copies ran while one was open for 2% -> 9% of each run, Pallas kernels for 47% -> 19%
where the time goes in v7:
time: 101 us; the launch traced here: 99.4 us
  starting transfers between devices  47 us (47%)
  Pallas kernels  27.2 us (27%)
  waiting for transfers between devices  12.7 us (13%)
  local copies, waits for them, and re-layouts  6.13 us (6%)
  other arithmetic  5.32 us (5%)
    pallas_call x5, Pallas kernels, call(): pl.pallas_call(kernel, in_specs=[scalar if x.ndim == 1 else space for x i...  27.2 us
    all_to_all x3, starting transfers between devices, exchange(): return lax.all_to_all(x, axis, split_axis=0, concat_axis=0, tiled=True)  25.4 us
    ppermute x4, starting transfers between devices, shift(): return lax.ppermute(x, SEQ, pairs)  13.2 us
    ppermute x4, waiting for transfers between devices, shift(): return lax.ppermute(x, SEQ, pairs)  8.67 us
    ppermute x3, starting transfers between devices, swap(): return lax.ppermute(x, SEQ, [(i, i ^ 1) for i in range(count)])  8.35 us
    another operation x1, local copies, waits for them, and re-layouts, per_device(): jnp.stack([half(queries, 1 - core), half(grad_out, 1 - core)])  3.3 us
    all_to_all x3, waiting for transfers between devices, exchange(): return lax.all_to_all(x, axis, split_axis=0, concat_axis=0, tiled=True)  3.03 us
  transfers between devices with their start and end apart: 10, of which 4 were waited for; matrix products, arithmetic and copies ran while one was open for 9% of the time, Pallas kernels for 19%

profile of v7, /device:TPU:1, one launch (start us, length us, event | category | flops | bytes accessed | tf_op | source)
XLA Modules:
  0.0 99.4 jit_solution(12571965872751803254)
XLA Ops:
  0.6 1.0 %pad_maximum_fusion.3.refs_0_ = bf16[2,128,512]{2,1,0:T(8,128)(2,1)S(1)} fusion(bf16[1,128,512]{2,1,0:T(8,128)(2,1)} %bitcast.46, bf16[1,128,512]{2,1,0:T(8,128)(2,1)} %bitcast.48), kind=kLoop, calls=%fused_computation.9 | loop fusion | flops 131072 | bytes 524288 | tf_op jit(solution)/shard_map/stack | solution.py:283
  1.6 6.7 %collective-permute-start.2 = (bf16[2,128,512]{2,1,0:T(8,128)(2,1)S(1)}, bf16[2,128,512]{2,1,0:T(8,128)(2,1)S(1)}, u32[]{:S(2)}, u32[]{:S(2)}) collective-permute-start(bf16[2,128,512]{2,1,0:T(8,128)(2,1)S(1)} %pad_maximum_fusion.3.refs_0_), channel_id=1, source_target_pairs={{0,4},{1,5},{2,6},{3,7},{4,8},{5,9},{6,10},{7,11},{8,12},{9,13},{1... | collective-permute-start | bytes 786440 | tf_op jit(solution)/shard_map/ppermute | solution.py:271
  8.3 4.0 %collective-permute-start.1 = (bf16[2,128,512]{2,1,0:T(8,128)(2,1)S(1)}, bf16[2,128,512]{2,1,0:T(8,128)(2,1)S(1)}, u32[]{:S(2)}, u32[]{:S(2)}) collective-permute-start(bf16[2,128,512]{2,1,0:T(8,128)(2,1)S(1)} %pad_maximum_fusion.3.refs_0_), channel_id=1, source_target_pairs={{0,2},{1,3},{2,4},{3,5},{4,6},{5,7},{6,8},{7,9},{8,10},{9,11},{10,... | collective-permute-start | bytes 786440 | tf_op jit(solution)/shard_map/ppermute | solution.py:271
  12.3 3.3 %dynamic-slice_bitcast_fusion = (bf16[1,128,3072]{2,1,0:T(8,128)(2,1)S(1)}, bf16[1,128,3072]{2,1,0:T(8,128)(2,1)}, bf16[1,128,3072]{2,1,0:T(8,128)(2,1)}, bf16[1,128,3072]{2,1,0:T(8,128)(2,1)S(1)}) fusion(bf16[128,6144]{1,0:T(8,128)(2,1)} %param.12, s32[]{:T(128)S(6)} %select_n.55, s32[]{:T(128)S(6)} %select_n.54, bf16[128,6144]{1,0:T(8,128)(2,1)} %param.9), kind=kLoop, calls=%fused_computation.2 | loop fusion | bytes 6291464 | tf_op jit(solution)/shard_map/stack | solution.py:289
  15.6 0.0 copy-start.6
  15.6 0.0 copy-start.7
  15.6 0.0 copy-start.8
  15.6 0.0 copy-start.9
  15.6 0.0 copy-start.10
  15.7 1.3 %pad_maximum_fusion.1 = bf16[2,128,3072]{2,1,0:T(8,128)(2,1)} fusion(bf16[1,128,3072]{2,1,0:T(8,128)(2,1)S(1)} %get-tuple-element.30, bf16[1,128,3072]{2,1,0:T(8,128)(2,1)S(1)} %get-tuple-element.39), kind=kLoop, calls=%fused_computation.1 | loop fusion | flops 786432 | bytes 3145728 | tf_op jit(solution)/shard_map/stack | solution.py:289
  16.9 0.0 copy-start.4
  16.9 0.0 copy-start.5
  16.9 3.3 %collective-permute-start = (bf16[2,128,3072]{2,1,0:T(8,128)(2,1)}, bf16[2,128,3072]{2,1,0:T(8,128)(2,1)}, u32[]{:S(2)}, u32[]{:S(2)}) collective-permute-start(bf16[2,128,3072]{2,1,0:T(8,128)(2,1)} %pad_maximum_fusion.1), channel_id=1, source_target_pairs={{0,1},{1,0},{2,3},{3,2},{4,5},{5,4},{6,7},{7,6},{8,9},{9,8},{10,11... | collective-permute-start | bytes 4718600 | tf_op jit(solution)/shard_map/ppermute | solution.py:274
  20.2 0.0 copy-done.6
  20.2 0.0 copy-done.7
  20.3 0.1 maximum_bitcast_fusion
  20.4 0.8 broadcast_in_dim.64
  21.2 7.7 %all-to-all-start = ((bf16[16,2,24,256]{3,2,1,0:T(8,128)(2,1)}), bf16[16,2,24,256]{3,2,1,0:T(8,128)(2,1)S(1)}, u32[]{:S(2)}, u32[]{:S(2)}) async-start(bf16[16,2,24,256]{3,2,1,0:T(8,128)(2,1)} %bitcast.5), calls=%async_computation | async-start | bytes 786432 | tf_op jit(solution)/shard_map/all_to_all | solution.py:277
  28.9 0.0 copy-done.8
  28.9 0.2 reduce-window.7
  29.1 0.1 convert_reduce_fusion.1
  29.2 0.0 copy-done.9
  29.2 0.0 copy-done.10
  29.2 0.2 select_reduce_fusion.4
  29.3 0.1 select_reduce_fusion.3
  29.4 0.0 copy-done.4
  29.4 0.0 copy-done.5
  29.5 0.0 collective-permute-done.2.refs_2_
  29.5 0.0 collective-permute-done.1.refs_1_
  29.6 2.0 %collective-permute-start.3 = (bf16[3,2,128,256]{3,2,1,0:T(8,128)(2,1)S(1)}, bf16[3,2,128,256]{3,2,1,0:T(8,128)(2,1)S(1)}, u32[]{:S(2)}, u32[]{:S(2)}) collective-permute-start(bf16[3,2,128,256]{3,2,1,0:T(8,128)(2,1)S(1)} %pad_maximum_fusion.2), channel_id=1, source_target_pairs={{0,1},{1,0},{2,3},{3,2},{4,5},{5,4},{6,7},{7,6},{8,9},{9,8},{10,11... | collective-permute-start | bytes 1179656 | tf_op jit(solution)/shard_map/ppermute | solution.py:274
  31.7 0.1 stack.110.where_ref
  31.8 1.5 %pad_maximum_fusion.mine_ref = bf16[2,128,3072]{2,1,0:T(8,128)(2,1)S(1)} fusion(bf16[1,128,3072]{2,1,0:T(8,128)(2,1)} %get-tuple-element.31, bf16[1,128,3072]{2,1,0:T(8,128)(2,1)} %get-tuple-element.38), kind=kLoop, calls=%fused_computation | loop fusion | flops 786432 | bytes 3145728 | tf_op jit(solution)/shard_map/stack | solution.py:303
  33.3 0.0 collective-permute-done.3.refs_3_
  33.3 0.0 copy-start
  33.3 0.0 collective-permute-done.others_ref
  33.3 7.5 %shard_map.120.stat_ref = f32[3,2,2,12,128]{4,3,2,1,0:T(8,128)S(1)} custom-call(s32[13]{0:T(128)S(1)} %stack.110.where_ref, bf16[2,128,3072]{2,1,0:T(8,128)(2,1)S(1)} %pad_maximum_fusion.mine_ref, bf16[2,128,3072]{2,1,0:T(8,128)(2,1)} %collective-permute-done.others_ref, bf16[2,128,512]{2,1,0:T(8,128)(2,1)S(1)} %pad_maximum_fusion.3.refs_0_, ...), custom_call_target="tpu_custom_call" | custom-call | flops 2013265920 | bytes 6291456 | tf_op jit(solution)/shard_map/pallas_call | solution.py:237
  40.8 0.0 copy-done
  40.8 2.6 %all-to-all-done.pref_ref = bf16[16,2,24,256]{3,2,1,0:T(8,128)(2,1)S(1)} async-done(((bf16[16,2,24,256]{3,2,1,0:T(8,128)(2,1)}), bf16[16,2,24,256]{3,2,1,0:T(8,128)(2,1)S(1)}, u32[]{:S(2)}, u32[]{:S(2)}) %all-to-all-start) | async-done | bytes 393248 | tf_op jit(solution)/shard_map/all_to_all | solution.py:277
  43.4 7.3 %shard_map.121 = (f32[2,2,2,12,128]{4,3,2,1,0:T(8,128)S(1)}, bf16[4,16,24,128]{3,2,1,0:T(8,128)(2,1)}) custom-call(bf16[2,128,3072]{2,1,0:T(8,128)(2,1)S(1)} %pad_maximum_fusion.mine_ref, bf16[2,128,3072]{2,1,0:T(8,128)(2,1)} %collective-permute-done.others_ref, bf16[16,2,24,256]{3,2,1,0:T(8,128)(2,1)S(1)} %all-to-all-done.pref_ref, ...), custom_call_target="tpu_custom_call" | custom-call | flops 2415919104 | bytes 6291456 | tf_op jit(solution)/shard_map/pallas_call | solution.py:237
  50.7 0.0 copy-start.2
  50.7 7.8 %all-to-all-start.1 = ((bf16[64,24,128]{2,1,0:T(8,128)(2,1)}), bf16[64,24,128]{2,1,0:T(8,128)(2,1)S(1)}, u32[]{:S(2)}, u32[]{:S(2)}) async-start(bf16[64,24,128]{2,1,0:T(8,128)(2,1)} %bitcast.29), calls=%async_computation.1 | async-start | bytes 786432 | tf_op jit(solution)/shard_map/all_to_all | solution.py:277
  58.5 0.0 copy-done.2
  58.5 0.0 copy-start.1
  58.5 1.0 copy-done.1
  59.5 0.0 copy-start.3
  59.5 0.8 copy-done.3
  60.4 11.0 %shard_map.123 = (f32[2,256,256]{2,1,0:T(8,128)S(1)}, bf16[2,256,256]{2,1,0:T(8,128)(2,1)}, bf16[2,256,256]{2,1,0:T(8,128)(2,1)S(1)}) custom-call(s32[13]{0:T(128)S(1)} %stack.110.where_ref, bf16[2,128,3072]{2,1,0:T(8,128)(2,1)S(1)} %pad_maximum_fusion.mine_ref, bf16[2,128,3072]{2,1,0:T(8,128)(2,1)} %collective-permute-done.others_ref, ...), custom_call_target="tpu_custom_call" | custom-call | flops 4026531840 | bytes 6291456 | tf_op jit(solution)/shard_map/pallas_call | solution.py:237
  71.4 1.3 %collective-permute-start.4 = (bf16[2,256,256]{2,1,0:T(8,128)(2,1)}, bf16[2,256,256]{2,1,0:T(8,128)(2,1)S(1)}, u32[]{:S(2)}, u32[]{:S(2)}) collective-permute-start(bf16[2,256,256]{2,1,0:T(8,128)(2,1)} %get-tuple-element.17), channel_id=1, source_target_pairs={{2,0},{3,1},{4,2},{5,3},{6,4},{7,5},{8,6},{9,7},{10,8},{11,9},{12,... | collective-permute-start | bytes 786440 | tf_op jit(solution)/shard_map/ppermute | solution.py:271
  72.7 1.3 %collective-permute-start.5 = (bf16[2,256,256]{2,1,0:T(8,128)(2,1)S(1)}, bf16[2,256,256]{2,1,0:T(8,128)(2,1)S(1)}, u32[]{:S(2)}, u32[]{:S(2)}) collective-permute-start(bf16[2,256,256]{2,1,0:T(8,128)(2,1)S(1)} %get-tuple-element.18), channel_id=1, source_target_pairs={{4,0},{5,1},{6,2},{7,3},{8,4},{9,5},{10,6},{11,7},{12,8},{13,9},{1... | collective-permute-start | bytes 786440 | tf_op jit(solution)/shard_map/ppermute | solution.py:271
  74.0 0.0 all-to-all-done.1.got_ref
  74.0 0.8 shard_map.122
  74.8 9.9 %all-to-all-start.2 = ((bf16[32,2,24,128]{3,2,1,0:T(8,128)(2,1)}), bf16[32,2,24,128]{3,2,1,0:T(8,128)(2,1)S(1)}, u32[]{:S(2)}, u32[]{:S(2)}) async-start(bf16[32,2,24,128]{3,2,1,0:T(8,128)(2,1)} %shard_map.122), calls=%async_computation.2 | async-start | bytes 786432 | tf_op jit(solution)/shard_map/all_to_all | solution.py:277
  84.7 0.0 collective-permute-done.4
  84.7 8.7 %collective-permute-done.5 = bf16[2,256,256]{2,1,0:T(8,128)(2,1)S(1)} collective-permute-done((bf16[2,256,256]{2,1,0:T(8,128)(2,1)S(1)}, bf16[2,256,256]{2,1,0:T(8,128)(2,1)S(1)}, u32[]{:S(2)}, u32[]{:S(2)}) %collective-permute-start.5) | collective-permute-done | bytes 262176 | tf_op jit(solution)/shard_map/ppermute | solution.py:271
  93.4 0.1 add_convert_fusion
  93.5 3.1 %collective-permute-start.6 = (bf16[2,128,256]{2,1,0:T(8,128)(2,1)S(1)}, bf16[2,128,256]{2,1,0:T(8,128)(2,1)S(1)}, u32[]{:S(2)}, u32[]{:S(2)}) collective-permute-start(bf16[2,128,256]{2,1,0:T(8,128)(2,1)S(1)} %slice.17), channel_id=1, source_target_pairs={{0,1},{1,0},{2,3},{3,2},{4,5},{5,4},{6,7},{7,6},{8,9},{9,8},{10,11... | collective-permute-start | bytes 393224 | tf_op jit(solution)/shard_map/ppermute | solution.py:274
  96.5 1.0 collective-permute-done.6
  97.5 0.7 fusion.4
  98.3 0.4 all-to-all-done.2
  98.7 0.7 shard_map.124
  (13 shorter events, 0.2 us)
Async XLA Ops:
  1.6 27.8 %collective-permute-start.2 = (bf16[2,128,512]{2,1,0:T(8,128)(2,1)S(1)}, bf16[2,128,512]{2,1,0:T(8,128)(2,1)S(1)}, u32[]{:S(2)}, u32[]{:S(2)}) collective-permute-start(bf16[2,128,512]{2,1,0:T(8,128)(2,1)S(1)} %pad_maximum_fusion.3.refs_0_), channel_id=1, source_target_pairs={{0,4},{1,5},{2,6},{3,7},{4,8},{5,9},{6,10},{7,11},{8,12},{9,13},{1... | collective-permute-start | bytes 786440 | tf_op jit(solution)/shard_map/ppermute | solution.py:271
  8.3 21.2 %collective-permute-start.1 = (bf16[2,128,512]{2,1,0:T(8,128)(2,1)S(1)}, bf16[2,128,512]{2,1,0:T(8,128)(2,1)S(1)}, u32[]{:S(2)}, u32[]{:S(2)}) collective-permute-start(bf16[2,128,512]{2,1,0:T(8,128)(2,1)S(1)} %pad_maximum_fusion.3.refs_0_), channel_id=1, source_target_pairs={{0,2},{1,3},{2,4},{3,5},{4,6},{5,7},{6,8},{7,9},{8,10},{9,11},{10,... | collective-permute-start | bytes 786440 | tf_op jit(solution)/shard_map/ppermute | solution.py:271
  15.6 4.6 %copy-start.6 = (bf16[24,512]{1,0:T(8,128)(2,1)S(1)}, bf16[24,512]{1,0:T(8,128)(2,1)}, u32[]{:S(2)}) copy-start(bf16[24,512]{1,0:T(8,128)(2,1)} %param.13) | copy-start | bytes 73732
  15.6 4.6 %copy-start.7 = (bf16[24,512]{1,0:T(8,128)(2,1)S(1)}, bf16[24,512]{1,0:T(8,128)(2,1)}, u32[]{:S(2)}) copy-start(bf16[24,512]{1,0:T(8,128)(2,1)} %param.14) | copy-start | bytes 73732
  15.6 13.2 %copy-start.8 = (s32[1,8]{1,0:T(1,128)S(1)}, s32[1,8]{1,0:T(1,128)}, u32[]{:S(2)}) copy-start(s32[1,8]{1,0:T(1,128)} %param.15) | copy-start | bytes 100
  15.6 13.5 %copy-start.9 = (s32[6]{0:T(128)S(1)}, s32[6]{0:T(128)}, u32[]{:S(2)}) copy-start(s32[6]{0:T(128)} %param.17) | copy-start | bytes 76
  15.6 13.5 %copy-start.10 = (s32[1,8]{1,0:T(1,128)S(1)}, s32[1,8]{1,0:T(1,128)}, u32[]{:S(2)}) copy-start(s32[1,8]{1,0:T(1,128)} %param.16) | copy-start | bytes 100
  16.9 12.5 %copy-start.4 = (bf16[128,512]{1,0:T(8,128)(2,1)S(1)}, bf16[128,512]{1,0:T(8,128)(2,1)}, u32[]{:S(2)}) copy-start(bf16[128,512]{1,0:T(8,128)(2,1)} %param.11) | copy-start | bytes 393220
  16.9 12.5 %copy-start.5 = (bf16[128,512]{1,0:T(8,128)(2,1)S(1)}, bf16[128,512]{1,0:T(8,128)(2,1)}, u32[]{:S(2)}) copy-start(bf16[128,512]{1,0:T(8,128)(2,1)} %param.10) | copy-start | bytes 393220
  16.9 16.4 %collective-permute-start = (bf16[2,128,3072]{2,1,0:T(8,128)(2,1)}, bf16[2,128,3072]{2,1,0:T(8,128)(2,1)}, u32[]{:S(2)}, u32[]{:S(2)}) collective-permute-start(bf16[2,128,3072]{2,1,0:T(8,128)(2,1)} %pad_maximum_fusion.1), channel_id=1, source_target_pairs={{0,1},{1,0},{2,3},{3,2},{4,5},{5,4},{6,7},{7,6},{8,9},{9,8},{10,11... | collective-permute-start | bytes 4718600 | tf_op jit(solution)/shard_map/ppermute | solution.py:274
  21.2 22.2 %all-to-all-start = ((bf16[16,2,24,256]{3,2,1,0:T(8,128)(2,1)}), bf16[16,2,24,256]{3,2,1,0:T(8,128)(2,1)S(1)}, u32[]{:S(2)}, u32[]{:S(2)}) async-start(bf16[16,2,24,256]{3,2,1,0:T(8,128)(2,1)} %bitcast.5), calls=%async_computation | async-start | bytes 786432 | tf_op jit(solution)/shard_map/all_to_all | solution.py:277
  29.6 3.7 %collective-permute-start.3 = (bf16[3,2,128,256]{3,2,1,0:T(8,128)(2,1)S(1)}, bf16[3,2,128,256]{3,2,1,0:T(8,128)(2,1)S(1)}, u32[]{:S(2)}, u32[]{:S(2)}) collective-permute-start(bf16[3,2,128,256]{3,2,1,0:T(8,128)(2,1)S(1)} %pad_maximum_fusion.2), channel_id=1, source_target_pairs={{0,1},{1,0},{2,3},{3,2},{4,5},{5,4},{6,7},{7,6},{8,9},{9,8},{10,11... | collective-permute-start | bytes 1179656 | tf_op jit(solution)/shard_map/ppermute | solution.py:274
  33.3 7.5 %copy-start = (bf16[3,2,128,256]{3,2,1,0:T(8,128)(2,1)}, bf16[3,2,128,256]{3,2,1,0:T(8,128)(2,1)S(1)}, u32[]{:S(2)}) copy-start(bf16[3,2,128,256]{3,2,1,0:T(8,128)(2,1)S(1)} %collective-permute-done.3.refs_3_) | copy-start | bytes 1179652
  50.7 7.8 %copy-start.2 = (f32[2,2,2,12,128]{4,3,2,1,0:T(8,128)}, f32[2,2,2,12,128]{4,3,2,1,0:T(8,128)S(1)}, u32[]{:S(2)}) copy-start(f32[2,2,2,12,128]{4,3,2,1,0:T(8,128)S(1)} %get-tuple-element.14.refs_5_) | copy-start | bytes 147460
  50.7 23.3 %all-to-all-start.1 = ((bf16[64,24,128]{2,1,0:T(8,128)(2,1)}), bf16[64,24,128]{2,1,0:T(8,128)(2,1)S(1)}, u32[]{:S(2)}, u32[]{:S(2)}) async-start(bf16[64,24,128]{2,1,0:T(8,128)(2,1)} %bitcast.29), calls=%async_computation.1 | async-start | bytes 786432 | tf_op jit(solution)/shard_map/all_to_all | solution.py:277
  58.5 1.0 %copy-start.1 = (bf16[3,2,128,256]{3,2,1,0:T(8,128)(2,1)S(1)}, bf16[3,2,128,256]{3,2,1,0:T(8,128)(2,1)}, u32[]{:S(2)}) copy-start(bf16[3,2,128,256]{3,2,1,0:T(8,128)(2,1)} %copy-done) | copy-start | bytes 1179652
  59.5 0.8 copy-start.3
  71.4 13.3 %collective-permute-start.4 = (bf16[2,256,256]{2,1,0:T(8,128)(2,1)}, bf16[2,256,256]{2,1,0:T(8,128)(2,1)S(1)}, u32[]{:S(2)}, u32[]{:S(2)}) collective-permute-start(bf16[2,256,256]{2,1,0:T(8,128)(2,1)} %get-tuple-element.17), channel_id=1, source_target_pairs={{2,0},{3,1},{4,2},{5,3},{6,4},{7,5},{8,6},{9,7},{10,8},{11,9},{12,... | collective-permute-start | bytes 786440 | tf_op jit(solution)/shard_map/ppermute | solution.py:271
  72.7 20.7 %collective-permute-start.5 = (bf16[2,256,256]{2,1,0:T(8,128)(2,1)S(1)}, bf16[2,256,256]{2,1,0:T(8,128)(2,1)S(1)}, u32[]{:S(2)}, u32[]{:S(2)}) collective-permute-start(bf16[2,256,256]{2,1,0:T(8,128)(2,1)S(1)} %get-tuple-element.18), channel_id=1, source_target_pairs={{4,0},{5,1},{6,2},{7,3},{8,4},{9,5},{10,6},{11,7},{12,8},{13,9},{1... | collective-permute-start | bytes 786440 | tf_op jit(solution)/shard_map/ppermute | solution.py:271
  74.8 23.9 %all-to-all-start.2 = ((bf16[32,2,24,128]{3,2,1,0:T(8,128)(2,1)}), bf16[32,2,24,128]{3,2,1,0:T(8,128)(2,1)S(1)}, u32[]{:S(2)}, u32[]{:S(2)}) async-start(bf16[32,2,24,128]{3,2,1,0:T(8,128)(2,1)} %shard_map.122), calls=%async_computation.2 | async-start | bytes 786432 | tf_op jit(solution)/shard_map/all_to_all | solution.py:277
  93.5 4.0 %collective-permute-start.6 = (bf16[2,128,256]{2,1,0:T(8,128)(2,1)S(1)}, bf16[2,128,256]{2,1,0:T(8,128)(2,1)S(1)}, u32[]{:S(2)}, u32[]{:S(2)}) collective-permute-start(bf16[2,128,256]{2,1,0:T(8,128)(2,1)S(1)} %slice.17), channel_id=1, source_target_pairs={{0,1},{1,0},{2,3},{3,2},{4,5},{5,4},{6,7},{7,6},{8,9},{9,8},{10,11... | collective-permute-start | bytes 393224 | tf_op jit(solution)/shard_map/ppermute | solution.py:274

commit v8 on v7

--- a/solution.py
+++ b/solution.py
@@ -19,6 +19,7 @@
 TO_LOG2 = SCALE * math.log2(math.e)
 F32 = jnp.float32
 BF16 = jnp.bfloat16
+SHORT = 4
 VMEM_BYTES = 20 << 20
 
 
@@ -36,15 +37,18 @@
         ref[kind, h, chunk, j : j + 1, :] = row[:, j * HD : (j + 1) * HD]
 
 
-def units(mine_ref, others_ref):
+def units(q_ref, g_ref, others_ref):
     kept = KVH // 2
-    run = mine_ref.shape[2] // kept
+    run = q_ref.shape[1] // kept
     found = []
     for h in range(kept):
-        for chunk, ref in enumerate((mine_ref, others_ref)):
-
-            def read(which, first, count, h=h, ref=ref):
-                return heads_of(ref, h * run + first * HD, count, (which,))
+        for chunk in range(2):
+
+            def read(which, first, count, h=h, chunk=chunk):
+                start = h * run + first * HD
+                if chunk:
+                    return heads_of(others_ref, start, count, (which,))
+                return heads_of(g_ref if which else q_ref, start, count)
 
             found.append((h, chunk, read))
     return found, run // HD
@@ -63,28 +67,54 @@
     )
 
 
-def masks(where_ref, first_ref, toks):
+def tokens(chunk, toks, where_ref, lengths_ref, tenants_ref, slots_ref):
+    core, index = where_ref[0], where_ref[1]
+    begin = (index + chunk * (1 - 2 * core)) * toks
+    here = lax.broadcasted_iota(jnp.int32, (1, toks), 1) + begin
+    docs = lengths_ref.shape[1]
+    doc = first = slot = jnp.zeros((1, toks), jnp.int32)
+    start, low, high = jnp.int32(0), jnp.int32(-1), jnp.int32(-1)
+    for n in range(docs):
+        reached = here >= start
+        doc = jnp.where(reached, n, doc)
+        first = jnp.where(reached, start, first)
+        slot = jnp.where(reached, slots_ref[tenants_ref[0, n]], slot)
+        low = low + (begin >= start).astype(jnp.int32)
+        high = high + (begin + toks - 1 >= start).astype(jnp.int32)
+        start = start + lengths_ref[0, n]
+    some = [slots_ref[tenants_ref[0, jnp.minimum(low + n, docs - 1)]] for n in range(SHORT)]
+    return here, first, slot, doc - low, high - low + 1, some
+
+
+def masks(toks, *where_refs):
+    core, index = where_refs[0][0], where_refs[0][1]
+    even = core == 0
+    facing = index + 1 - 2 * core
+    near, far = jnp.where(even, index - 1, index - 3), jnp.where(even, index - 3, index - 1)
+    last = jnp.where(even, index, index - 4)
+    shards = (
+        (index, index - 2, index - 4, near, far),
+        (facing, index - 2, facing - 2, facing - 4, last),
+    )
     down = lax.broadcasted_iota(jnp.int32, (toks, toks), 0)
-    along = lax.broadcasted_iota(jnp.int32, (toks, toks), 1)
     found = []
     for chunk in range(2):
-        at = 1 + chunk * 6
-        here = along + where_ref[at] * toks
+        here, first = tokens(chunk, toks, *where_refs)[:2]
         found.append([])
-        for b in range(5):
-            key = down + where_ref[at + 1 + b] * toks
-            seen = (key >= first_ref[chunk]) & (key <= here)
+        for shard in shards[chunk]:
+            key = down + shard * toks
+            seen = (key >= first) & (key <= here)
             found[-1].append(jnp.where(seen, 0.0, -1e30).astype(F32))
     return found
 
 
-def token_stats_kernel(where_ref, mine_ref, others_ref, *refs):
-    window, (first_ref, stat_ref) = refs[:4], refs[4:]
+def token_stats_kernel(where_ref, lengths_ref, tenants_ref, slots_ref, q_ref, g_ref, others_ref, *refs):
+    window, (stat_ref,) = refs[:4], refs[4:]
     core = where_ref[0]
-    toks = mine_ref.shape[1]
-    hidden = masks(where_ref, first_ref, toks)
+    toks = q_ref.shape[0]
+    hidden = masks(toks, where_ref, lengths_ref, tenants_ref, slots_ref)
     blocks = len(hidden[0])
-    found, heads = units(mine_ref, others_ref)
+    found, heads = units(q_ref, g_ref, others_ref)
     for h, chunk, read in found:
         keys, values = (windows(core, h, which, *window)[chunk] for which in range(2))
 
@@ -119,67 +149,87 @@
             stat_ref[2, h, chunk, j : j + 1, :] = jnp.sum(dot * weight, axis=0, keepdims=True)
 
 
-def prefix_kernel(mine_ref, others_ref, pref_ref, slot_ref, stat_ref, full_ref, out_ref):
+def prefix_kernel(
+    where_ref, lengths_ref, tenants_ref, slots_ref, q_ref, g_ref, others_ref, pref_ref, stat_ref,
+    full_ref, out_ref, rows_ref, sum_ref,
+):
     count, _, each, _ = pref_ref.shape
-    found, heads = units(mine_ref, others_ref)
+    found, heads = units(q_ref, g_ref, others_ref)
     slots = count * each // PLEN
-    grads = {}
-    for h, chunk, read in found:
-        if not chunk:
-            columns = slice(h * HD, (h + 1) * HD)
+    found_docs = [
+        tokens(chunk, q_ref.shape[0], where_ref, lengths_ref, tenants_ref, slots_ref)
+        for chunk in range(2)
+    ]
+    for which in range(2):
+        for h in range(KVH // 2):
+            parts = [pref_ref[n, which, :, h * HD : (h + 1) * HD].astype(F32) for n in range(count)]
+            rows_ref[which, h] = jnp.concatenate(parts, axis=0).astype(BF16)
+
+    def form(short):
+        for h, chunk, read in found:
+            _, _, slot, place, _, some = found_docs[chunk]
+            if short:
+                places = [pl.ds(pl.multiple_of(n * PLEN, PLEN), PLEN) for n in some]
+            else:
+                places = [slice(k * PLEN, (k + 1) * PLEN) for k in range(slots)]
             keys, values = (
-                jnp.concatenate(
-                    [pref_ref[part, which, :, columns].astype(F32) for part in range(count)], axis=0
-                ).astype(BF16)
+                jnp.concatenate([rows_ref[which, h, p] for p in places], axis=0)
                 for which in range(2)
             )
-        q, g = read(0, 0, heads), read(1, 0, heads)
-        slot = jnp.concatenate([slot_ref[chunk]] * heads, axis=1)
-        s_all = lax.dot_general(keys, q, NT, preferred_element_type=F32)
-        dp_all = lax.dot_general(values, g, NT, preferred_element_type=F32)
-        s, dp = s_all[:PLEN], dp_all[:PLEN]
-        for k in range(1, slots):
-            rows = slice(k * PLEN, (k + 1) * PLEN)
-            s = jnp.where(slot == k, s_all[rows], s)
-            dp = jnp.where(slot == k, dp_all[rows], dp)
-        top = joined(stat_ref, 0, h, chunk)
-        new = jnp.maximum(top, jnp.max(s, axis=0, keepdims=True) * TO_LOG2)
-        e = jnp.exp2(s * TO_LOG2 - new)
-        old = jnp.exp2(top - new)
-        total = old * joined(stat_ref, 1, h, chunk) + jnp.sum(e, axis=0, keepdims=True)
-        dot = old * joined(stat_ref, 2, h, chunk) + jnp.sum(e * dp, axis=0, keepdims=True)
-        inverse = 1.0 / total
-        delta = dot * inverse
-        p = e * inverse
-        ds = p * (dp - delta)
-        split(full_ref, 0, h, chunk, new + jnp.log2(total))
-        split(full_ref, 1, h, chunk, delta)
-        zero = jnp.zeros_like(p)
-
-        def spread(x, slot=slot, zero=zero):
-            return jnp.concatenate(
-                [jnp.where(slot == k, x, zero).astype(BF16) for k in range(slots)], axis=0
+            q, g = read(0, 0, heads), read(1, 0, heads)
+            place = jnp.concatenate([place if short else slot] * heads, axis=1)
+            s_all = lax.dot_general(keys, q, NT, preferred_element_type=F32)
+            dp_all = lax.dot_general(values, g, NT, preferred_element_type=F32)
+            s, dp = s_all[:PLEN], dp_all[:PLEN]
+            for k in range(1, len(places)):
+                rows = slice(k * PLEN, (k + 1) * PLEN)
+                s = jnp.where(place == k, s_all[rows], s)
+                dp = jnp.where(place == k, dp_all[rows], dp)
+            top = joined(stat_ref, 0, h, chunk)
+            new = jnp.maximum(top, jnp.max(s, axis=0, keepdims=True) * TO_LOG2)
+            e = jnp.exp2(s * TO_LOG2 - new)
+            old = jnp.exp2(top - new)
+            total = old * joined(stat_ref, 1, h, chunk) + jnp.sum(e, axis=0, keepdims=True)
+            dot = old * joined(stat_ref, 2, h, chunk) + jnp.sum(e * dp, axis=0, keepdims=True)
+            inverse = 1.0 / total
+            delta = dot * inverse
+            p = e * inverse
+            ds = p * (dp - delta)
+            split(full_ref, 0, h, chunk, new + jnp.log2(total))
+            split(full_ref, 1, h, chunk, delta)
+            zero = jnp.zeros_like(p)
+
+            def spread(x, place=place, zero=zero, places=places):
+                return jnp.concatenate(
+                    [jnp.where(place == k, x, zero).astype(BF16) for k in range(len(places))], axis=0
+                )
+
+            grads = (
+                lax.dot_general(spread(ds), q, NN, preferred_element_type=F32) * SCALE,
+                lax.dot_general(spread(p), g, NN, preferred_element_type=F32),
             )
-
-        grads[chunk] = (
-            lax.dot_general(spread(ds), q, NN, preferred_element_type=F32),
-            lax.dot_general(spread(p), g, NN, preferred_element_type=F32),
-        )
-        if chunk:
-            dk, dv = (grads[0][0] + grads[1][0]) * SCALE, grads[0][1] + grads[1][1]
-            for which, grad in enumerate((dk, dv)):
-                for part in range(count):
-                    rows = grad[part * each : (part + 1) * each]
-                    out_ref[2 * which + h, part] = rows.astype(BF16)
-
-
-def token_grads_kernel(where_ref, mine_ref, others_ref, *refs):
-    window, (first_ref, full_ref, home_ref, one_ref, two_ref) = refs[:4], refs[4:]
+            if not chunk:
+                sum_ref[...] = jnp.zeros_like(sum_ref)
+            for which, grad in enumerate(grads):
+                for k, p in enumerate(places):
+                    sum_ref[which, p] += grad[k * PLEN : (k + 1) * PLEN]
+                if chunk:
+                    for part in range(count):
+                        rows = sum_ref[which, part * each : (part + 1) * each]
+                        out_ref[2 * which + h, part] = rows.astype(BF16)
+
+    few = jnp.maximum(found_docs[0][4], found_docs[1][4]) <= SHORT
+    pl.when(few)(lambda: form(True))
+    pl.when(jnp.logical_not(few))(lambda: form(False))
+
+
+def token_grads_kernel(where_ref, lengths_ref, tenants_ref, slots_ref, q_ref, g_ref, others_ref, *refs):
+    window, (full_ref, home_ref, one_ref, two_ref) = refs[:4], refs[4:]
     core = where_ref[0]
     even = core == 0
-    toks = mine_ref.shape[1]
-    hidden = masks(where_ref, first_ref, toks)
-    found, heads = units(mine_ref, others_ref)
+    toks = q_ref.shape[0]
+    hidden = masks(toks, where_ref, lengths_ref, tenants_ref, slots_ref)
+    found, heads = units(q_ref, g_ref, others_ref)
     grads = {}
     for h, chunk, read in found:
         keys, values = (windows(core, h, which, *window)[chunk] for which in range(2))
@@ -231,30 +281,18 @@
                 out_ref[:, at : at + HD] = total
 
 
-def call(kernel, flops, exps, ins, outs):
+def call(kernel, flops, exps, ins, outs, scratch=()):
     space = pl.BlockSpec(memory_space=pltpu.VMEM)
-    scalar = pl.BlockSpec(memory_space=pltpu.SMEM)
+    scalars = pl.BlockSpec(memory_space=pltpu.SMEM)
     return pl.pallas_call(
         kernel,
-        in_specs=[scalar if x.ndim == 1 else space for x in ins],
+        in_specs=[scalars if x.dtype == jnp.int32 else space for x in ins],
         out_specs=[space] * len(outs),
         out_shape=outs,
+        scratch_shapes=scratch,
         compiler_params=pltpu.CompilerParams(vmem_limit_bytes=VMEM_BYTES),
         cost_estimate=pl.CostEstimate(flops=flops, bytes_accessed=6 << 20, transcendentals=exps),
     )(*ins)
-
-
-def layout(lengths, tenants, slots, block, toks):
-    ends = jnp.cumsum(lengths)
-    slot_of = jnp.sum(
-        jnp.where(tenants[:, None] == jnp.arange(slots.shape[0])[None, :], slots[None, :], 0), axis=1
-    )
-    here = block * toks + jnp.arange(toks, dtype=jnp.int32)
-    doc = jnp.sum((here[None, :] >= ends[:, None]).astype(jnp.int32), axis=0)
-    pick = doc[None, :] == jnp.arange(lengths.shape[0])[:, None]
-    first = jnp.sum(jnp.where(pick, (ends - lengths)[:, None], 0), axis=0)
-    slot = jnp.sum(jnp.where(pick, slot_of[:, None], 0), axis=0)
-    return first[None, :].astype(jnp.int32), slot[None, :].astype(jnp.int32)
 
 
 def per_device(
@@ -289,21 +327,11 @@
     others = swap(jnp.stack([half(queries, 1 - core), half(grad_out, 1 - core)]))
     cross = swap(jnp.stack([half(x, 1 - core) for x in (own, one, two)]))
 
-    facing = index ^ 1
-    near, far = jnp.where(even, index - 1, index - 3), jnp.where(even, index - 3, index - 1)
-    docs = (doc_lengths[0], doc_tenants[0], tenant_slots)
-    first0, slot0 = layout(*docs, index, toks)
-    first1, slot1 = layout(*docs, facing, toks)
-    first, slot = jnp.stack([first0, first1]), jnp.stack([slot0, slot1])
-    last = jnp.where(even, index, index - 4)
-    where = [core, index, index, index - 2, index - 4, near, far]
-    where += [facing, facing, index - 2, facing - 2, facing - 4, last]
-    where = jnp.stack(where).astype(jnp.int32)
-
-    heads = [jnp.stack([half(queries, core), half(grad_out, core)]), others]
+    where = (jnp.stack([core, index.astype(jnp.int32)]), doc_lengths, doc_tenants, tenant_slots)
+    heads = [half(queries, core), half(grad_out, core), others]
     shape = (KVH // 2, 2, HQ // KVH, toks)
     work = queries.size // HD * 5 * toks
-    window = [where, *heads, own, one, two, cross, first]
+    window = [*where, *heads, own, one, two, cross]
     (stats,) = call(
         token_stats_kernel,
         flops=4 * HD * work,
@@ -316,7 +344,11 @@
         prefix_kernel,
         flops=8 * HD * prefs,
         exps=prefs // 6,
-        ins=[*heads, pref, slot, stats],
+        ins=[*where, *heads, pref, stats],
+        scratch=[
+            pltpu.VMEM((2, KVH // 2, count * pref.shape[2], HD), BF16),
+            pltpu.VMEM((2, count * pref.shape[2], HD), F32),
+        ],
         outs=[
             jax.ShapeDtypeStruct((2, *shape), F32),
             jax.ShapeDtypeStruct((KVH, count, pref.shape[2], HD), BF16),

time: 101 us -> 106 us (1.050)
  waiting for transfers between devices: 12.7 us -> 18.3 us
  starting transfers between devices: 47 us -> 51.8 us
  other arithmetic: 5.32 us -> 3.07 us
  local copies, waits for them, and re-layouts: 6.13 us -> 4.82 us
  Pallas kernels: 27.2 us -> 25.9 us
    ppermute x4, starting transfers between devices: 13.2 us -> 7.03 us  [shift(): return lax.ppermute(x, SEQ, pairs)]
    all_to_all x3, starting transfers between devices: 25.4 us -> 30.9 us  [exchange(): return lax.all_to_all(x, axis, split_axis=0, concat_axis=0, tiled=True)]
    ppermute x3, starting transfers between devices: 8.35 us -> 13.8 us  [swap(): return lax.ppermute(x, SEQ, [(i, i ^ 1) for i in range(count)])]
    all_to_all x3, waiting for transfers between devices: 3.03 us -> 6.91 us  [exchange(): return lax.all_to_all(x, axis, split_axis=0, concat_axis=0, tiled=True)]
    ppermute x3, waiting for transfers between devices: 0.97 us -> 2.67 us  [swap(): return lax.ppermute(x, SEQ, [(i, i ^ 1) for i in range(count)])]
    another operation x3 -> x1, other arithmetic: 1.71 us -> 0.08 us  [per_device(): jnp.stack([core, index.astype(jnp.int32)])]
    pallas_call x5, Pallas kernels: 27.2 us -> 25.9 us  [call(): pl.pallas_call(kernel, in_specs=[scalars if x.dtype == jnp.int32 else spa...]
    another operation x1, local copies, waits for them, and re-layouts: 3.3 us -> 2.09 us  [per_device(): jnp.stack([half(queries, 1 - core), half(grad_out, 1 - core)])]
  transfers between devices with their start and end apart: 10 -> 10, of which waited for: 4 -> 5; matrix products, arithmetic and copies ran while one was open for 9% -> 3% of each run, Pallas kernels for 19% -> 18%
where the time goes in v8:
time: 106 us; the launch traced here: 105 us
  starting transfers between devices  51.8 us (49%)
  Pallas kernels  25.9 us (24%)
  waiting for transfers between devices  18.3 us (17%)
  local copies, waits for them, and re-layouts  4.82 us (5%)
  other arithmetic  3.07 us (3%)
    all_to_all x3, starting transfers between devices, exchange(): return lax.all_to_all(x, axis, split_axis=0, concat_axis=0, tiled=True)  30.9 us
    pallas_call x5, Pallas kernels, call(): pl.pallas_call(kernel, in_specs=[scalars if x.dtype == jnp.int32 else spa...  25.9 us
    ppermute x3, starting transfers between devices, swap(): return lax.ppermute(x, SEQ, [(i, i ^ 1) for i in range(count)])  13.8 us
    ppermute x4, waiting for transfers between devices, shift(): return lax.ppermute(x, SEQ, pairs)  8.67 us
    ppermute x4, starting transfers between devices, shift(): return lax.ppermute(x, SEQ, pairs)  7.03 us
    all_to_all x3, waiting for transfers between devices, exchange(): return lax.all_to_all(x, axis, split_axis=0, concat_axis=0, tiled=True)  6.91 us
    ppermute x3, waiting for transfers between devices, swap(): return lax.ppermute(x, SEQ, [(i, i ^ 1) for i in range(count)])  2.67 us
  transfers between devices with their start and end apart: 10, of which 5 were waited for; matrix products, arithmetic and copies ran while one was open for 3% of the time, Pallas kernels for 18%

profile of v8, /device:TPU:1, one launch (start us, length us, event | category | flops | bytes accessed | tf_op | source)
XLA Modules:
  0.0 104.8 jit_solution(17405391776371403300)
XLA Ops:
  0.6 2.1 %dynamic-slice_bitcast_fusion = (bf16[1,128,3072]{2,1,0:T(8,128)(2,1)S(1)}, bf16[128,3072]{1,0:T(8,128)(2,1)S(1)}, bf16[128,3072]{1,0:T(8,128)(2,1)S(1)}, bf16[1,128,3072]{2,1,0:T(8,128)(2,1)S(1)}) fusion(bf16[128,6144]{1,0:T(8,128)(2,1)} %param.12, s32[]{:T(128)S(6)} %select_n.27, s32[]{:T(128)S(6)} %select_n.26, bf16[128,6144]{1,0:T(8,128)(2,1)} %param.9), kind=kLoop, calls=%fused_computation.1 | loop fusion | bytes 6291464 | tf_op jit(solution)/shard_map/stack | solution.py:327
  2.7 0.0 copy-start.7
  2.8 0.0 copy-start.8
  2.8 0.0 copy-start.9
  2.8 0.0 copy-start.10
  2.8 1.3 %pad_maximum_fusion = bf16[2,128,3072]{2,1,0:T(8,128)(2,1)} fusion(bf16[1,128,3072]{2,1,0:T(8,128)(2,1)S(1)} %get-tuple-element.24, bf16[1,128,3072]{2,1,0:T(8,128)(2,1)S(1)} %get-tuple-element.31), kind=kLoop, calls=%fused_computation | loop fusion | flops 786432 | bytes 3145728 | tf_op jit(solution)/shard_map/stack | solution.py:327
  4.1 8.8 %collective-permute-start = (bf16[2,128,3072]{2,1,0:T(8,128)(2,1)}, bf16[2,128,3072]{2,1,0:T(8,128)(2,1)}, u32[]{:S(2)}, u32[]{:S(2)}) collective-permute-start(bf16[2,128,3072]{2,1,0:T(8,128)(2,1)} %pad_maximum_fusion), channel_id=1, source_target_pairs={{0,1},{1,0},{2,3},{3,2},{4,5},{5,4},{6,7},{7,6},{8,9},{9,8},{10,11... | collective-permute-start | bytes 4718600 | tf_op jit(solution)/shard_map/ppermute | solution.py:312
  12.8 0.0 copy-done.7
  12.9 0.0 copy-done.8
  12.9 1.3 %collective-permute-start.2 = (bf16[2,128,512]{2,1,0:T(8,128)(2,1)S(1)}, bf16[2,128,512]{2,1,0:T(8,128)(2,1)S(1)}, u32[]{:S(2)}, u32[]{:S(2)}) collective-permute-start(bf16[2,128,512]{2,1,0:T(8,128)(2,1)S(1)} %pad_maximum_fusion.2.refs_0_), channel_id=1, source_target_pairs={{0,4},{1,5},{2,6},{3,7},{4,8},{5,9},{6,10},{7,11},{8,12},{9,13},{1... | collective-permute-start | bytes 786440 | tf_op jit(solution)/shard_map/ppermute | solution.py:309
  14.2 3.2 %collective-permute-start.1 = (bf16[2,128,512]{2,1,0:T(8,128)(2,1)S(1)}, bf16[2,128,512]{2,1,0:T(8,128)(2,1)S(1)}, u32[]{:S(2)}, u32[]{:S(2)}) collective-permute-start(bf16[2,128,512]{2,1,0:T(8,128)(2,1)S(1)} %pad_maximum_fusion.2.refs_0_), channel_id=1, source_target_pairs={{0,2},{1,3},{2,4},{3,5},{4,6},{5,7},{6,8},{7,9},{8,10},{9,11},{10,... | collective-permute-start | bytes 786440 | tf_op jit(solution)/shard_map/ppermute | solution.py:309
  17.4 0.0 copy-done.9
  17.4 0.0 copy-done.10
  17.4 0.0 copy-start.2
  17.4 0.0 copy-start.3
  17.5 0.0 copy-start.4
  17.5 0.1 maximum_bitcast_fusion
  17.6 0.8 broadcast_in_dim.2
  18.3 8.1 %all-to-all-start = ((bf16[16,2,24,256]{3,2,1,0:T(8,128)(2,1)}), bf16[16,2,24,256]{3,2,1,0:T(8,128)(2,1)S(1)}, u32[]{:S(2)}, u32[]{:S(2)}) async-start(bf16[16,2,24,256]{3,2,1,0:T(8,128)(2,1)} %bitcast.5), calls=%async_computation | async-start | bytes 786432 | tf_op jit(solution)/shard_map/all_to_all | solution.py:315
  26.5 0.0 collective-permute-done.2.refs_2_
  26.5 0.0 collective-permute-done.1.refs_1_
  26.6 0.8 pad_maximum_fusion.1
  27.4 2.0 %collective-permute-start.3 = (bf16[3,2,128,256]{3,2,1,0:T(8,128)(2,1)}, bf16[3,2,128,256]{3,2,1,0:T(8,128)(2,1)S(1)}, u32[]{:S(2)}, u32[]{:S(2)}) collective-permute-start(bf16[3,2,128,256]{3,2,1,0:T(8,128)(2,1)} %pad_maximum_fusion.1), channel_id=1, source_target_pairs={{0,1},{1,0},{2,3},{3,2},{4,5},{5,4},{6,7},{7,6},{8,9},{9,8},{10,11... | collective-permute-start | bytes 1179656 | tf_op jit(solution)/shard_map/ppermute | solution.py:312
  29.4 0.1 pad_add_fusion.where_ref
  29.5 1.7 %collective-permute-done.3.refs_3_ = bf16[3,2,128,256]{3,2,1,0:T(8,128)(2,1)S(1)} collective-permute-done((bf16[3,2,128,256]{3,2,1,0:T(8,128)(2,1)}, bf16[3,2,128,256]{3,2,1,0:T(8,128)(2,1)S(1)}, u32[]{:S(2)}, u32[]{:S(2)}) %collective-permute-start.3) | collective-permute-done | bytes 393248 | tf_op jit(solution)/shard_map/ppermute | solution.py:312
  31.2 0.0 copy-start
  31.2 0.0 collective-permute-done.others_ref
  31.2 0.0 copy-done.2
  31.2 0.0 copy-done.3
  31.2 0.0 copy-done.4
  31.2 7.4 %shard_map.120.stat_ref = f32[3,2,2,12,128]{4,3,2,1,0:T(8,128)S(1)} custom-call(s32[2]{0:T(128)S(1)} %pad_add_fusion.where_ref, s32[1,8]{1,0:T(1,128)S(1)} %copy-done.2, s32[1,8]{1,0:T(1,128)S(1)} %copy-done.3, s32[6]{0:T(128)S(1)} %copy-done.4, bf16[128,3072]{1,0:T(8,128)(2,1)S(1)} %get-tuple-element.30.q_ref, ...), custom_call_target="tpu_custom_call" | custom-call | flops 2013265920 | bytes 6291456 | tf_op jit(solution)/shard_map/pallas_call | solution.py:287
  38.6 0.0 copy-done
  38.6 6.6 %all-to-all-done.pref_ref = bf16[16,2,24,256]{3,2,1,0:T(8,128)(2,1)S(1)} async-done(((bf16[16,2,24,256]{3,2,1,0:T(8,128)(2,1)}), bf16[16,2,24,256]{3,2,1,0:T(8,128)(2,1)S(1)}, u32[]{:S(2)}, u32[]{:S(2)}) %all-to-all-start) | async-done | bytes 393248 | tf_op jit(solution)/shard_map/all_to_all | solution.py:315
  45.2 6.1 %shard_map.121 = (f32[2,2,2,12,128]{4,3,2,1,0:T(8,128)S(1)}, bf16[4,16,24,128]{3,2,1,0:T(8,128)(2,1)}) custom-call(s32[2]{0:T(128)S(1)} %pad_add_fusion.where_ref, s32[1,8]{1,0:T(1,128)S(1)} %copy-done.2, s32[1,8]{1,0:T(1,128)S(1)} %copy-done.3, s32[6]{0:T(128)S(1)} %copy-done.4, bf16[128,3072]{1,0:T(8,128)(2,1)S(1)} %get-tuple-element.30.q_ref, ...), custom_call_target="tpu_custom_call" | custom-call | flops 2415919104 | bytes 6291456 | tf_op jit(solution)/shard_map/pallas_call | solution.py:287
  51.2 0.0 copy-start.5
  51.2 12.9 %all-to-all-start.1 = ((bf16[64,24,128]{2,1,0:T(8,128)(2,1)}), bf16[64,24,128]{2,1,0:T(8,128)(2,1)S(1)}, u32[]{:S(2)}, u32[]{:S(2)}) async-start(bf16[64,24,128]{2,1,0:T(8,128)(2,1)} %bitcast.11), calls=%async_computation.1 | async-start | bytes 786432 | tf_op jit(solution)/shard_map/all_to_all | solution.py:315
  64.1 0.0 copy-done.5
  64.1 0.0 copy-start.1
  64.1 1.0 copy-done.1
  65.1 0.0 copy-start.6
  65.1 0.8 copy-done.6
  66.0 10.9 %shard_map.123 = (f32[2,256,256]{2,1,0:T(8,128)S(1)}, bf16[2,256,256]{2,1,0:T(8,128)(2,1)}, bf16[2,256,256]{2,1,0:T(8,128)(2,1)S(1)}) custom-call(s32[2]{0:T(128)S(1)} %pad_add_fusion.where_ref, s32[1,8]{1,0:T(1,128)S(1)} %copy-done.2, s32[1,8]{1,0:T(1,128)S(1)} %copy-done.3, s32[6]{0:T(128)S(1)} %copy-done.4, ...), custom_call_target="tpu_custom_call" | custom-call | flops 4026531840 | bytes 6291456 | tf_op jit(solution)/shard_map/pallas_call | solution.py:287
  76.9 1.3 %collective-permute-start.4 = (bf16[2,256,256]{2,1,0:T(8,128)(2,1)}, bf16[2,256,256]{2,1,0:T(8,128)(2,1)S(1)}, u32[]{:S(2)}, u32[]{:S(2)}) collective-permute-start(bf16[2,256,256]{2,1,0:T(8,128)(2,1)} %get-tuple-element.17), channel_id=1, source_target_pairs={{2,0},{3,1},{4,2},{5,3},{6,4},{7,5},{8,6},{9,7},{10,8},{11,9},{12,... | collective-permute-start | bytes 786440 | tf_op jit(solution)/shard_map/ppermute | solution.py:309
  78.2 1.3 %collective-permute-start.5 = (bf16[2,256,256]{2,1,0:T(8,128)(2,1)S(1)}, bf16[2,256,256]{2,1,0:T(8,128)(2,1)S(1)}, u32[]{:S(2)}, u32[]{:S(2)}) collective-permute-start(bf16[2,256,256]{2,1,0:T(8,128)(2,1)S(1)} %get-tuple-element.18), channel_id=1, source_target_pairs={{4,0},{5,1},{6,2},{7,3},{8,4},{9,5},{10,6},{11,7},{12,8},{13,9},{1... | collective-permute-start | bytes 786440 | tf_op jit(solution)/shard_map/ppermute | solution.py:309
  79.5 0.0 all-to-all-done.1.got_ref
  79.5 0.8 shard_map.122
  80.3 9.9 %all-to-all-start.2 = ((bf16[32,2,24,128]{3,2,1,0:T(8,128)(2,1)}), bf16[32,2,24,128]{3,2,1,0:T(8,128)(2,1)S(1)}, u32[]{:S(2)}, u32[]{:S(2)}) async-start(bf16[32,2,24,128]{3,2,1,0:T(8,128)(2,1)} %shard_map.122), calls=%async_computation.2 | async-start | bytes 786432 | tf_op jit(solution)/shard_map/all_to_all | solution.py:315
  90.2 0.0 collective-permute-done.4
  90.2 8.7 %collective-permute-done.5 = bf16[2,256,256]{2,1,0:T(8,128)(2,1)S(1)} collective-permute-done((bf16[2,256,256]{2,1,0:T(8,128)(2,1)S(1)}, bf16[2,256,256]{2,1,0:T(8,128)(2,1)S(1)}, u32[]{:S(2)}, u32[]{:S(2)}) %collective-permute-start.5) | collective-permute-done | bytes 262176 | tf_op jit(solution)/shard_map/ppermute | solution.py:309
  98.9 0.1 add_convert_fusion
  99.0 3.0 %collective-permute-start.6 = (bf16[2,128,256]{2,1,0:T(8,128)(2,1)S(1)}, bf16[2,128,256]{2,1,0:T(8,128)(2,1)S(1)}, u32[]{:S(2)}, u32[]{:S(2)}) collective-permute-start(bf16[2,128,256]{2,1,0:T(8,128)(2,1)S(1)} %slice.17), channel_id=1, source_target_pairs={{0,1},{1,0},{2,3},{3,2},{4,5},{5,4},{6,7},{7,6},{8,9},{9,8},{10,11... | collective-permute-start | bytes 393224 | tf_op jit(solution)/shard_map/ppermute | solution.py:312
  102.1 1.0 collective-permute-done.6
  103.0 0.7 fusion.4
  103.8 0.3 all-to-all-done.2
  104.1 0.7 shard_map.124
  (9 shorter events, 0.1 us)
Async XLA Ops:
  2.7 10.1 %copy-start.7 = (bf16[128,512]{1,0:T(8,128)(2,1)S(1)}, bf16[128,512]{1,0:T(8,128)(2,1)}, u32[]{:S(2)}) copy-start(bf16[128,512]{1,0:T(8,128)(2,1)} %param.11) | copy-start | bytes 393220
  2.8 10.1 %copy-start.8 = (bf16[128,512]{1,0:T(8,128)(2,1)S(1)}, bf16[128,512]{1,0:T(8,128)(2,1)}, u32[]{:S(2)}) copy-start(bf16[128,512]{1,0:T(8,128)(2,1)} %param.10) | copy-start | bytes 393220
  2.8 14.6 %copy-start.9 = (bf16[24,512]{1,0:T(8,128)(2,1)S(1)}, bf16[24,512]{1,0:T(8,128)(2,1)}, u32[]{:S(2)}) copy-start(bf16[24,512]{1,0:T(8,128)(2,1)} %param.13) | copy-start | bytes 73732
  2.8 14.6 %copy-start.10 = (bf16[24,512]{1,0:T(8,128)(2,1)S(1)}, bf16[24,512]{1,0:T(8,128)(2,1)}, u32[]{:S(2)}) copy-start(bf16[24,512]{1,0:T(8,128)(2,1)} %param.14) | copy-start | bytes 73732
  4.1 27.1 %collective-permute-start = (bf16[2,128,3072]{2,1,0:T(8,128)(2,1)}, bf16[2,128,3072]{2,1,0:T(8,128)(2,1)}, u32[]{:S(2)}, u32[]{:S(2)}) collective-permute-start(bf16[2,128,3072]{2,1,0:T(8,128)(2,1)} %pad_maximum_fusion), channel_id=1, source_target_pairs={{0,1},{1,0},{2,3},{3,2},{4,5},{5,4},{6,7},{7,6},{8,9},{9,8},{10,11... | collective-permute-start | bytes 4718600 | tf_op jit(solution)/shard_map/ppermute | solution.py:312
  12.9 13.6 %collective-permute-start.2 = (bf16[2,128,512]{2,1,0:T(8,128)(2,1)S(1)}, bf16[2,128,512]{2,1,0:T(8,128)(2,1)S(1)}, u32[]{:S(2)}, u32[]{:S(2)}) collective-permute-start(bf16[2,128,512]{2,1,0:T(8,128)(2,1)S(1)} %pad_maximum_fusion.2.refs_0_), channel_id=1, source_target_pairs={{0,4},{1,5},{2,6},{3,7},{4,8},{5,9},{6,10},{7,11},{8,12},{9,13},{1... | collective-permute-start | bytes 786440 | tf_op jit(solution)/shard_map/ppermute | solution.py:309
  14.2 12.3 %collective-permute-start.1 = (bf16[2,128,512]{2,1,0:T(8,128)(2,1)S(1)}, bf16[2,128,512]{2,1,0:T(8,128)(2,1)S(1)}, u32[]{:S(2)}, u32[]{:S(2)}) collective-permute-start(bf16[2,128,512]{2,1,0:T(8,128)(2,1)S(1)} %pad_maximum_fusion.2.refs_0_), channel_id=1, source_target_pairs={{0,2},{1,3},{2,4},{3,5},{4,6},{5,7},{6,8},{7,9},{8,10},{9,11},{10,... | collective-permute-start | bytes 786440 | tf_op jit(solution)/shard_map/ppermute | solution.py:309
  17.4 13.7 %copy-start.2 = (s32[1,8]{1,0:T(1,128)S(1)}, s32[1,8]{1,0:T(1,128)}, u32[]{:S(2)}) copy-start(s32[1,8]{1,0:T(1,128)} %lengths_ref.5) | copy-start | bytes 100
  17.4 13.7 %copy-start.3 = (s32[1,8]{1,0:T(1,128)S(1)}, s32[1,8]{1,0:T(1,128)}, u32[]{:S(2)}) copy-start(s32[1,8]{1,0:T(1,128)} %tenants_ref.5) | copy-start | bytes 100
  17.5 13.7 %copy-start.4 = (s32[6]{0:T(128)S(1)}, s32[6]{0:T(128)}, u32[]{:S(2)}) copy-start(s32[6]{0:T(128)} %slots_ref.5) | copy-start | bytes 76
  18.3 26.9 %all-to-all-start = ((bf16[16,2,24,256]{3,2,1,0:T(8,128)(2,1)}), bf16[16,2,24,256]{3,2,1,0:T(8,128)(2,1)S(1)}, u32[]{:S(2)}, u32[]{:S(2)}) async-start(bf16[16,2,24,256]{3,2,1,0:T(8,128)(2,1)} %bitcast.5), calls=%async_computation | async-start | bytes 786432 | tf_op jit(solution)/shard_map/all_to_all | solution.py:315
  27.4 3.8 %collective-permute-start.3 = (bf16[3,2,128,256]{3,2,1,0:T(8,128)(2,1)}, bf16[3,2,128,256]{3,2,1,0:T(8,128)(2,1)S(1)}, u32[]{:S(2)}, u32[]{:S(2)}) collective-permute-start(bf16[3,2,128,256]{3,2,1,0:T(8,128)(2,1)} %pad_maximum_fusion.1), channel_id=1, source_target_pairs={{0,1},{1,0},{2,3},{3,2},{4,5},{5,4},{6,7},{7,6},{8,9},{9,8},{10,11... | collective-permute-start | bytes 1179656 | tf_op jit(solution)/shard_map/ppermute | solution.py:312
  31.2 7.4 %copy-start = (bf16[3,2,128,256]{3,2,1,0:T(8,128)(2,1)}, bf16[3,2,128,256]{3,2,1,0:T(8,128)(2,1)S(1)}, u32[]{:S(2)}) copy-start(bf16[3,2,128,256]{3,2,1,0:T(8,128)(2,1)S(1)} %collective-permute-done.3.refs_3_) | copy-start | bytes 1179652
  51.2 12.9 %copy-start.5 = (f32[2,2,2,12,128]{4,3,2,1,0:T(8,128)}, f32[2,2,2,12,128]{4,3,2,1,0:T(8,128)S(1)}, u32[]{:S(2)}) copy-start(f32[2,2,2,12,128]{4,3,2,1,0:T(8,128)S(1)} %get-tuple-element.14.refs_4_) | copy-start | bytes 147460
  51.2 28.2 %all-to-all-start.1 = ((bf16[64,24,128]{2,1,0:T(8,128)(2,1)}), bf16[64,24,128]{2,1,0:T(8,128)(2,1)S(1)}, u32[]{:S(2)}, u32[]{:S(2)}) async-start(bf16[64,24,128]{2,1,0:T(8,128)(2,1)} %bitcast.11), calls=%async_computation.1 | async-start | bytes 786432 | tf_op jit(solution)/shard_map/all_to_all | solution.py:315
  64.1 1.0 copy-start.1
  65.1 0.8 copy-start.6
  76.9 13.3 %collective-permute-start.4 = (bf16[2,256,256]{2,1,0:T(8,128)(2,1)}, bf16[2,256,256]{2,1,0:T(8,128)(2,1)S(1)}, u32[]{:S(2)}, u32[]{:S(2)}) collective-permute-start(bf16[2,256,256]{2,1,0:T(8,128)(2,1)} %get-tuple-element.17), channel_id=1, source_target_pairs={{2,0},{3,1},{4,2},{5,3},{6,4},{7,5},{8,6},{9,7},{10,8},{11,9},{12,... | collective-permute-start | bytes 786440 | tf_op jit(solution)/shard_map/ppermute | solution.py:309
  78.2 20.7 %collective-permute-start.5 = (bf16[2,256,256]{2,1,0:T(8,128)(2,1)S(1)}, bf16[2,256,256]{2,1,0:T(8,128)(2,1)S(1)}, u32[]{:S(2)}, u32[]{:S(2)}) collective-permute-start(bf16[2,256,256]{2,1,0:T(8,128)(2,1)S(1)} %get-tuple-element.18), channel_id=1, source_target_pairs={{4,0},{5,1},{6,2},{7,3},{8,4},{9,5},{10,6},{11,7},{12,8},{13,9},{1... | collective-permute-start | bytes 786440 | tf_op jit(solution)/shard_map/ppermute | solution.py:309
  80.3 23.8 %all-to-all-start.2 = ((bf16[32,2,24,128]{3,2,1,0:T(8,128)(2,1)}), bf16[32,2,24,128]{3,2,1,0:T(8,128)(2,1)S(1)}, u32[]{:S(2)}, u32[]{:S(2)}) async-start(bf16[32,2,24,128]{3,2,1,0:T(8,128)(2,1)} %shard_map.122), calls=%async_computation.2 | async-start | bytes 786432 | tf_op jit(solution)/shard_map/all_to_all | solution.py:315
  99.0 4.0 %collective-permute-start.6 = (bf16[2,128,256]{2,1,0:T(8,128)(2,1)S(1)}, bf16[2,128,256]{2,1,0:T(8,128)(2,1)S(1)}, u32[]{:S(2)}, u32[]{:S(2)}) collective-permute-start(bf16[2,128,256]{2,1,0:T(8,128)(2,1)S(1)} %slice.17), channel_id=1, source_target_pairs={{0,1},{1,0},{2,3},{3,2},{4,5},{5,4},{6,7},{7,6},{8,9},{9,8},{10,11... | collective-permute-start | bytes 393224 | tf_op jit(solution)/shard_map/ppermute | solution.py:312

commit v9 on v8

--- a/solution.py
+++ b/solution.py
@@ -37,18 +37,15 @@
         ref[kind, h, chunk, j : j + 1, :] = row[:, j * HD : (j + 1) * HD]
 
 
-def units(q_ref, g_ref, others_ref):
+def units(mine_ref, others_ref):
     kept = KVH // 2
-    run = q_ref.shape[1] // kept
+    run = mine_ref.shape[2] // kept
     found = []
     for h in range(kept):
-        for chunk in range(2):
-
-            def read(which, first, count, h=h, chunk=chunk):
-                start = h * run + first * HD
-                if chunk:
-                    return heads_of(others_ref, start, count, (which,))
-                return heads_of(g_ref if which else q_ref, start, count)
+        for chunk, ref in enumerate((mine_ref, others_ref)):
+
+            def read(which, first, count, h=h, ref=ref):
+                return heads_of(ref, h * run + first * HD, count, (which,))
 
             found.append((h, chunk, read))
     return found, run // HD
@@ -86,35 +83,28 @@
     return here, first, slot, doc - low, high - low + 1, some
 
 
-def masks(toks, *where_refs):
-    core, index = where_refs[0][0], where_refs[0][1]
-    even = core == 0
-    facing = index + 1 - 2 * core
-    near, far = jnp.where(even, index - 1, index - 3), jnp.where(even, index - 3, index - 1)
-    last = jnp.where(even, index, index - 4)
-    shards = (
-        (index, index - 2, index - 4, near, far),
-        (facing, index - 2, facing - 2, facing - 4, last),
-    )
+def masks(where_ref, first_ref, toks):
     down = lax.broadcasted_iota(jnp.int32, (toks, toks), 0)
+    along = lax.broadcasted_iota(jnp.int32, (toks, toks), 1)
     found = []
     for chunk in range(2):
-        here, first = tokens(chunk, toks, *where_refs)[:2]
+        at = 1 + chunk * 6
+        here = along + where_ref[at] * toks
         found.append([])
-        for shard in shards[chunk]:
-            key = down + shard * toks
-            seen = (key >= first) & (key <= here)
+        for b in range(5):
+            key = down + where_ref[at + 1 + b] * toks
+            seen = (key >= first_ref[chunk]) & (key <= here)
             found[-1].append(jnp.where(seen, 0.0, -1e30).astype(F32))
     return found
 
 
-def token_stats_kernel(where_ref, lengths_ref, tenants_ref, slots_ref, q_ref, g_ref, others_ref, *refs):
-    window, (stat_ref,) = refs[:4], refs[4:]
+def token_stats_kernel(where_ref, mine_ref, others_ref, *refs):
+    window, (first_ref, stat_ref) = refs[:4], refs[4:]
     core = where_ref[0]
-    toks = q_ref.shape[0]
-    hidden = masks(toks, where_ref, lengths_ref, tenants_ref, slots_ref)
+    toks = mine_ref.shape[1]
+    hidden = masks(where_ref, first_ref, toks)
     blocks = len(hidden[0])
-    found, heads = units(q_ref, g_ref, others_ref)
+    found, heads = units(mine_ref, others_ref)
     for h, chunk, read in found:
         keys, values = (windows(core, h, which, *window)[chunk] for which in range(2))
 
@@ -150,14 +140,14 @@
 
 
 def prefix_kernel(
-    where_ref, lengths_ref, tenants_ref, slots_ref, q_ref, g_ref, others_ref, pref_ref, stat_ref,
+    where_ref, lengths_ref, tenants_ref, slots_ref, mine_ref, others_ref, pref_ref, stat_ref,
     full_ref, out_ref, rows_ref, sum_ref,
 ):
     count, _, each, _ = pref_ref.shape
-    found, heads = units(q_ref, g_ref, others_ref)
+    found, heads = units(mine_ref, others_ref)
     slots = count * each // PLEN
     found_docs = [
-        tokens(chunk, q_ref.shape[0], where_ref, lengths_ref, tenants_ref, slots_ref)
+        tokens(chunk, mine_ref.shape[1], where_ref, lengths_ref, tenants_ref, slots_ref)
         for chunk in range(2)
     ]
     for which in range(2):
@@ -223,13 +213,13 @@
     pl.when(jnp.logical_not(few))(lambda: form(False))
 
 
-def token_grads_kernel(where_ref, lengths_ref, tenants_ref, slots_ref, q_ref, g_ref, others_ref, *refs):
-    window, (full_ref, home_ref, one_ref, two_ref) = refs[:4], refs[4:]
+def token_grads_kernel(where_ref, mine_ref, others_ref, *refs):
+    window, (first_ref, full_ref, home_ref, one_ref, two_ref) = refs[:4], refs[4:]
     core = where_ref[0]
     even = core == 0
-    toks = q_ref.shape[0]
-    hidden = masks(toks, where_ref, lengths_ref, tenants_ref, slots_ref)
-    found, heads = units(q_ref, g_ref, others_ref)
+    toks = mine_ref.shape[1]
+    hidden = masks(where_ref, first_ref, toks)
+    found, heads = units(mine_ref, others_ref)
     grads = {}
     for h, chunk, read in found:
         keys, values = (windows(core, h, which, *window)[chunk] for which in range(2))
@@ -281,18 +271,31 @@
                 out_ref[:, at : at + HD] = total
 
 
-def call(kernel, flops, exps, ins, outs, scratch=()):
+def call(kernel, flops, exps, ins, outs, scratch=(), scalar=()):
     space = pl.BlockSpec(memory_space=pltpu.VMEM)
     scalars = pl.BlockSpec(memory_space=pltpu.SMEM)
     return pl.pallas_call(
         kernel,
-        in_specs=[scalars if x.dtype == jnp.int32 else space for x in ins],
+        in_specs=[scalars if n in scalar else space for n in range(len(ins))],
         out_specs=[space] * len(outs),
         out_shape=outs,
         scratch_shapes=scratch,
         compiler_params=pltpu.CompilerParams(vmem_limit_bytes=VMEM_BYTES),
         cost_estimate=pl.CostEstimate(flops=flops, bytes_accessed=6 << 20, transcendentals=exps),
     )(*ins)
+
+
+def layout(lengths, tenants, slots, block, toks):
+    ends = jnp.cumsum(lengths)
+    slot_of = jnp.sum(
+        jnp.where(tenants[:, None] == jnp.arange(slots.shape[0])[None, :], slots[None, :], 0), axis=1
+    )
+    here = block * toks + jnp.arange(toks, dtype=jnp.int32)
+    doc = jnp.sum((here[None, :] >= ends[:, None]).astype(jnp.int32), axis=0)
+    pick = doc[None, :] == jnp.arange(lengths.shape[0])[:, None]
+    first = jnp.sum(jnp.where(pick, (ends - lengths)[:, None], 0), axis=0)
+    slot = jnp.sum(jnp.where(pick, slot_of[:, None], 0), axis=0)
+    return first[None, :].astype(jnp.int32), slot[None, :].astype(jnp.int32)
 
 
 def per_device(
@@ -327,16 +330,27 @@
     others = swap(jnp.stack([half(queries, 1 - core), half(grad_out, 1 - core)]))
     cross = swap(jnp.stack([half(x, 1 - core) for x in (own, one, two)]))
 
-    where = (jnp.stack([core, index.astype(jnp.int32)]), doc_lengths, doc_tenants, tenant_slots)
-    heads = [half(queries, core), half(grad_out, core), others]
+    facing = index ^ 1
+    near, far = jnp.where(even, index - 1, index - 3), jnp.where(even, index - 3, index - 1)
+    docs = (doc_lengths[0], doc_tenants[0], tenant_slots)
+    first0, slot0 = layout(*docs, index, toks)
+    first1, slot1 = layout(*docs, facing, toks)
+    first, slot = jnp.stack([first0, first1]), jnp.stack([slot0, slot1])
+    last = jnp.where(even, index, index - 4)
+    where = [core, index, index, index - 2, index - 4, near, far]
+    where += [facing, facing, index - 2, facing - 2, facing - 4, last]
+    where = jnp.stack(where).astype(jnp.int32)
+
+    heads = [jnp.stack([half(queries, core), half(grad_out, core)]), others]
     shape = (KVH // 2, 2, HQ // KVH, toks)
     work = queries.size // HD * 5 * toks
-    window = [*where, *heads, own, one, two, cross]
+    window = [where, *heads, own, one, two, cross, first]
     (stats,) = call(
         token_stats_kernel,
         flops=4 * HD * work,
         exps=work,
         ins=window,
+        scalar=(0,),
         outs=[jax.ShapeDtypeStruct((3, *shape), F32)],
     )
     prefs = queries.size // HD * count * pref.shape[2]
@@ -344,11 +358,12 @@
         prefix_kernel,
         flops=8 * HD * prefs,
         exps=prefs // 6,
-        ins=[*where, *heads, pref, stats],
+        ins=[where, doc_lengths, doc_tenants, tenant_slots, *heads, pref, stats],
         scratch=[
             pltpu.VMEM((2, KVH // 2, count * pref.shape[2], HD), BF16),
             pltpu.VMEM((2, count * pref.shape[2], HD), F32),
         ],
+        scalar=(0, 1, 2, 3),
         outs=[
             jax.ShapeDtypeStruct((2, *shape), F32),
             jax.ShapeDtypeStruct((KVH, count, pref.shape[2], HD), BF16),
@@ -360,6 +375,7 @@
         flops=8 * HD * work,
         exps=work,
         ins=window + [full],
+        scalar=(0,),
         outs=[jax.ShapeDtypeStruct(wide, kind) for kind in (F32, BF16, BF16)],
     )
 

time: 106 us -> 100 us (0.943)
  waiting for transfers between devices: 18.3 us -> 12.3 us
  starting transfers between devices: 51.8 us -> 47.5 us
  other arithmetic: 3.07 us -> 5.9 us
  local copies, waits for them, and re-layouts: 4.82 us -> 6.13 us
    ppermute x4, starting transfers between devices: 7.03 us -> 13.2 us  [shift(): return lax.ppermute(x, SEQ, pairs)]
    ppermute x3, starting transfers between devices: 13.8 us -> 8.19 us  [swap(): return lax.ppermute(x, SEQ, [(i, i ^ 1) for i in range(count)])]
    all_to_all x3, starting transfers between devices: 30.9 us -> 26.1 us  [exchange(): return lax.all_to_all(x, axis, split_axis=0, concat_axis=0, tiled=True)]
    all_to_all x3, waiting for transfers between devices: 6.91 us -> 2.53 us  [exchange(): return lax.all_to_all(x, axis, split_axis=0, concat_axis=0, tiled=True)]
    another operation x1 -> x3, other arithmetic: 0.08 us -> 1.71 us  [the longest x1 1.52 us: per_device(): heads = [jnp.stack([half(queries, core), half(grad_out, core)]), others]]
    ppermute x3, waiting for transfers between devices: 2.67 us -> 1.09 us  [swap(): return lax.ppermute(x, SEQ, [(i, i ^ 1) for i in range(count)])]
    another operation x1, local copies, waits for them, and re-layouts: 2.09 us -> 3.31 us  [per_device(): jnp.stack([half(queries, 1 - core), half(grad_out, 1 - core)])]
  transfers between devices with their start and end apart: 10 -> 10, of which waited for: 5 -> 5; matrix products, arithmetic and copies ran while one was open for 3% -> 9% of each run, Pallas kernels for 18% -> 19%
where the time goes in v9:
time: 100 us; the launch traced here: 98.7 us
  starting transfers between devices  47.5 us (48%)
  Pallas kernels  25.9 us (26%)
  waiting for transfers between devices  12.3 us (12%)
  local copies, waits for them, and re-layouts  6.13 us (6%)
  other arithmetic  5.9 us (6%)
    all_to_all x3, starting transfers between devices, exchange(): return lax.all_to_all(x, axis, split_axis=0, concat_axis=0, tiled=True)  26.1 us
    pallas_call x5, Pallas kernels, call(): pl.pallas_call(kernel, in_specs=[scalars if n in scalar else space for n...  25.9 us
    ppermute x4, starting transfers between devices, shift(): return lax.ppermute(x, SEQ, pairs)  13.2 us
    ppermute x4, waiting for transfers between devices, shift(): return lax.ppermute(x, SEQ, pairs)  8.65 us
    ppermute x3, starting transfers between devices, swap(): return lax.ppermute(x, SEQ, [(i, i ^ 1) for i in range(count)])  8.19 us
    another operation x1, local copies, waits for them, and re-layouts, per_device(): jnp.stack([half(queries, 1 - core), half(grad_out, 1 - core)])  3.31 us
    all_to_all x3, waiting for transfers between devices, exchange(): return lax.all_to_all(x, axis, split_axis=0, concat_axis=0, tiled=True)  2.53 us
  transfers between devices with their start and end apart: 10, of which 5 were waited for; matrix products, arithmetic and copies ran while one was open for 9% of the time, Pallas kernels for 19%

profile of v9, /device:TPU:1, one launch (start us, length us, event | category | flops | bytes accessed | tf_op | source)
XLA Modules:
  0.0 98.7 jit_solution(5510457388904675576)
XLA Ops:
  0.6 1.0 %pad_maximum_fusion.3.refs_0_ = bf16[2,128,512]{2,1,0:T(8,128)(2,1)S(1)} fusion(bf16[1,128,512]{2,1,0:T(8,128)(2,1)} %bitcast.44, bf16[1,128,512]{2,1,0:T(8,128)(2,1)} %bitcast.46), kind=kLoop, calls=%fused_computation.9 | loop fusion | flops 131072 | bytes 524288 | tf_op jit(solution)/shard_map/stack | solution.py:324
  1.6 6.7 %collective-permute-start.2 = (bf16[2,128,512]{2,1,0:T(8,128)(2,1)S(1)}, bf16[2,128,512]{2,1,0:T(8,128)(2,1)S(1)}, u32[]{:S(2)}, u32[]{:S(2)}) collective-permute-start(bf16[2,128,512]{2,1,0:T(8,128)(2,1)S(1)} %pad_maximum_fusion.3.refs_0_), channel_id=1, source_target_pairs={{0,4},{1,5},{2,6},{3,7},{4,8},{5,9},{6,10},{7,11},{8,12},{9,13},{1... | collective-permute-start | bytes 786440 | tf_op jit(solution)/shard_map/ppermute | solution.py:312
  8.3 4.0 %collective-permute-start.1 = (bf16[2,128,512]{2,1,0:T(8,128)(2,1)S(1)}, bf16[2,128,512]{2,1,0:T(8,128)(2,1)S(1)}, u32[]{:S(2)}, u32[]{:S(2)}) collective-permute-start(bf16[2,128,512]{2,1,0:T(8,128)(2,1)S(1)} %pad_maximum_fusion.3.refs_0_), channel_id=1, source_target_pairs={{0,2},{1,3},{2,4},{3,5},{4,6},{5,7},{6,8},{7,9},{8,10},{9,11},{10,... | collective-permute-start | bytes 786440 | tf_op jit(solution)/shard_map/ppermute | solution.py:312
  12.3 3.3 %dynamic-slice_bitcast_fusion = (bf16[1,128,3072]{2,1,0:T(8,128)(2,1)S(1)}, bf16[1,128,3072]{2,1,0:T(8,128)(2,1)}, bf16[1,128,3072]{2,1,0:T(8,128)(2,1)}, bf16[1,128,3072]{2,1,0:T(8,128)(2,1)S(1)}) fusion(bf16[128,6144]{1,0:T(8,128)(2,1)} %param.12, s32[]{:T(128)S(6)} %select_n.47, s32[]{:T(128)S(6)} %select_n.46, bf16[128,6144]{1,0:T(8,128)(2,1)} %param.9), kind=kLoop, calls=%fused_computation.2 | loop fusion | bytes 6291464 | tf_op jit(solution)/shard_map/stack | solution.py:330
  15.6 0.0 copy-start.9
  15.6 0.0 copy-start.10
  15.6 0.0 copy-start.2
  15.6 0.0 copy-start.7
  15.6 0.0 copy-start.8
  15.7 1.3 %pad_maximum_fusion.1 = bf16[2,128,3072]{2,1,0:T(8,128)(2,1)} fusion(bf16[1,128,3072]{2,1,0:T(8,128)(2,1)S(1)} %get-tuple-element.28, bf16[1,128,3072]{2,1,0:T(8,128)(2,1)S(1)} %get-tuple-element.35), kind=kLoop, calls=%fused_computation.1 | loop fusion | flops 786432 | bytes 3145728 | tf_op jit(solution)/shard_map/stack | solution.py:330
  16.9 3.1 %collective-permute-start = (bf16[2,128,3072]{2,1,0:T(8,128)(2,1)}, bf16[2,128,3072]{2,1,0:T(8,128)(2,1)}, u32[]{:S(2)}, u32[]{:S(2)}) collective-permute-start(bf16[2,128,3072]{2,1,0:T(8,128)(2,1)} %pad_maximum_fusion.1), channel_id=1, source_target_pairs={{0,1},{1,0},{2,3},{3,2},{4,5},{5,4},{6,7},{7,6},{8,9},{9,8},{10,11... | collective-permute-start | bytes 4718600 | tf_op jit(solution)/shard_map/ppermute | solution.py:315
  20.1 0.0 copy-done.9
  20.1 0.0 copy-done.10
  20.1 0.1 maximum_bitcast_fusion
  20.2 0.8 broadcast_in_dim.18
  21.0 7.7 %all-to-all-start = ((bf16[16,2,24,256]{3,2,1,0:T(8,128)(2,1)}), bf16[16,2,24,256]{3,2,1,0:T(8,128)(2,1)S(1)}, u32[]{:S(2)}, u32[]{:S(2)}) async-start(bf16[16,2,24,256]{3,2,1,0:T(8,128)(2,1)} %bitcast.15), calls=%async_computation | async-start | bytes 786432 | tf_op jit(solution)/shard_map/all_to_all | solution.py:318
  28.7 0.0 copy-done.2
  28.7 0.2 reduce-window.7
  28.9 0.1 convert_reduce_fusion.1
  29.0 0.1 select_reduce_fusion.1
  29.1 0.0 copy-done.7
  29.1 0.0 copy-done.8
  29.1 0.0 collective-permute-done.2.refs_2_
  29.1 0.0 collective-permute-done.1.refs_1_
  29.2 0.8 pad_maximum_fusion.2
  30.0 2.0 %collective-permute-start.3 = (bf16[3,2,128,256]{3,2,1,0:T(8,128)(2,1)}, bf16[3,2,128,256]{3,2,1,0:T(8,128)(2,1)S(1)}, u32[]{:S(2)}, u32[]{:S(2)}) collective-permute-start(bf16[3,2,128,256]{3,2,1,0:T(8,128)(2,1)} %pad_maximum_fusion.2), channel_id=1, source_target_pairs={{0,1},{1,0},{2,3},{3,2},{4,5},{5,4},{6,7},{7,6},{8,9},{9,8},{10,11... | collective-permute-start | bytes 1179656 | tf_op jit(solution)/shard_map/ppermute | solution.py:315
  32.0 0.1 stack.97.where_ref
  32.1 1.5 %pad_maximum_fusion.mine_ref = bf16[2,128,3072]{2,1,0:T(8,128)(2,1)S(1)} fusion(bf16[1,128,3072]{2,1,0:T(8,128)(2,1)} %get-tuple-element.29, bf16[1,128,3072]{2,1,0:T(8,128)(2,1)} %get-tuple-element.34), kind=kLoop, calls=%fused_computation | loop fusion | flops 786432 | bytes 3145728 | tf_op jit(solution)/shard_map/stack | solution.py:344
  33.7 0.0 copy-start.3
  33.7 0.0 copy-start.4
  33.7 0.1 collective-permute-done.3.refs_3_
  33.8 0.0 copy-start
  33.8 0.0 collective-permute-done.others_ref
  33.8 7.4 %shard_map.120.stat_ref = f32[3,2,2,12,128]{4,3,2,1,0:T(8,128)S(1)} custom-call(s32[13]{0:T(128)S(1)} %stack.97.where_ref, bf16[2,128,3072]{2,1,0:T(8,128)(2,1)S(1)} %pad_maximum_fusion.mine_ref, bf16[2,128,3072]{2,1,0:T(8,128)(2,1)} %collective-permute-done.others_ref, bf16[2,128,512]{2,1,0:T(8,128)(2,1)S(1)} %pad_maximum_fusion.3.refs_0_, ...), custom_call_target="tpu_custom_call" | custom-call | flops 2013265920 | bytes 6291456 | tf_op jit(solution)/shard_map/pallas_call | solution.py:277
  41.2 0.0 copy-done
  41.2 2.0 %all-to-all-done.pref_ref = bf16[16,2,24,256]{3,2,1,0:T(8,128)(2,1)S(1)} async-done(((bf16[16,2,24,256]{3,2,1,0:T(8,128)(2,1)}), bf16[16,2,24,256]{3,2,1,0:T(8,128)(2,1)S(1)}, u32[]{:S(2)}, u32[]{:S(2)}) %all-to-all-start) | async-done | bytes 393248 | tf_op jit(solution)/shard_map/all_to_all | solution.py:318
  43.2 0.0 copy-done.3
  43.2 0.0 copy-done.4
  43.3 6.0 %shard_map.121 = (f32[2,2,2,12,128]{4,3,2,1,0:T(8,128)S(1)}, bf16[4,16,24,128]{3,2,1,0:T(8,128)(2,1)}) custom-call(s32[13]{0:T(128)S(1)} %stack.97.where_ref, s32[1,8]{1,0:T(1,128)S(1)} %copy-done.2, s32[1,8]{1,0:T(1,128)S(1)} %copy-done.3, s32[6]{0:T(128)S(1)} %copy-done.4, bf16[2,128,3072]{2,1,0:T(8,128)(2,1)S(1)} %pad_maximum_fusion.mine_ref, ...), custom_call_target="tpu_custom_call" | custom-call | flops 2415919104 | bytes 6291456 | tf_op jit(solution)/shard_map/pallas_call | solution.py:277
  49.3 0.0 copy-start.5
  49.3 8.5 %all-to-all-start.1 = ((bf16[64,24,128]{2,1,0:T(8,128)(2,1)}), bf16[64,24,128]{2,1,0:T(8,128)(2,1)S(1)}, u32[]{:S(2)}, u32[]{:S(2)}) async-start(bf16[64,24,128]{2,1,0:T(8,128)(2,1)} %bitcast.26), calls=%async_computation.1 | async-start | bytes 786432 | tf_op jit(solution)/shard_map/all_to_all | solution.py:318
  57.8 0.0 copy-done.5
  57.8 0.0 copy-start.1
  57.8 1.0 %copy-done.1 = bf16[3,2,128,256]{3,2,1,0:T(8,128)(2,1)S(1)} copy-done((bf16[3,2,128,256]{3,2,1,0:T(8,128)(2,1)S(1)}, bf16[3,2,128,256]{3,2,1,0:T(8,128)(2,1)}, u32[]{:S(2)}) %copy-start.1) | copy-done | bytes 393240
  58.8 0.0 copy-start.6
  58.8 0.8 copy-done.6
  59.6 11.0 %shard_map.123 = (f32[2,256,256]{2,1,0:T(8,128)S(1)}, bf16[2,256,256]{2,1,0:T(8,128)(2,1)}, bf16[2,256,256]{2,1,0:T(8,128)(2,1)S(1)}) custom-call(s32[13]{0:T(128)S(1)} %stack.97.where_ref, bf16[2,128,3072]{2,1,0:T(8,128)(2,1)S(1)} %pad_maximum_fusion.mine_ref, bf16[2,128,3072]{2,1,0:T(8,128)(2,1)} %collective-permute-done.others_ref, ...), custom_call_target="tpu_custom_call" | custom-call | flops 4026531840 | bytes 6291456 | tf_op jit(solution)/shard_map/pallas_call | solution.py:277
  70.6 1.3 %collective-permute-start.4 = (bf16[2,256,256]{2,1,0:T(8,128)(2,1)}, bf16[2,256,256]{2,1,0:T(8,128)(2,1)S(1)}, u32[]{:S(2)}, u32[]{:S(2)}) collective-permute-start(bf16[2,256,256]{2,1,0:T(8,128)(2,1)} %get-tuple-element.17), channel_id=1, source_target_pairs={{2,0},{3,1},{4,2},{5,3},{6,4},{7,5},{8,6},{9,7},{10,8},{11,9},{12,... | collective-permute-start | bytes 786440 | tf_op jit(solution)/shard_map/ppermute | solution.py:312
  71.9 1.3 %collective-permute-start.5 = (bf16[2,256,256]{2,1,0:T(8,128)(2,1)S(1)}, bf16[2,256,256]{2,1,0:T(8,128)(2,1)S(1)}, u32[]{:S(2)}, u32[]{:S(2)}) collective-permute-start(bf16[2,256,256]{2,1,0:T(8,128)(2,1)S(1)} %get-tuple-element.18), channel_id=1, source_target_pairs={{4,0},{5,1},{6,2},{7,3},{8,4},{9,5},{10,6},{11,7},{12,8},{13,9},{1... | collective-permute-start | bytes 786440 | tf_op jit(solution)/shard_map/ppermute | solution.py:312
  73.2 0.0 all-to-all-done.1.got_ref
  73.2 0.8 shard_map.122
  74.0 9.9 %all-to-all-start.2 = ((bf16[32,2,24,128]{3,2,1,0:T(8,128)(2,1)}), bf16[32,2,24,128]{3,2,1,0:T(8,128)(2,1)S(1)}, u32[]{:S(2)}, u32[]{:S(2)}) async-start(bf16[32,2,24,128]{3,2,1,0:T(8,128)(2,1)} %shard_map.122), calls=%async_computation.2 | async-start | bytes 786432 | tf_op jit(solution)/shard_map/all_to_all | solution.py:318
  84.0 0.0 collective-permute-done.4
  84.0 8.6 %collective-permute-done.5 = bf16[2,256,256]{2,1,0:T(8,128)(2,1)S(1)} collective-permute-done((bf16[2,256,256]{2,1,0:T(8,128)(2,1)S(1)}, bf16[2,256,256]{2,1,0:T(8,128)(2,1)S(1)}, u32[]{:S(2)}, u32[]{:S(2)}) %collective-permute-start.5) | collective-permute-done | bytes 262176 | tf_op jit(solution)/shard_map/ppermute | solution.py:312
  92.6 0.1 add_convert_fusion
  92.7 3.0 %collective-permute-start.6 = (bf16[2,128,256]{2,1,0:T(8,128)(2,1)S(1)}, bf16[2,128,256]{2,1,0:T(8,128)(2,1)S(1)}, u32[]{:S(2)}, u32[]{:S(2)}) collective-permute-start(bf16[2,128,256]{2,1,0:T(8,128)(2,1)S(1)} %slice.17), channel_id=1, source_target_pairs={{0,1},{1,0},{2,3},{3,2},{4,5},{5,4},{6,7},{7,6},{8,9},{9,8},{10,11... | collective-permute-start | bytes 393224 | tf_op jit(solution)/shard_map/ppermute | solution.py:315
  95.8 1.0 collective-permute-done.6
  96.8 0.7 fusion.4
  97.5 0.5 all-to-all-done.2
  98.0 0.7 shard_map.124
  (11 shorter events, 0.1 us)
Async XLA Ops:
  1.6 27.5 %collective-permute-start.2 = (bf16[2,128,512]{2,1,0:T(8,128)(2,1)S(1)}, bf16[2,128,512]{2,1,0:T(8,128)(2,1)S(1)}, u32[]{:S(2)}, u32[]{:S(2)}) collective-permute-start(bf16[2,128,512]{2,1,0:T(8,128)(2,1)S(1)} %pad_maximum_fusion.3.refs_0_), channel_id=1, source_target_pairs={{0,4},{1,5},{2,6},{3,7},{4,8},{5,9},{6,10},{7,11},{8,12},{9,13},{1... | collective-permute-start | bytes 786440 | tf_op jit(solution)/shard_map/ppermute | solution.py:312
  8.3 20.8 %collective-permute-start.1 = (bf16[2,128,512]{2,1,0:T(8,128)(2,1)S(1)}, bf16[2,128,512]{2,1,0:T(8,128)(2,1)S(1)}, u32[]{:S(2)}, u32[]{:S(2)}) collective-permute-start(bf16[2,128,512]{2,1,0:T(8,128)(2,1)S(1)} %pad_maximum_fusion.3.refs_0_), channel_id=1, source_target_pairs={{0,2},{1,3},{2,4},{3,5},{4,6},{5,7},{6,8},{7,9},{8,10},{9,11},{10,... | collective-permute-start | bytes 786440 | tf_op jit(solution)/shard_map/ppermute | solution.py:312
  15.6 4.5 %copy-start.9 = (bf16[24,512]{1,0:T(8,128)(2,1)S(1)}, bf16[24,512]{1,0:T(8,128)(2,1)}, u32[]{:S(2)}) copy-start(bf16[24,512]{1,0:T(8,128)(2,1)} %param.13) | copy-start | bytes 73732
  15.6 4.5 %copy-start.10 = (bf16[24,512]{1,0:T(8,128)(2,1)S(1)}, bf16[24,512]{1,0:T(8,128)(2,1)}, u32[]{:S(2)}) copy-start(bf16[24,512]{1,0:T(8,128)(2,1)} %param.14) | copy-start | bytes 73732
  15.6 13.1 %copy-start.2 = (s32[1,8]{1,0:T(1,128)S(1)}, s32[1,8]{1,0:T(1,128)}, u32[]{:S(2)}) copy-start(s32[1,8]{1,0:T(1,128)} %lengths_ref.1) | copy-start | bytes 100
  15.6 13.4 %copy-start.7 = (bf16[128,512]{1,0:T(8,128)(2,1)S(1)}, bf16[128,512]{1,0:T(8,128)(2,1)}, u32[]{:S(2)}) copy-start(bf16[128,512]{1,0:T(8,128)(2,1)} %param.11) | copy-start | bytes 393220
  15.6 13.4 %copy-start.8 = (bf16[128,512]{1,0:T(8,128)(2,1)S(1)}, bf16[128,512]{1,0:T(8,128)(2,1)}, u32[]{:S(2)}) copy-start(bf16[128,512]{1,0:T(8,128)(2,1)} %param.10) | copy-start | bytes 393220
  16.9 16.9 %collective-permute-start = (bf16[2,128,3072]{2,1,0:T(8,128)(2,1)}, bf16[2,128,3072]{2,1,0:T(8,128)(2,1)}, u32[]{:S(2)}, u32[]{:S(2)}) collective-permute-start(bf16[2,128,3072]{2,1,0:T(8,128)(2,1)} %pad_maximum_fusion.1), channel_id=1, source_target_pairs={{0,1},{1,0},{2,3},{3,2},{4,5},{5,4},{6,7},{7,6},{8,9},{9,8},{10,11... | collective-permute-start | bytes 4718600 | tf_op jit(solution)/shard_map/ppermute | solution.py:315
  21.0 22.2 %all-to-all-start = ((bf16[16,2,24,256]{3,2,1,0:T(8,128)(2,1)}), bf16[16,2,24,256]{3,2,1,0:T(8,128)(2,1)S(1)}, u32[]{:S(2)}, u32[]{:S(2)}) async-start(bf16[16,2,24,256]{3,2,1,0:T(8,128)(2,1)} %bitcast.15), calls=%async_computation | async-start | bytes 786432 | tf_op jit(solution)/shard_map/all_to_all | solution.py:318
  30.0 3.8 %collective-permute-start.3 = (bf16[3,2,128,256]{3,2,1,0:T(8,128)(2,1)}, bf16[3,2,128,256]{3,2,1,0:T(8,128)(2,1)S(1)}, u32[]{:S(2)}, u32[]{:S(2)}) collective-permute-start(bf16[3,2,128,256]{3,2,1,0:T(8,128)(2,1)} %pad_maximum_fusion.2), channel_id=1, source_target_pairs={{0,1},{1,0},{2,3},{3,2},{4,5},{5,4},{6,7},{7,6},{8,9},{9,8},{10,11... | collective-permute-start | bytes 1179656 | tf_op jit(solution)/shard_map/ppermute | solution.py:315
  33.7 9.6 %copy-start.3 = (s32[1,8]{1,0:T(1,128)S(1)}, s32[1,8]{1,0:T(1,128)}, u32[]{:S(2)}) copy-start(s32[1,8]{1,0:T(1,128)} %tenants_ref.1) | copy-start | bytes 100
  33.7 9.6 %copy-start.4 = (s32[6]{0:T(128)S(1)}, s32[6]{0:T(128)}, u32[]{:S(2)}) copy-start(s32[6]{0:T(128)} %slots_ref.1) | copy-start | bytes 76
  33.8 7.4 %copy-start = (bf16[3,2,128,256]{3,2,1,0:T(8,128)(2,1)}, bf16[3,2,128,256]{3,2,1,0:T(8,128)(2,1)S(1)}, u32[]{:S(2)}) copy-start(bf16[3,2,128,256]{3,2,1,0:T(8,128)(2,1)S(1)} %collective-permute-done.3.refs_3_) | copy-start | bytes 1179652
  49.3 8.5 %copy-start.5 = (f32[2,2,2,12,128]{4,3,2,1,0:T(8,128)}, f32[2,2,2,12,128]{4,3,2,1,0:T(8,128)S(1)}, u32[]{:S(2)}) copy-start(f32[2,2,2,12,128]{4,3,2,1,0:T(8,128)S(1)} %get-tuple-element.14.refs_5_) | copy-start | bytes 147460
  49.3 23.9 %all-to-all-start.1 = ((bf16[64,24,128]{2,1,0:T(8,128)(2,1)}), bf16[64,24,128]{2,1,0:T(8,128)(2,1)S(1)}, u32[]{:S(2)}, u32[]{:S(2)}) async-start(bf16[64,24,128]{2,1,0:T(8,128)(2,1)} %bitcast.26), calls=%async_computation.1 | async-start | bytes 786432 | tf_op jit(solution)/shard_map/all_to_all | solution.py:318
  57.8 1.0 %copy-start.1 = (bf16[3,2,128,256]{3,2,1,0:T(8,128)(2,1)S(1)}, bf16[3,2,128,256]{3,2,1,0:T(8,128)(2,1)}, u32[]{:S(2)}) copy-start(bf16[3,2,128,256]{3,2,1,0:T(8,128)(2,1)} %copy-done) | copy-start | bytes 1179652
  58.8 0.8 copy-start.6
  70.6 13.4 %collective-permute-start.4 = (bf16[2,256,256]{2,1,0:T(8,128)(2,1)}, bf16[2,256,256]{2,1,0:T(8,128)(2,1)S(1)}, u32[]{:S(2)}, u32[]{:S(2)}) collective-permute-start(bf16[2,256,256]{2,1,0:T(8,128)(2,1)} %get-tuple-element.17), channel_id=1, source_target_pairs={{2,0},{3,1},{4,2},{5,3},{6,4},{7,5},{8,6},{9,7},{10,8},{11,9},{12,... | collective-permute-start | bytes 786440 | tf_op jit(solution)/shard_map/ppermute | solution.py:312
  71.9 20.7 %collective-permute-start.5 = (bf16[2,256,256]{2,1,0:T(8,128)(2,1)S(1)}, bf16[2,256,256]{2,1,0:T(8,128)(2,1)S(1)}, u32[]{:S(2)}, u32[]{:S(2)}) collective-permute-start(bf16[2,256,256]{2,1,0:T(8,128)(2,1)S(1)} %get-tuple-element.18), channel_id=1, source_target_pairs={{4,0},{5,1},{6,2},{7,3},{8,4},{9,5},{10,6},{11,7},{12,8},{13,9},{1... | collective-permute-start | bytes 786440 | tf_op jit(solution)/shard_map/ppermute | solution.py:312
  74.0 24.0 %all-to-all-start.2 = ((bf16[32,2,24,128]{3,2,1,0:T(8,128)(2,1)}), bf16[32,2,24,128]{3,2,1,0:T(8,128)(2,1)S(1)}, u32[]{:S(2)}, u32[]{:S(2)}) async-start(bf16[32,2,24,128]{3,2,1,0:T(8,128)(2,1)} %shard_map.122), calls=%async_computation.2 | async-start | bytes 786432 | tf_op jit(solution)/shard_map/all_to_all | solution.py:318
  92.7 4.0 %collective-permute-start.6 = (bf16[2,128,256]{2,1,0:T(8,128)(2,1)S(1)}, bf16[2,128,256]{2,1,0:T(8,128)(2,1)S(1)}, u32[]{:S(2)}, u32[]{:S(2)}) collective-permute-start(bf16[2,128,256]{2,1,0:T(8,128)(2,1)S(1)} %slice.17), channel_id=1, source_target_pairs={{0,1},{1,0},{2,3},{3,2},{4,5},{5,4},{6,7},{7,6},{8,9},{9,8},{10,11... | collective-permute-start | bytes 393224 | tf_op jit(solution)/shard_map/ppermute | solution.py:315
